TPU v7x, 128 devices: a whole 4x4x4 slice. The times are simulated.
128 devices in a mesh: gx: 8 (over z_hi, y), gy: 16 (over x, z_lo, core).
Axes of the slice: x: 4, y: 4, z: 4 (z_hi: 2, z_lo: 2; z = z_hi * 2 + z_lo), core: 2. Of those that a mesh axis runs over, the one named last changes fastest.
Arguments:
- src_value: bfloat16 [32, 1048576], P(None, ('gx', 'gy')), may hold values from -6 to 6
- src_point: int32 [2, 1048576], P(None, ('gx', 'gy')), may hold values from 0 to 255
- src_owner: int32 [1048576, 1], P(('gx', 'gy')), may hold values from 0 to 127; in each aligned block of 8192 rows (0 to 8191, 8192 to 16383, ...) at most 128 rows name the same one
- translation: bfloat16 [11, 2, 2, 2, 4096], replicated, may hold values from -0.375 to 0.375
Outputs:
- box_weights: bfloat16 [128, 8, 16, 4096], P(None, 'gx', 'gy')
Inputs may be any that keep to these rules, and one draw needn't show every extreme that they name: `src_owner`: among the sources listed on one device, at most 128 have the same owner, and exactly 128 do for some owner on some device.
All inputs are finite; a program needn't handle non-finite values.
Results may differ from a plain program's by a relative error of at most 0.023.
Values may be sent and summed in bfloat16 or wider, within the bound.
No kernel may reach another device: no remote copies, remote signals or barrier semaphores. Data moves between devices by JAX's collectives and lax.ppermute only.
A program may use at most 128 MiB of HBM per device.

v0:
```python
import math

import jax
import jax.numpy as jnp
from jax import lax
from jax.sharding import PartitionSpec as P

QX = 8
R = 64
LEVX = 4
LB = 16
LAT = 16
CAP = 128


phase_modulus = 61


def partner_2(value, axis, stride):
    mask = 2**stride
    pairs = [(source, source ^ mask) for source in range(lax.axis_size(axis))]
    return lax.ppermute(value, axis, pairs)


def chebyshev(count):
    index = jnp.arange(count, dtype=jnp.float32)
    return 0.5 + 0.5 * jnp.cos(math.pi * (2.0 * index + 1.0) / (2.0 * count))


def lagrange(position, count):
    nodes = chebyshev(count)
    rows_out = []
    for first in range(count):
        term = jnp.ones_like(position)
        for second in range(count):
            if second != first:
                term = term * (position - nodes[second]) / (nodes[first] - nodes[second])
        rows_out.append(term)
    return jnp.stack(rows_out)


def phase_angle(parents, targets):
    product = parents[:, None] * targets[None, :] % phase_modulus
    return 2.0 * math.pi / phase_modulus * product.astype(jnp.float32)


def rotate(values, angle):
    half = values.shape[0] // 2
    cosine = jnp.cos(angle)
    sine = jnp.sin(angle)
    upper = values[:half]
    lower = values[half:]
    return jnp.concatenate(
        [upper * cosine - lower * sine, upper * sine + lower * cosine], axis=0
    ).astype(jnp.bfloat16)


def block_matrix(translation, level):
    parts = translation[level].reshape(2, 2, 2, R, R)
    real_part = parts[:, :, 0]
    imag_part = parts[:, :, 1]
    top = jnp.concatenate([real_part, -imag_part], axis=3)
    bottom = jnp.concatenate([imag_part, real_part], axis=3)
    return jnp.concatenate([top, bottom], axis=2)


def level_x(weights, mats, offset):
    rows, sx, sy, tx, ty, fields = weights.shape
    pieces = weights.reshape(rows, sx // 2, 2, sy, tx, ty, fields)
    out = jnp.einsum("tcoi,ipcsxyh->opsxtyh", mats, pieces, preferred_element_type=jnp.float32)
    out = out.reshape(rows, sx // 2, sy, 2 * tx, ty, fields)
    parents = offset * (sx // 2) + jnp.arange(sx // 2, dtype=jnp.int32)
    angle = phase_angle(parents, jnp.arange(2 * tx, dtype=jnp.int32))
    return rotate(out, angle[None, :, None, :, None, None])


def level_y(weights, mats, offset):
    rows, sx, sy, tx, ty, fields = weights.shape
    pieces = weights.reshape(rows, sx, sy // 2, 2, tx, ty, fields)
    out = jnp.einsum("tcoi,ispcxyh->ospxyth", mats, pieces, preferred_element_type=jnp.float32)
    out = out.reshape(rows, sx, sy // 2, tx, 2 * ty, fields)
    parents = offset * (sy // 2) + jnp.arange(sy // 2, dtype=jnp.int32)
    angle = phase_angle(parents, jnp.arange(2 * ty, dtype=jnp.int32))
    return rotate(out, angle[None, None, :, None, :, None])


def combine_sibling(weights, partner, mats, mine, parent, keys, shape_keys):
    rows = weights.shape[0]
    ordered = jnp.where(mine == 0, jnp.stack([weights, partner]), jnp.stack([partner, weights]))
    chosen = lax.dynamic_index_in_dim(mats, mine, 0, keepdims=False)
    out = jnp.einsum(
        "coi,cim->om", chosen, ordered.reshape(2, rows, -1), preferred_element_type=jnp.float32
    )
    out = out.reshape(weights.shape)
    new_keys = 2 * keys + mine
    angle = phase_angle(parent.reshape(1), new_keys)[0]
    return (rotate(out, angle.reshape(shape_keys)), new_keys)


def across_x(weights, translation, level, bit, row_x, keys):
    partner = partner_2(weights, "gx", bit)
    mine = row_x >> bit & 1
    parent = row_x >> bit + 1
    return combine_sibling(
        weights,
        partner,
        block_matrix(translation, level),
        mine,
        parent,
        keys,
        (1, 1, 1, keys.shape[0], 1, 1),
    )


def across_y(weights, translation, level, bit, row_y, keys):
    partner = partner_2(weights, "gy", bit)
    mine = row_y >> bit & 1
    parent = row_y >> bit + 1
    return combine_sibling(
        weights,
        partner,
        block_matrix(translation, level),
        mine,
        parent,
        keys,
        (1, 1, 1, 1, keys.shape[0], 1),
    )


def body(src_value, src_point, src_owner, translation):
    across = lax.axis_size("gx")
    down = lax.axis_size("gy")
    devices = across * down
    row_x = lax.axis_index("gx")
    row_y = lax.axis_index("gy")
    fields = src_value.shape[0] // 2
    dest = src_owner[:, 0]
    member = (dest[:, None] == jnp.arange(devices, dtype=jnp.int32)[None, :]).astype(jnp.int32)
    before = jnp.sum((jnp.cumsum(member, axis=0) - member) * member, axis=1)
    place = dest * CAP + before
    send_vals = jnp.zeros((2 * fields, devices * CAP), jnp.bfloat16).at[:, place].set(src_value)
    send_pts = jnp.zeros((2, devices * CAP), jnp.int32).at[:, place].set(src_point)
    got_vals, got_pts = (
        lax.all_to_all(
            send_vals.reshape(2 * fields, devices, CAP),
            ("gx", "gy"),
            split_axis=1,
            concat_axis=1,
            tiled=True,
        ),
        lax.all_to_all(
            send_pts.reshape(2, devices, CAP), ("gx", "gy"), split_axis=1, concat_axis=1, tiled=True
        ),
    )
    got_vals = got_vals.reshape(2 * fields, devices * CAP)
    got_pts = got_pts.reshape(2, devices * CAP)
    px = got_pts[0]
    py = got_pts[1]
    leaf_x = px // LAT
    leaf_y = py // LAT
    u = ((px % LAT).astype(jnp.float32) + 0.5) / LAT
    v = ((py % LAT).astype(jnp.float32) + 0.5) / LAT
    weights_x = lagrange(u, QX)
    weights_y = lagrange(v, QX).astype(jnp.bfloat16)
    glob_x = row_x * (LB * LAT) + px
    glob_y = row_y * (LB * LAT) + py
    angle = 2.0 * math.pi / phase_modulus * (glob_x * glob_y % phase_modulus).astype(jnp.float32)
    source = got_vals.astype(jnp.float32).reshape(2, fields, -1)
    cosine = jnp.cos(angle)
    sine = jnp.sin(angle)
    charge = jnp.stack(
        [cosine * source[0] - sine * source[1], sine * source[0] + cosine * source[1]]
    )
    spread = (weights_x[None, :, None, :] * charge[:, None, :, :]).astype(jnp.bfloat16)
    cells_y = jnp.arange(LB, dtype=jnp.int32)

    def one_column(column):
        inside = (leaf_x == column)[None, :] & (leaf_y[None, :] == cells_y[:, None])
        table = jnp.where(inside[:, None, :], weights_y[None, :, :], jnp.zeros((), jnp.bfloat16))
        return jnp.einsum("ybs,rahs->rabyh", table, spread, preferred_element_type=jnp.float32)

    leaves = lax.map(one_column, jnp.arange(LB, dtype=jnp.int32))
    weights = (
        jnp.transpose(leaves, (1, 2, 3, 0, 4, 5))
        .reshape(2 * R, LB, LB, 1, 1, fields)
        .astype(jnp.bfloat16)
    )
    for step in range(LEVX):
        weights = level_x(weights, block_matrix(translation, 2 * step), row_x)
        weights = level_y(weights, block_matrix(translation, 2 * step + 1), row_y)
    keys_x = jnp.arange(LB, dtype=jnp.int32)
    keys_y = jnp.arange(LB, dtype=jnp.int32)
    weights, keys_x = across_x(weights, translation, 2 * LEVX, 0, row_x, keys_x)
    weights, keys_y = across_y(weights, translation, 2 * LEVX + 1, 0, row_y, keys_y)
    weights, keys_x = across_x(weights, translation, 2 * LEVX + 2, 1, row_x, keys_x)
    return weights.reshape(2 * R, 1, 1, LB * LB * fields)


def solution(mesh):
    return jax.shard_map(
        body,
        mesh=mesh,
        in_specs=(P(None, ("gx", "gy")), P(None, ("gx", "gy")), P(("gx", "gy"), None), P()),
        out_specs=P(None, "gx", "gy", None),
        check_vma=False,
    )
```

profile of v0, /device:TPU:1, one launch (start us, length us, event | category | flops | bytes accessed | tf_op | source)
XLA Modules:
  0.0 537.1 jit_solution(4825851594114279166)
XLA Ops:
  14.9 24.7 %scatter_custom_fusion = s32[2,16384]{0,1:T(8,128)} fusion(s32[8192]{0:T(1024)S(1)} %bitcast.434, s32[8192,2]{1,0:T(8,128)} %copy.185, s32[]{:T(128)} %constant.149.clone.1), kind=kCustom, calls=%fused_computation.30 | custom fusion | bytes 131584 | tf_op jit(solution)/shard_map/scatter | solution.py:142
  39.6 6.0 %copy.186 = s32[2,128,128]{2,0,1:T(2,128)} copy(s32[2,128,128]{0,2,1:T(8,128)} %bitcast.399) | data formatting | bytes 262144 | tf_op jit(solution)/shard_map/reshape | solution.py:152
  45.5 11.8 %all-to-all-start = ((s32[2,128,128]{2,0,1:T(2,128)}), s32[2,128,128]{2,0,1:T(2,128)S(1)}, u32[]{:S(2)}, u32[]{:S(2)}) async-start(s32[2,128,128]{2,0,1:T(2,128)} %copy.186), calls=%async_computation | async-start | bytes 262144 | tf_op jit(solution)/shard_map/all_to_all | solution.py:151
  148.0 23.8 %scatter_custom_fusion.1 = bf16[32,16384]{0,1:T(8,128)(2,1)} fusion(s32[8192]{0:T(1024)S(1)} %bitcast.435, bf16[8192,32]{1,0:T(8,128)(2,1)S(1)} %copy.189, bf16[]{:T(256)} %constant.167.clone.1), kind=kCustom, calls=%fused_computation.91 | custom fusion | bytes 1048578 | tf_op jit(solution)/shard_map/scatter | solution.py:141
  180.1 10.1 %all-to-all-start.1 = ((bf16[32,128,128]{2,0,1:T(8,128)(2,1)}), bf16[32,128,128]{2,0,1:T(8,128)(2,1)S(1)}, u32[]{:S(2)}, u32[]{:S(2)}) async-start(bf16[32,128,128]{2,0,1:T(8,128)(2,1)} %copy.190), calls=%async_computation.1 | async-start | bytes 2097152 | tf_op jit(solution)/shard_map/all_to_all | solution.py:144
  190.3 5.7 %fusion.188 = (f32[1,16384]{1,0:T(1,128)S(1)}, f32[1,16384]{1,0:T(1,128)S(1)}, bf16[1,16384]{1,0:T(2,128)(2,1)S(1)}, f32[1,16384]{1,0:T(1,128)S(1)}) fusion(f32[]{:T(128)S(6)} %sub.1178, f32[]{:T(128)S(6)} %sub.1177, f32[]{:T(128)S(6)} %sub.1176, f32[]{:T(128)S(6)} %sub.1175, f32[]{:T(128)S(6)} %sub.1174, f32[]{:T(128)S(6)} %sub.1173, f32[]{:T(128)S(6)} %sub.1172, ...), kind=kLoop, calls=%fused_computation.405 | loop fusion | flops 1130496 | bytes 360504 | tf_op jit(solution)/shard_map/div | solution.py:37
  196.0 5.2 divide_convert_fusion.1
  201.1 5.2 divide_convert_fusion.2
  206.3 5.2 divide_convert_fusion.3
  211.5 5.1 divide_convert_fusion.4
  216.6 5.2 divide_convert_fusion.5
  221.8 5.1 divide_convert_fusion.6
  236.6 195.9 %while.13 = (s32[]{:T(128)}, bf16[16,2,8,8,16,16]{5,3,2,1,4,0:T(8,128)(2,1)}, s32[16]{0:T(128)S(1)}, s32[16384]{0:T(1024)S(1)}, s32[16384]{0:T(1024)S(1)}, /*ind...) while((s32[]{:T(128)}, ...), condition=%wide.region_6.7_spmd.clone.clone, body=%wide.region_5.6_spmd.clone.clone.sunk | while | flops 1084768256 | bytes 4620973 | solution.py:182
  238.6 10.7 %fusion.291 = bf16[16,2,8,8,16,16]{5,3,2,1,4,0:T(8,128)(2,1)} fusion(bf16[16,2,8,8,16,16]{5,3,2,1,4,0:T(8,128)(2,1)} %get-tuple-element.326, s32[]{:T(128)} %get-tuple-element.325, f32[2,16,16384]{2,1,0:T(8,128)S(1)} %get-tuple-element.340, f32[8,16384]{1,0:T(8,128)S(1)} %get-tuple-element.341, pred[16,16384]{1,0:T(8,128)(4,1)S(1)} %compare_and_fusion.2, ...), kind=kOutput, calls=%fused_computation.14.clone.1 | convolution fusion | flops 1084227584 | bytes 4194816 | tf_op jit(solution)/shard_map/while/body/eval_jaxpr/ybs,rahs->rabyh/dot_general | solution.py:180
  250.8 10.7 %fusion.291 = bf16[16,2,8,8,16,16]{5,3,2,1,4,0:T(8,128)(2,1)} fusion(bf16[16,2,8,8,16,16]{5,3,2,1,4,0:T(8,128)(2,1)} %get-tuple-element.326, s32[]{:T(128)} %get-tuple-element.325, f32[2,16,16384]{2,1,0:T(8,128)S(1)} %get-tuple-element.340, f32[8,16384]{1,0:T(8,128)S(1)} %get-tuple-element.341, pred[16,16384]{1,0:T(8,128)(4,1)S(1)} %compare_and_fusion.2, ...), kind=kOutput, calls=%fused_computation.14.clone.1 | convolution fusion | flops 1084227584 | bytes 4194816 | tf_op jit(solution)/shard_map/while/body/eval_jaxpr/ybs,rahs->rabyh/dot_general | solution.py:180
  263.0 10.7 %fusion.291 = bf16[16,2,8,8,16,16]{5,3,2,1,4,0:T(8,128)(2,1)} fusion(bf16[16,2,8,8,16,16]{5,3,2,1,4,0:T(8,128)(2,1)} %get-tuple-element.326, s32[]{:T(128)} %get-tuple-element.325, f32[2,16,16384]{2,1,0:T(8,128)S(1)} %get-tuple-element.340, f32[8,16384]{1,0:T(8,128)S(1)} %get-tuple-element.341, pred[16,16384]{1,0:T(8,128)(4,1)S(1)} %compare_and_fusion.2, ...), kind=kOutput, calls=%fused_computation.14.clone.1 | convolution fusion | flops 1084227584 | bytes 4194816 | tf_op jit(solution)/shard_map/while/body/eval_jaxpr/ybs,rahs->rabyh/dot_general | solution.py:180
  275.2 10.7 %fusion.291 = bf16[16,2,8,8,16,16]{5,3,2,1,4,0:T(8,128)(2,1)} fusion(bf16[16,2,8,8,16,16]{5,3,2,1,4,0:T(8,128)(2,1)} %get-tuple-element.326, s32[]{:T(128)} %get-tuple-element.325, f32[2,16,16384]{2,1,0:T(8,128)S(1)} %get-tuple-element.340, f32[8,16384]{1,0:T(8,128)S(1)} %get-tuple-element.341, pred[16,16384]{1,0:T(8,128)(4,1)S(1)} %compare_and_fusion.2, ...), kind=kOutput, calls=%fused_computation.14.clone.1 | convolution fusion | flops 1084227584 | bytes 4194816 | tf_op jit(solution)/shard_map/while/body/eval_jaxpr/ybs,rahs->rabyh/dot_general | solution.py:180
  287.4 10.7 %fusion.291 = bf16[16,2,8,8,16,16]{5,3,2,1,4,0:T(8,128)(2,1)} fusion(bf16[16,2,8,8,16,16]{5,3,2,1,4,0:T(8,128)(2,1)} %get-tuple-element.326, s32[]{:T(128)} %get-tuple-element.325, f32[2,16,16384]{2,1,0:T(8,128)S(1)} %get-tuple-element.340, f32[8,16384]{1,0:T(8,128)S(1)} %get-tuple-element.341, pred[16,16384]{1,0:T(8,128)(4,1)S(1)} %compare_and_fusion.2, ...), kind=kOutput, calls=%fused_computation.14.clone.1 | convolution fusion | flops 1084227584 | bytes 4194816 | tf_op jit(solution)/shard_map/while/body/eval_jaxpr/ybs,rahs->rabyh/dot_general | solution.py:180
  299.6 10.7 %fusion.291 = bf16[16,2,8,8,16,16]{5,3,2,1,4,0:T(8,128)(2,1)} fusion(bf16[16,2,8,8,16,16]{5,3,2,1,4,0:T(8,128)(2,1)} %get-tuple-element.326, s32[]{:T(128)} %get-tuple-element.325, f32[2,16,16384]{2,1,0:T(8,128)S(1)} %get-tuple-element.340, f32[8,16384]{1,0:T(8,128)S(1)} %get-tuple-element.341, pred[16,16384]{1,0:T(8,128)(4,1)S(1)} %compare_and_fusion.2, ...), kind=kOutput, calls=%fused_computation.14.clone.1 | convolution fusion | flops 1084227584 | bytes 4194816 | tf_op jit(solution)/shard_map/while/body/eval_jaxpr/ybs,rahs->rabyh/dot_general | solution.py:180
  311.8 10.7 %fusion.291 = bf16[16,2,8,8,16,16]{5,3,2,1,4,0:T(8,128)(2,1)} fusion(bf16[16,2,8,8,16,16]{5,3,2,1,4,0:T(8,128)(2,1)} %get-tuple-element.326, s32[]{:T(128)} %get-tuple-element.325, f32[2,16,16384]{2,1,0:T(8,128)S(1)} %get-tuple-element.340, f32[8,16384]{1,0:T(8,128)S(1)} %get-tuple-element.341, pred[16,16384]{1,0:T(8,128)(4,1)S(1)} %compare_and_fusion.2, ...), kind=kOutput, calls=%fused_computation.14.clone.1 | convolution fusion | flops 1084227584 | bytes 4194816 | tf_op jit(solution)/shard_map/while/body/eval_jaxpr/ybs,rahs->rabyh/dot_general | solution.py:180
  324.0 10.7 %fusion.291 = bf16[16,2,8,8,16,16]{5,3,2,1,4,0:T(8,128)(2,1)} fusion(bf16[16,2,8,8,16,16]{5,3,2,1,4,0:T(8,128)(2,1)} %get-tuple-element.326, s32[]{:T(128)} %get-tuple-element.325, f32[2,16,16384]{2,1,0:T(8,128)S(1)} %get-tuple-element.340, f32[8,16384]{1,0:T(8,128)S(1)} %get-tuple-element.341, pred[16,16384]{1,0:T(8,128)(4,1)S(1)} %compare_and_fusion.2, ...), kind=kOutput, calls=%fused_computation.14.clone.1 | convolution fusion | flops 1084227584 | bytes 4194816 | tf_op jit(solution)/shard_map/while/body/eval_jaxpr/ybs,rahs->rabyh/dot_general | solution.py:180
  336.2 10.7 %fusion.291 = bf16[16,2,8,8,16,16]{5,3,2,1,4,0:T(8,128)(2,1)} fusion(bf16[16,2,8,8,16,16]{5,3,2,1,4,0:T(8,128)(2,1)} %get-tuple-element.326, s32[]{:T(128)} %get-tuple-element.325, f32[2,16,16384]{2,1,0:T(8,128)S(1)} %get-tuple-element.340, f32[8,16384]{1,0:T(8,128)S(1)} %get-tuple-element.341, pred[16,16384]{1,0:T(8,128)(4,1)S(1)} %compare_and_fusion.2, ...), kind=kOutput, calls=%fused_computation.14.clone.1 | convolution fusion | flops 1084227584 | bytes 4194816 | tf_op jit(solution)/shard_map/while/body/eval_jaxpr/ybs,rahs->rabyh/dot_general | solution.py:180
  348.4 10.7 %fusion.291 = bf16[16,2,8,8,16,16]{5,3,2,1,4,0:T(8,128)(2,1)} fusion(bf16[16,2,8,8,16,16]{5,3,2,1,4,0:T(8,128)(2,1)} %get-tuple-element.326, s32[]{:T(128)} %get-tuple-element.325, f32[2,16,16384]{2,1,0:T(8,128)S(1)} %get-tuple-element.340, f32[8,16384]{1,0:T(8,128)S(1)} %get-tuple-element.341, pred[16,16384]{1,0:T(8,128)(4,1)S(1)} %compare_and_fusion.2, ...), kind=kOutput, calls=%fused_computation.14.clone.1 | convolution fusion | flops 1084227584 | bytes 4194816 | tf_op jit(solution)/shard_map/while/body/eval_jaxpr/ybs,rahs->rabyh/dot_general | solution.py:180
  360.6 10.7 %fusion.291 = bf16[16,2,8,8,16,16]{5,3,2,1,4,0:T(8,128)(2,1)} fusion(bf16[16,2,8,8,16,16]{5,3,2,1,4,0:T(8,128)(2,1)} %get-tuple-element.326, s32[]{:T(128)} %get-tuple-element.325, f32[2,16,16384]{2,1,0:T(8,128)S(1)} %get-tuple-element.340, f32[8,16384]{1,0:T(8,128)S(1)} %get-tuple-element.341, pred[16,16384]{1,0:T(8,128)(4,1)S(1)} %compare_and_fusion.2, ...), kind=kOutput, calls=%fused_computation.14.clone.1 | convolution fusion | flops 1084227584 | bytes 4194816 | tf_op jit(solution)/shard_map/while/body/eval_jaxpr/ybs,rahs->rabyh/dot_general | solution.py:180
  372.8 10.7 %fusion.291 = bf16[16,2,8,8,16,16]{5,3,2,1,4,0:T(8,128)(2,1)} fusion(bf16[16,2,8,8,16,16]{5,3,2,1,4,0:T(8,128)(2,1)} %get-tuple-element.326, s32[]{:T(128)} %get-tuple-element.325, f32[2,16,16384]{2,1,0:T(8,128)S(1)} %get-tuple-element.340, f32[8,16384]{1,0:T(8,128)S(1)} %get-tuple-element.341, pred[16,16384]{1,0:T(8,128)(4,1)S(1)} %compare_and_fusion.2, ...), kind=kOutput, calls=%fused_computation.14.clone.1 | convolution fusion | flops 1084227584 | bytes 4194816 | tf_op jit(solution)/shard_map/while/body/eval_jaxpr/ybs,rahs->rabyh/dot_general | solution.py:180
  385.0 10.7 %fusion.291 = bf16[16,2,8,8,16,16]{5,3,2,1,4,0:T(8,128)(2,1)} fusion(bf16[16,2,8,8,16,16]{5,3,2,1,4,0:T(8,128)(2,1)} %get-tuple-element.326, s32[]{:T(128)} %get-tuple-element.325, f32[2,16,16384]{2,1,0:T(8,128)S(1)} %get-tuple-element.340, f32[8,16384]{1,0:T(8,128)S(1)} %get-tuple-element.341, pred[16,16384]{1,0:T(8,128)(4,1)S(1)} %compare_and_fusion.2, ...), kind=kOutput, calls=%fused_computation.14.clone.1 | convolution fusion | flops 1084227584 | bytes 4194816 | tf_op jit(solution)/shard_map/while/body/eval_jaxpr/ybs,rahs->rabyh/dot_general | solution.py:180
  397.2 10.7 %fusion.291 = bf16[16,2,8,8,16,16]{5,3,2,1,4,0:T(8,128)(2,1)} fusion(bf16[16,2,8,8,16,16]{5,3,2,1,4,0:T(8,128)(2,1)} %get-tuple-element.326, s32[]{:T(128)} %get-tuple-element.325, f32[2,16,16384]{2,1,0:T(8,128)S(1)} %get-tuple-element.340, f32[8,16384]{1,0:T(8,128)S(1)} %get-tuple-element.341, pred[16,16384]{1,0:T(8,128)(4,1)S(1)} %compare_and_fusion.2, ...), kind=kOutput, calls=%fused_computation.14.clone.1 | convolution fusion | flops 1084227584 | bytes 4194816 | tf_op jit(solution)/shard_map/while/body/eval_jaxpr/ybs,rahs->rabyh/dot_general | solution.py:180
  409.5 10.7 %fusion.291 = bf16[16,2,8,8,16,16]{5,3,2,1,4,0:T(8,128)(2,1)} fusion(bf16[16,2,8,8,16,16]{5,3,2,1,4,0:T(8,128)(2,1)} %get-tuple-element.326, s32[]{:T(128)} %get-tuple-element.325, f32[2,16,16384]{2,1,0:T(8,128)S(1)} %get-tuple-element.340, f32[8,16384]{1,0:T(8,128)S(1)} %get-tuple-element.341, pred[16,16384]{1,0:T(8,128)(4,1)S(1)} %compare_and_fusion.2, ...), kind=kOutput, calls=%fused_computation.14.clone.1 | convolution fusion | flops 1084227584 | bytes 4194816 | tf_op jit(solution)/shard_map/while/body/eval_jaxpr/ybs,rahs->rabyh/dot_general | solution.py:180
  421.7 10.7 %fusion.291 = bf16[16,2,8,8,16,16]{5,3,2,1,4,0:T(8,128)(2,1)} fusion(bf16[16,2,8,8,16,16]{5,3,2,1,4,0:T(8,128)(2,1)} %get-tuple-element.326, s32[]{:T(128)} %get-tuple-element.325, f32[2,16,16384]{2,1,0:T(8,128)S(1)} %get-tuple-element.340, f32[8,16384]{1,0:T(8,128)S(1)} %get-tuple-element.341, pred[16,16384]{1,0:T(8,128)(4,1)S(1)} %compare_and_fusion.2, ...), kind=kOutput, calls=%fused_computation.14.clone.1 | convolution fusion | flops 1084227584 | bytes 4194816 | tf_op jit(solution)/shard_map/while/body/eval_jaxpr/ybs,rahs->rabyh/dot_general | solution.py:180
  432.6 5.8 %fusion.68 = f32[128,8,16,1,2,1,16]{0,6,4,2,1,5,3:T(8,128)S(1)} fusion(bf16[128,8,2,16,16,1]{4,0,3,2,1,5:T(8,128)(2,1)} %bitcast.437, bf16[2,2,64,64]{3,2,1,0:T(8,128)(2,1)S(1)} %copy-done.42, bf16[2,2,64,64]{3,2,1,0:T(8,128)(2,1)S(1)} %copy-done.41, bf16[2,2,64,64]{3,2,1,0:T(8,128)(2,1)S(1)} %copy-done.38), kind=kOutput, calls=%fused_computation.98 | convolution fusion | flops 268959744 | bytes 3244032 | tf_op jit(solution)/shard_map/tcoi,ipcsxyh->opsxtyh/dot_general | solution.py:70
  464.4 20.1 %collective-permute-done = bf16[128,1,1,16,16,16]{0,5,4,3,2,1:T(8,128)(2,1)S(1)} collective-permute-done((bf16[128,1,1,16,16,16]{0,5,4,3,2,1:T(8,128)(2,1)S(1)}, bf16[128,1,1,16,16,16]{0,5,4,3,2,1:T(8,128)(2,1)S(1)}, u32[]{:S(2)}, u32[]{:S(2)}) %collective-permute-start) | collective-permute-done | bytes 1048608 | tf_op jit(solution)/shard_map/ppermute | solution.py:22
  511.7 22.3 %collective-permute-done.2 = bf16[128,1,1,16,16,16]{0,5,4,3,2,1:T(8,128)(2,1)S(1)} collective-permute-done((bf16[128,1,1,16,16,16]{0,5,4,3,2,1:T(8,128)(2,1)S(1)}, bf16[128,1,1,16,16,16]{0,5,4,3,2,1:T(8,128)(2,1)S(1)}, u32[]{:S(2)}, u32[]{:S(2)}) %collective-permute-start.2) | collective-permute-done | bytes 1048608 | tf_op jit(solution)/shard_map/ppermute | solution.py:22
  (330 shorter events, 130.8 us)
Async XLA Ops:
  2.0 2.0 copy-start
  6.8 2.5 copy-start.8
  9.2 2.9 copy-start.32
  39.6 17.8 %copy-start.1 = (bf16[11,2,2,2,4096]{4,3,2,1,0:T(2,128)(2,1)S(1)}, bf16[11,2,2,2,4096]{4,3,2,1,0:T(2,128)(2,1)}, u32[]{:S(2)}) copy-start(bf16[11,2,2,2,4096]{4,3,2,1,0:T(2,128)(2,1)} %param.9) | copy-start | bytes 2162692
  45.5 134.6 %all-to-all-start = ((s32[2,128,128]{2,0,1:T(2,128)}), s32[2,128,128]{2,0,1:T(2,128)S(1)}, u32[]{:S(2)}, u32[]{:S(2)}) async-start(s32[2,128,128]{2,0,1:T(2,128)} %copy.186), calls=%async_computation | async-start | bytes 262144 | tf_op jit(solution)/shard_map/all_to_all | solution.py:151
  63.7 83.3 %copy-start.2 = (bf16[32,8192]{1,0:T(8,128)(2,1)S(1)}, bf16[32,8192]{1,0:T(8,128)(2,1)}, u32[]{:S(2)}) copy-start(bf16[32,8192]{1,0:T(8,128)(2,1)} %param.6) | copy-start | bytes 1572868
  71.1 105.2 %copy-start.61 = (f32[16]{0:T(128)}, f32[16]{0:T(128)S(1)}, u32[]{:S(2)}) copy-start(f32[16]{0:T(128)S(1)} %get-tuple-element.242) | copy-start | bytes 196
  71.2 106.0 %copy-start.59 = (f32[16]{0:T(128)}, f32[16]{0:T(128)S(1)}, u32[]{:S(2)}) copy-start(f32[16]{0:T(128)S(1)} %get-tuple-element.241) | copy-start | bytes 196
  75.6 102.3 %copy-start.53 = (f32[16]{0:T(128)}, f32[16]{0:T(128)S(1)}, u32[]{:S(2)}) copy-start(f32[16]{0:T(128)S(1)} %get-tuple-element.248) | copy-start | bytes 196
  75.7 103.1 %copy-start.51 = (f32[16]{0:T(128)}, f32[16]{0:T(128)S(1)}, u32[]{:S(2)}) copy-start(f32[16]{0:T(128)S(1)} %get-tuple-element.247) | copy-start | bytes 196
  180.1 54.7 %all-to-all-start.1 = ((bf16[32,128,128]{2,0,1:T(8,128)(2,1)}), bf16[32,128,128]{2,0,1:T(8,128)(2,1)S(1)}, u32[]{:S(2)}, u32[]{:S(2)}) async-start(bf16[32,128,128]{2,0,1:T(8,128)(2,1)} %copy.190), calls=%async_computation.1 | async-start | bytes 2097152 | tf_op jit(solution)/shard_map/all_to_all | solution.py:144
  236.6 195.9 %copy-start.38 = (bf16[2,2,64,64]{3,2,1,0:T(8,128)(2,1)S(1)}, bf16[2,2,64,64]{3,2,1,0:T(8,128)(2,1)}, u32[]{:S(2)}) copy-start(bf16[2,2,64,64]{3,2,1,0:T(8,128)(2,1)} %fusion.265) | copy-start | bytes 98308
  236.6 195.9 %copy-start.41 = (bf16[2,2,64,64]{3,2,1,0:T(8,128)(2,1)S(1)}, bf16[2,2,64,64]{3,2,1,0:T(8,128)(2,1)}, u32[]{:S(2)}) copy-start(bf16[2,2,64,64]{3,2,1,0:T(8,128)(2,1)} %get-tuple-element.207) | copy-start | bytes 98308
  236.6 196.0 %copy-start.42 = (bf16[2,2,64,64]{3,2,1,0:T(8,128)(2,1)S(1)}, bf16[2,2,64,64]{3,2,1,0:T(8,128)(2,1)}, u32[]{:S(2)}) copy-start(bf16[2,2,64,64]{3,2,1,0:T(8,128)(2,1)} %get-tuple-element.208) | copy-start | bytes 98308
  460.1 2.1 copy-start.35
  460.1 2.1 copy-start.36
  460.7 23.8 %copy-start.37 = (bf16[2,2,64,64]{3,2,1,0:T(8,128)(2,1)S(1)}, bf16[2,2,64,64]{3,2,1,0:T(8,128)(2,1)}, u32[]{:S(2)}) copy-start(bf16[2,2,64,64]{3,2,1,0:T(8,128)(2,1)} %fusion.264) | copy-start | bytes 98308
  460.7 23.8 %copy-start.39 = (bf16[2,2,64,64]{3,2,1,0:T(8,128)(2,1)S(1)}, bf16[2,2,64,64]{3,2,1,0:T(8,128)(2,1)}, u32[]{:S(2)}) copy-start(bf16[2,2,64,64]{3,2,1,0:T(8,128)(2,1)} %get-tuple-element.191) | copy-start | bytes 98308
  460.8 23.8 %copy-start.40 = (bf16[2,2,64,64]{3,2,1,0:T(8,128)(2,1)S(1)}, bf16[2,2,64,64]{3,2,1,0:T(8,128)(2,1)}, u32[]{:S(2)}) copy-start(bf16[2,2,64,64]{3,2,1,0:T(8,128)(2,1)} %get-tuple-element.192) | copy-start | bytes 98308
  460.8 23.8 %collective-permute-start = (bf16[128,1,1,16,16,16]{0,5,4,3,2,1:T(8,128)(2,1)S(1)}, bf16[128,1,1,16,16,16]{0,5,4,3,2,1:T(8,128)(2,1)S(1)}, u32[]{:S(2)}, u32[]{:S(2)}) collective-permute-start(bf16[128,1,1,16,16,16]{0,5,4,3,2,1:T(8,128)(2,1)S(1)} %pad_maximum_fusion.1), channel_id=1, source_target_pairs={{0,16},{16,0},{32,48},{48,32},{64,80},{80,64},{96,112},{112,96},{1... | collective-permute-start | bytes 3145736 | tf_op jit(solution)/shard_map/ppermute | solution.py:22
  484.6 1.2 copy-start.33
  484.6 1.2 copy-start.34
  489.3 1.9 copy-start.52
  489.3 1.9 copy-start.54
  493.4 2.6 copy-start.31
  494.0 5.0 copy-start.5
  494.0 5.0 copy-start.6
  494.1 4.2 collective-permute-start.1
  507.4 3.6 copy-start.30
  508.0 26.5 %copy-start.3 = (bf16[1,64,4096]{2,1,0:T(8,128)(2,1)S(1)}, bf16[1,64,4096]{2,1,0:T(8,128)(2,1)}, u32[]{:S(2)}) copy-start(bf16[1,64,4096]{2,1,0:T(8,128)(2,1)} %get-tuple-element.150) | copy-start | bytes 1572868
  508.0 26.5 %copy-start.4 = (bf16[1,64,4096]{2,1,0:T(8,128)(2,1)S(1)}, bf16[1,64,4096]{2,1,0:T(8,128)(2,1)}, u32[]{:S(2)}) copy-start(bf16[1,64,4096]{2,1,0:T(8,128)(2,1)} %get-tuple-element.151) | copy-start | bytes 1572868
  508.0 26.0 %collective-permute-start.2 = (bf16[128,1,1,16,16,16]{0,5,4,3,2,1:T(8,128)(2,1)S(1)}, bf16[128,1,1,16,16,16]{0,5,4,3,2,1:T(8,128)(2,1)S(1)}, u32[]{:S(2)}, u32[]{:S(2)}) collective-permute-start(bf16[128,1,1,16,16,16]{0,5,4,3,2,1:T(8,128)(2,1)S(1)} %pad_maximum_fusion.3), channel_id=1, source_target_pairs={{0,32},{16,48},{32,0},{48,16},{64,96},{80,112},{96,64},{112,80},{1... | collective-permute-start | bytes 3145736 | tf_op jit(solution)/shard_map/ppermute | solution.py:22
  (38 other events, 31.4 us)
where the time goes:
time: 546 us; the launch traced here: 537 us
  matrix products  185 us (34%)
  local copies, waits for them, and re-layouts  114 us (21%)
  other arithmetic  91.4 us (17%)
  between operations  73.1 us (13%)
  waiting for transfers between devices  44.2 us (8%)
  starting transfers between devices  28.3 us (5%)
    dot_general x16, matrix products, one_column(): jnp.einsum('ybs,rahs->rabyh', table, spread, preferred_element_type=jnp.f...  171 us
    another operation x18, other arithmetic  46.8 us
    ppermute x3, waiting for transfers between devices, partner_2(): return lax.ppermute(value, axis, pairs)  44.2 us
    scatter x1, local copies, waits for them, and re-layouts, body(): jnp.zeros((2, devices * CAP), jnp.int32).at[:, place].set(src_point)  24.7 us
    scatter x1, local copies, waits for them, and re-layouts, body(): jnp.zeros((2 * fields, devices * CAP), jnp.bfloat16).at[:, place]  23.8 us
    all_to_all x1, starting transfers between devices, body(): lax.all_to_all(send_pts.reshape(2, devices, CAP), ('gx', 'gy'), split_axi...  11.8 us
    concatenate x10, other arithmetic, rotate(): jnp.concatenate([upper * cosine - lower * sine, upper * sine + lower * co...  11.4 us
  transfers between devices with their start and end apart: 5, of which 3 were waited for; matrix products, arithmetic and copies ran while one was open for 18% of the time, Pallas kernels for 0%

commit v1 on v0

v1 whole, which is shorter than its diff:
```python
import math

import jax
import jax.numpy as jnp
from jax import lax
from jax.experimental import pallas as pl
from jax.experimental.pallas import tpu as pltpu
from jax.sharding import PartitionSpec as P

QX = 8
R = 64
LEVX = 4
LB = 16
LAT = 16
CAP = 128

F32 = jnp.float32
BF16 = jnp.bfloat16
MODULUS = 61.0

ROUTE_STEP = 1024
ROUTE_BLOCK = 256
LEAF_SOURCES = 8
MIB = 1024 * 1024


def matmul_nt(lhs, rhs):
    return lax.dot_general(lhs, rhs, (((1,), (1,)), ((), ())), preferred_element_type=F32)


def unit_phase(product):
    rest = product - MODULUS * jnp.floor(product * (1.0 / MODULUS) + 0.5)
    x = rest * (math.pi / MODULUS)
    x2 = x * x
    s = x * (1.0 + x2 * (-1 / 6 + x2 * (1 / 120 + x2 * (-1 / 5040 + x2 * (1 / 362880 + x2 * (-1 / 39916800))))))
    c = 1.0 + x2 * (-1 / 2 + x2 * (1 / 24 + x2 * (-1 / 720 + x2 * (1 / 40320 + x2 * (-1 / 3628800)))))
    return 1.0 - 2.0 * s * s, 2.0 * s * c


def iota(shape, dim):
    return lax.broadcasted_iota(jnp.int32, shape, dim)


def reversed_bits(value, bits):
    out = 0
    for bit in range(bits):
        out |= (value >> bit & 1) << (bits - 1 - bit)
    return out


def nibble_reversed(value):
    return (value & 1) << 3 | (value & 2) << 1 | value >> 1 & 2 | value >> 3 & 1


def route_kernel(own_ref, point_ref, value_ref, send_ref, acc, carry, tri, points, left, right):
    step = pl.program_id(0)
    width = ROUTE_BLOCK

    @pl.when(step == 0)
    def _():
        acc[...] = jnp.zeros_like(acc)
        carry[...] = jnp.zeros_like(carry)
        earlier = (iota((width, width + 128), 0) < iota((width, width + 128), 1))
        earlier = earlier | (iota((width, width + 128), 1) >= width)
        tri[...] = jnp.where(earlier, 1.0, 0.0).astype(BF16)

    rows = iota((128, width), 0)
    for block in range(ROUTE_STEP // width):
        span = pl.ds(block * width, width)
        own = own_ref[0:1, span]
        hit = rows == own
        counts = jnp.dot(
            jnp.where(hit, 1.0, 0.0).astype(BF16), tri[...], preferred_element_type=F32
        )
        held = carry[...]
        before = counts[:, :width] + jnp.concatenate([held] * (width // 128), axis=1)
        rank = jnp.sum(jnp.where(hit, before, 0.0), axis=0, keepdims=True)
        carry[...] = held + counts[:, width:]

        sibling = own >> 4 & 3
        low = (own >> 6) * 16 + (own & 15)
        place = jnp.where(rows.astype(F32) == rank, 1.0, 0.0)
        for y in range(4):
            right[y * 128 : (y + 1) * 128, span] = jnp.where(sibling == y, place, 0.0).astype(BF16)

        px = point_ref[0:1, span]
        py = point_ref[1:2, span]
        big_x = (own >> 4) * (LB * LAT) + px
        big_y = (own & 15) * (LB * LAT) + py
        cosine, sine = unit_phase(big_x.astype(F32) * big_y.astype(F32))
        real = value_ref[0:16, span].astype(F32)
        imag = value_ref[16:32, span].astype(F32)
        turned_real = cosine * real - sine * imag
        turned_imag = sine * real + cosine * imag
        parts = []
        for group in range(4):
            parts.append(turned_real[4 * group : 4 * group + 4])
            parts.append(turned_imag[4 * group : 4 * group + 4])
        charge = jnp.concatenate(parts, axis=0).astype(BF16)
        box = (nibble_reversed(px >> 4) * 16 + nibble_reversed(py >> 4)).astype(F32)
        offset = ((px & 15) * 16 + (py & 15)).astype(F32)
        mine = jnp.where(iota((32, width), 0) == low, 1.0, 0.0)
        left[1024:1056, span] = (mine * box).astype(BF16)
        left[1056:1088, span] = (mine * offset).astype(BF16)
        for number in range(32):
            mask = jnp.where(low == number, 1.0, 0.0).astype(BF16)
            left[number * 32 : (number + 1) * 32, span] = charge * mask

    acc[...] += matmul_nt(left[...], right[...])

    @pl.when(step == pl.num_programs(0) - 1)
    def _():
        for y in range(4):
            points[y] = acc[1024:1088, y * 128 : (y + 1) * 128]

        def one(number, carried):
            high = number // 16
            gy = number % 16
            taken = [
                points[y, pl.ds(32 * kind + number, 1), :]
                for kind in range(2)
                for y in range(4)
            ]
            taken = jnp.concatenate(taken, axis=0).astype(BF16)
            for group in range(4):
                dest = high * 64 + group * 16 + gy
                base = pl.multiple_of(number * 32 + group * 8, 8)
                for y in range(4):
                    send_ref[dest, y] = acc[pl.ds(base, 8), y * 128 : (y + 1) * 128].astype(BF16)
                send_ref[dest, 4] = taken
            return carried

        lax.fori_loop(0, 32, one, 0)


def route(owner, point, value):
    sources = owner.shape[1]
    return pl.pallas_call(
        route_kernel,
        grid=(sources // ROUTE_STEP,),
        in_specs=[
            pl.BlockSpec((1, ROUTE_STEP), lambda i: (0, i)),
            pl.BlockSpec((2, ROUTE_STEP), lambda i: (0, i)),
            pl.BlockSpec((32, ROUTE_STEP), lambda i: (0, i)),
        ],
        out_specs=pl.BlockSpec((128, 5, 8, 128), lambda i: (0, 0, 0, 0)),
        out_shape=jax.ShapeDtypeStruct((128, 5, 8, 128), BF16),
        scratch_shapes=[
            pltpu.VMEM((1088, 512), F32),
            pltpu.VMEM((128, 128), F32),
            pltpu.VMEM((ROUTE_BLOCK, ROUTE_BLOCK + 128), BF16),
            pltpu.VMEM((4, 64, 128), F32),
            pltpu.VMEM((1088, ROUTE_STEP), BF16),
            pltpu.VMEM((512, ROUTE_STEP), BF16),
        ],
        compiler_params=pltpu.CompilerParams(vmem_limit_bytes=40 * MIB),
        name="route",
    )(owner, point, value)


def nodes_and_scales():
    nodes = [0.5 + 0.5 * math.cos(math.pi * (2 * a + 1) / (2 * QX)) for a in range(QX)]
    scales = []
    for a in range(QX):
        scale = 1.0
        for c in range(QX):
            if c != a:
                scale /= nodes[a] - nodes[c]
        scales.append(scale)
    return nodes, scales


def column(values, shape):
    row = iota(shape, 0)
    out = jnp.full(shape, values[0], F32)
    for index in range(1, len(values)):
        out = jnp.where(row == index, values[index], out)
    return out


def interpolation(position, nodes, scales):
    gap = position - nodes
    one = jnp.roll(gap, -1, axis=0)
    two = one * jnp.roll(one, -1, axis=0)
    four = two * jnp.roll(two, -2, axis=0)
    return scales * four * jnp.roll(two, -4, axis=0) * jnp.roll(one, -6, axis=0)


def turn(values, cosine, sine):
    return values * cosine + pltpu.roll(values, 64, axis=values.ndim - 1) * sine


def signs(shape):
    return jnp.where(iota(shape, len(shape) - 1) < 64, -1.0, 1.0)


def inner_kernel(
    where_ref, got_ref, mats_ref, out_ref, points, total, held, work, left0, right0, left1, right1
):
    row_high = where_ref[0]
    row_y = where_ref[1]
    chunk = LEAF_SOURCES
    chunks = 128 // chunk

    points[...] = got_ref[:, 4].astype(F32)
    total[...] = jnp.zeros_like(total)

    nodes, scales = nodes_and_scales()
    nodes = column(nodes, (8, 128))
    scales = column(scales, (8, 128))
    cells = iota((256, 128), 0).astype(F32)

    def build(turn_number, left, right):
        y = turn_number // chunks
        first = (turn_number % chunks) * chunk
        for i in range(chunk):
            span = pl.ds(i * 128, 128)
            source = first + i
            charge = got_ref[source, y].astype(F32)
            box = points[source, pl.ds(y, 1), :]
            offset = points[source, pl.ds(4 + y, 1), :]
            left[:, span] = jnp.where(cells == box, 1.0, 0.0).astype(BF16)
            coarse = jnp.floor(offset * (1.0 / 16))
            fine = offset - 16.0 * coarse
            over_x = interpolation((coarse + 0.5) * (1.0 / LAT), nodes, scales)
            over_y = interpolation((fine + 0.5) * (1.0 / LAT), nodes, scales)
            both = jnp.concatenate(
                [over_x[a : a + 1] * over_y for a in range(QX)], axis=0
            ).astype(BF16)
            for h in range(4):
                for part in range(2):
                    row = charge[part * 4 + h : part * 4 + h + 1].astype(BF16)
                    base = (h * 2 + part) * 64
                    right[base : base + 64, span] = both * row

    def product(turn_number, left, right):
        y = turn_number // chunks
        total[y] += matmul_nt(left[...], right[...])

    turns = 4 * chunks
    build(0, left0, right0)

    def pair(i, carried):
        build(2 * i + 1, left1, right1)
        product(2 * i, left0, right0)
        build(jnp.minimum(2 * i + 2, turns - 1), left0, right0)
        product(2 * i + 1, left1, right1)
        return carried

    lax.fori_loop(0, turns // 2, pair, 0)

    for y in range(4):
        for h in range(4):
            held[pl.ds(y * 4 + h, 256, stride=16), :] = total[y, :, h * 128 : (h + 1) * 128]
    for x in range(16):
        work[x] = held[x * 256 : (x + 1) * 256].astype(BF16).reshape(16, 16, 128)

    sign16 = signs((16, 128))
    member = (iota((16, 128), 0) >> 2).astype(F32)
    row_x = row_high.astype(F32) * 4.0 + member
    row_y_f = row_y.astype(F32)

    for depth in range(LEVX):
        below = LEVX - 1 - depth
        count = 2**below
        for axis in range(2):
            mats = mats_ref[2 * depth + axis]
            for high in range(2**depth):
                for low in range(count):
                    start = high << below + 1 | low
                    parent = reversed_bits(low, below)
                    ends = [start, start | 1 << below]
                    if axis == 0:
                        both = [work[e].reshape(256, 128) for e in ends]
                    else:
                        both = [work[:, e].reshape(256, 128) for e in ends]
                    made = matmul_nt(jnp.concatenate(both, axis=1), mats)
                    for t in range(2):
                        target = float(2 * high + t)
                        if axis == 0:
                            cosine, sine = unit_phase((row_x * float(count) + float(parent)) * target)
                        else:
                            cosine, sine = unit_phase(
                                jnp.full((16, 128), 1.0, F32)
                                * ((row_y_f * float(count) + float(parent)) * target)
                            )
                        piece = made[:, t * 128 : (t + 1) * 128].reshape(16, 16, 128)
                        piece = turn(piece, cosine[None], (sine * sign16)[None])
                        e = ends[t]
                        if axis == 0:
                            work[e] = piece.astype(BF16)
                        elif depth < LEVX - 1:
                            work[:, e] = piece.astype(BF16)
                        else:
                            for x in range(16):
                                held[(x * 16 + e) * 16 : (x * 16 + e + 1) * 16] = piece[x]

    key = iota((16, 8, 128), 0).astype(F32)
    sign8 = signs((16, 8, 128))
    mats = mats_ref[2 * LEVX]
    for pair_number in range(2):
        tables = []
        for t in range(2):
            parent = row_high.astype(F32) * 2.0 + float(pair_number)
            cosine, sine = unit_phase(parent * (2.0 * key + float(t)))
            tables.append((cosine[:, None], (sine * sign8)[:, None]))
        for h in range(4):
            both = [
                held[pl.ds((2 * pair_number + c) * 4 + h, 256, stride=16), :].astype(BF16)
                for c in range(2)
            ]
            made = matmul_nt(jnp.concatenate(both, axis=1), mats)
            for t in range(2):
                piece = made[:, t * 128 : (t + 1) * 128].reshape(16, 2, 8, 128)
                piece = turn(piece, *tables[t]).reshape(256, 128)
                out_ref[pair_number, t, h] = piece.astype(BF16)


def inner(where, got, mats):
    width = LEAF_SOURCES * 128
    vmem = pl.BlockSpec(memory_space=pltpu.VMEM)
    return pl.pallas_call(
        inner_kernel,
        in_specs=[pl.BlockSpec(memory_space=pltpu.SMEM), vmem, vmem],
        out_specs=vmem,
        out_shape=jax.ShapeDtypeStruct((2, 2, 4, 256, 128), BF16),
        scratch_shapes=[
            pltpu.VMEM((128, 8, 128), F32),
            pltpu.VMEM((4, 256, 512), F32),
            pltpu.VMEM((4096, 128), F32),
            pltpu.VMEM((16, 16, 16, 128), BF16),
            pltpu.VMEM((256, width), BF16),
            pltpu.VMEM((512, width), BF16),
            pltpu.VMEM((256, width), BF16),
            pltpu.VMEM((512, width), BF16),
        ],
        compiler_params=pltpu.CompilerParams(vmem_limit_bytes=48 * MIB),
        name="inner",
    )(where, got, mats)


def outer_kernel(where_ref, mine_ref, other_ref, mats_y_ref, mats_x_ref, out_ref, work):
    row_high = where_ref[0].astype(F32)
    row_y = where_ref[1]
    parent_y = (row_y >> 1).astype(F32)
    core = (row_y & 1).astype(F32)
    target = 2.0 * iota((16, 128), 0).astype(F32) + core
    cosine, sine = unit_phase(parent_y * target)
    table = (cosine[None], (sine * signs((16, 128)))[None])
    mats_y = mats_y_ref[...]
    mats_x = mats_x_ref[...]
    key = iota((16, 8, 128), 0).astype(F32)
    sign8 = signs((16, 8, 128))
    for t8 in range(2):
        tables = []
        for t in range(2):
            cosine, sine = unit_phase(row_high * (2.0 * (2.0 * key + float(t8)) + float(t)))
            tables.append((cosine[:, None], (sine * sign8)[:, None]))
        for h in range(4):
            both = []
            for c in range(2):
                pair = jnp.concatenate([mine_ref[c, t8, h], other_ref[c, t8, h]], axis=1)
                made = matmul_nt(pair, mats_y).reshape(16, 16, 128)
                both.append(turn(made, *table).reshape(256, 128).astype(BF16))
            made = matmul_nt(jnp.concatenate(both, axis=1), mats_x)
            for t in range(2):
                piece = made[:, t * 128 : (t + 1) * 128].reshape(16, 2, 8, 128)
                piece = turn(piece, *tables[t]).reshape(256, 128)
                out_ref[2 * t + t8, h] = piece.astype(BF16)


def outer(where, mine, other, mats_y, mats_x):
    vmem = pl.BlockSpec(memory_space=pltpu.VMEM)
    return pl.pallas_call(
        outer_kernel,
        in_specs=[pl.BlockSpec(memory_space=pltpu.SMEM), vmem, vmem, vmem, vmem],
        out_specs=vmem,
        out_shape=jax.ShapeDtypeStruct((4, 4, 256, 128), BF16),
        scratch_shapes=[pltpu.VMEM((8, 128), F32)],
        compiler_params=pltpu.CompilerParams(vmem_limit_bytes=40 * MIB),
        name="outer",
    )(where, mine, other, mats_y, mats_x)


def finish_kernel(got_ref, out_ref, held):
    for group in range(4):
        for h in range(4):
            held[pl.ds(group * 4 + h, 256, stride=16), :] = got_ref[group, h].astype(F32)
    for block in range(32):
        span = slice(block * 128, (block + 1) * 128)
        out_ref[:, span] = held[span].T.astype(BF16)


def finish(got):
    vmem = pl.BlockSpec(memory_space=pltpu.VMEM)
    return pl.pallas_call(
        finish_kernel,
        in_specs=[vmem],
        out_specs=vmem,
        out_shape=jax.ShapeDtypeStruct((128, 4096), BF16),
        scratch_shapes=[pltpu.VMEM((4096, 128), F32)],
        compiler_params=pltpu.CompilerParams(vmem_limit_bytes=40 * MIB),
        name="finish",
    )(got)


def block_matrices(translation):
    parts = translation.reshape(-1, 2, 2, 2, R, R)
    real = parts[:, :, :, 0]
    imag = parts[:, :, :, 1]
    top = jnp.stack([real, -imag], axis=4)
    bottom = jnp.stack([imag, real], axis=4)
    whole = jnp.stack([top, bottom], axis=2)
    whole = jnp.transpose(whole, (0, 1, 2, 4, 3, 5, 6))
    return whole.reshape(-1, 4 * R, 4 * R)


def body(src_value, src_point, src_owner, translation):
    row_x = lax.axis_index("gx")
    row_y = lax.axis_index("gy")
    where = jnp.stack([row_x >> 2, row_y]).astype(jnp.int32)
    mats = block_matrices(translation)

    send = route(src_owner.reshape(1, -1), src_point, src_value)
    got = lax.all_to_all(send, ("gx", "gy"), split_axis=0, concat_axis=0, tiled=True)
    mine = inner(where, got, mats)

    pairs = [(i, i ^ 1) for i in range(lax.axis_size("gy"))]
    other = lax.ppermute(mine, "gy", pairs)
    core = row_y & 1
    rows = lax.dynamic_slice_in_dim(mats[2 * LEVX + 1], core * 128, 128, axis=0)
    mats_y = jnp.where(
        core == 0, rows, jnp.concatenate([rows[:, 128:], rows[:, :128]], axis=1)
    )
    out = outer(where, mine, other, mats_y, mats[2 * LEVX + 2])
    groups = [[0, 1, 2, 3], [4, 5, 6, 7]]
    out = lax.all_to_all(
        out, "gx", split_axis=0, concat_axis=0, axis_index_groups=groups, tiled=True
    )
    return finish(out).reshape(128, 1, 1, 4096)


def solution(mesh):
    return jax.shard_map(
        body,
        mesh=mesh,
        in_specs=(P(None, ("gx", "gy")), P(None, ("gx", "gy")), P(("gx", "gy"), None), P()),
        out_specs=P(None, "gx", "gy", None),
        check_vma=False,
    )
```

time: 546 us -> 123 us (0.23); the launches traced: 537 us -> 122 us
  matrix products: 185 us -> 0 us
  local copies, waits for them, and re-layouts: 114 us -> 18.5 us
  other arithmetic: 91.4 us -> 1.49 us
  between operations: 73.1 us -> 0.15 us
  Pallas kernels: 0 us -> 65.9 us
  waiting for transfers between devices: 44.2 us -> 6.39 us
  blocking collectives: 0 us -> 17.3 us
  starting transfers between devices: 28.3 us -> 12.7 us
    dot_general x27 -> x0, matrix products: 185 us -> none  [the longest x16 171 us: one_column(): jnp.einsum('ybs,rahs->rabyh', table, spread, preferred_element_type=jnp.f...]
    pallas_call x0 -> x4, Pallas kernels: none -> 65.9 us  [the longest x1 45.7 us: inner(): pl.pallas_call(inner_kernel, in_specs=[pl.BlockSpec(memory_space=pltpu.SM...]
    scatter x2 -> x0, local copies, waits for them, and re-layouts: 48.5 us -> none  [the longest x1 24.7 us: body(): jnp.zeros((2, devices * CAP), jnp.int32).at[:, place].set(src_point)]
    another operation x20 -> x2, other arithmetic: 47.2 us -> 0.72 us  [the longest x1 0.64 us: block_matrices(): whole = jnp.stack([top, bottom], axis=2)]
    ppermute x3 -> x1, waiting for transfers between devices: 44.2 us -> 0.38 us  [body(): other = lax.ppermute(mine, 'gy', pairs)]
    all_to_all x0 -> x1, blocking collectives: none -> 17.3 us  [body(): lax.all_to_all(out, 'gx', split_axis=0, concat_axis=0, axis_index_groups=...]
    slice x29 -> x4, local copies, waits for them, and re-layouts: 18.1 us -> 1.63 us  [the longest x2 1.34 us: body(): out = outer(where, mine, other, mats_y, mats[2 * LEVX + 2])]
    concatenate x10 -> x0, other arithmetic: 11.4 us -> none  [rotate(): jnp.concatenate([upper * cosine - lower * sine, upper * sine + lower * co...]
  transfers between devices with their start and end apart: 5 -> 2, of which waited for: 3 -> 2; matrix products, arithmetic and copies ran while one was open for 18% -> 13% of each run, Pallas kernels for 0% -> 0%
where the time goes in v1:
time: 123 us; the launch traced here: 122 us
  Pallas kernels  65.9 us (54%)
  local copies, waits for them, and re-layouts  18.5 us (15%)
  blocking collectives  17.3 us (14%)
  starting transfers between devices  12.7 us (10%)
  waiting for transfers between devices  6.39 us (5%)
  other arithmetic  1.49 us (1%)
    pallas_call x1, Pallas kernels, inner(): pl.pallas_call(inner_kernel, in_specs=[pl.BlockSpec(memory_space=pltpu.SM...  45.7 us
    all_to_all x1, blocking collectives, body(): lax.all_to_all(out, 'gx', split_axis=0, concat_axis=0, axis_index_groups=...  17.3 us
    pallas_call x1, Pallas kernels, route(): pl.pallas_call(route_kernel, grid=(sources // ROUTE_STEP,), in_specs=[pl....  14.7 us
    all_to_all x1, starting transfers between devices, body(): lax.all_to_all(send, ('gx', 'gy'), split_axis=0, concat_axis=0, tiled=True)  11.5 us
    all_to_all x1, waiting for transfers between devices, body(): lax.all_to_all(send, ('gx', 'gy'), split_axis=0, concat_axis=0, tiled=True)  6.02 us
    reshape x1, local copies, waits for them, and re-layouts, block_matrices(): return whole.reshape(-1, 4 * R, 4 * R)  5.67 us
    unnamed x11, local copies, waits for them, and re-layouts  5.1 us
    transpose x1, local copies, waits for them, and re-layouts, block_matrices(): whole = jnp.transpose(whole, (0, 1, 2, 4, 3, 5, 6))  4.58 us
  transfers between devices with their start and end apart: 2, of which 2 were waited for; matrix products, arithmetic and copies ran while one was open for 13% of the time, Pallas kernels for 0%

profile of v1, /device:TPU:1, one launch (start us, length us, event | category | flops | bytes accessed | tf_op | source)
XLA Modules:
  0.0 122.4 jit_solution(10202718615935720147)
XLA Ops:
  0.0 0.0 copy-start
  0.0 1.0 copy-done
  1.0 0.0 copy-start.1
  1.0 0.8 copy-done.1
  1.9 0.8 copy-done.2
  2.6 14.7 %route.1 = bf16[128,5,8,128]{3,2,1,0:T(8,128)(2,1)} custom-call(s32[1,8192]{1,0:T(1,128)S(1)} %bitcast.18, s32[2,8192]{1,0:T(2,128)S(1)} %copy-done.1, bf16[32,8192]{1,0:T(8,128)(2,1)S(1)} %copy-done), custom_call_target="tpu_custom_call" | custom-call | tf_op jit(solution)/shard_map/route/pallas_call | solution.py:138
  17.4 0.0 copy-start.4
  17.4 11.5 %all-to-all-start = ((bf16[128,5,8,128]{3,2,1,0:T(8,128)(2,1)}), bf16[128,5,8,128]{3,2,1,0:T(8,128)(2,1)S(1)}, u32[]{:S(2)}, u32[]{:S(2)}) async-start(bf16[128,5,8,128]{3,2,1,0:T(8,128)(2,1)} %route.1), calls=%async_computation | async-start | bytes 2621440 | tf_op jit(solution)/shard_map/all_to_all | solution.py:425
  28.9 0.0 copy-done.4
  28.9 0.9 copy.8
  29.8 0.9 reshape.27
  30.7 0.1 fusion
  30.8 0.1 slice_bitcast_fusion
  31.0 0.6 maximum_bitcast_fusion.1
  31.6 0.6 maximum_bitcast_fusion
  32.3 0.0 copy-start.3
  32.3 1.6 %copy-done.3 = bf16[11,2,2,64,2,2,64]{6,3,4,1,0,5,2:T(8,128)(2,1)} copy-done((bf16[11,2,2,64,2,2,64]{6,3,4,1,0,5,2:T(8,128)(2,1)}, bf16[11,2,2,64,2,2,64]{6,3,4,1,0,5,2:T(8,128)(2,1)S(1)}, u32[]{:S(2)}) %copy-start.3) | copy-done | bytes 1441816
  33.9 4.6 %copy.9 = bf16[11,2,2,64,2,2,64]{6,5,4,3,2,1,0:T(2,128)(2,1)} copy(bf16[11,2,2,64,2,2,64]{6,3,4,1,0,5,2:T(8,128)(2,1)S(1)} %maximum_bitcast_fusion) | data formatting | bytes 2883584 | tf_op jit(solution)/shard_map/transpose | solution.py:414
  38.5 5.7 %reshape.28.mats_ref = bf16[11,256,256]{2,1,0:T(8,128)(2,1)S(1)} reshape(bf16[11,2,2,64,2,2,64]{6,5,4,3,2,1,0:T(2,128)(2,1)} %copy.9) | data formatting | bytes 2883584 | tf_op jit(solution)/shard_map/reshape | solution.py:415
  44.1 0.1 pad_add_fusion.where_ref
  44.2 6.0 %all-to-all-done.got_ref = bf16[128,5,8,128]{3,2,1,0:T(8,128)(2,1)S(1)} async-done(((bf16[128,5,8,128]{3,2,1,0:T(8,128)(2,1)}), bf16[128,5,8,128]{3,2,1,0:T(8,128)(2,1)S(1)}, u32[]{:S(2)}, u32[]{:S(2)}) %all-to-all-start) | async-done | bytes 1310752 | tf_op jit(solution)/shard_map/all_to_all | solution.py:425
  50.2 45.7 %inner.1.mine_ref = bf16[2,2,4,256,128]{4,3,2,1,0:T(8,128)(2,1)} custom-call(s32[2]{0:T(128)S(1)} %pad_add_fusion.where_ref, bf16[128,5,8,128]{3,2,1,0:T(8,128)(2,1)S(1)} %all-to-all-done.got_ref, bf16[11,256,256]{2,1,0:T(8,128)(2,1)S(1)} %reshape.28.mats_ref), custom_call_target="tpu_custom_call" | custom-call | tf_op jit(solution)/shard_map/inner/pallas_call | solution.py:322
  95.9 1.2 collective-permute-start
  97.1 1.1 fusion.1
  98.2 0.3 copy.10
  98.5 0.2 squeeze.10
  98.7 0.3 copy.11
  99.0 0.2 squeeze.11.mats_x_ref
  99.2 0.4 collective-permute-done.other_ref
  99.6 3.6 %outer.1 = bf16[4,4,256,128]{3,2,1,0:T(8,128)(2,1)S(1)} custom-call(s32[2]{0:T(128)S(1)} %pad_add_fusion.where_ref, bf16[2,2,4,256,128]{4,3,2,1,0:T(8,128)(2,1)} %inner.1.mine_ref, bf16[2,2,4,256,128]{4,3,2,1,0:T(8,128)(2,1)S(1)} %collective-permute-done.other_ref, bf16[128,256]{1,0:T(8,128)(2,1)S(1)} %maximum_select_fusion.mats_y_ref, ...), custom_call_target="tpu_custom_call" | custom-call | tf_op jit(solution)/shard_map/outer/pallas_call | solution.py:374
  103.3 17.3 %all_to_all.10.got_ref = bf16[4,4,256,128]{3,2,1,0:T(8,128)(2,1)S(1)} all-to-all(bf16[4,4,256,128]{3,2,1,0:T(8,128)(2,1)S(1)} %outer.1), channel_id=1, replica_groups={{0,16,32,48},{64,80,96,112},{1,17,33,49},{65,81,97,113},{2,18,34,50},{6..., dimensions={0} | all-to-all | bytes 2097152 | tf_op jit(solution)/shard_map/all_to_all | solution.py:437
  120.5 1.9 %finish.1 = bf16[128,4096]{1,0:T(8,128)(2,1)} custom-call(bf16[4,4,256,128]{3,2,1,0:T(8,128)(2,1)S(1)} %all_to_all.10.got_ref), custom_call_target="tpu_custom_call" | custom-call | tf_op jit(solution)/shard_map/finish/pallas_call | solution.py:396
  (3 shorter events, 0.0 us)
Async XLA Ops:
  0.0 1.0 copy-start
  1.0 0.8 copy-start.1
  1.9 0.8 copy-start.2
  17.4 11.5 %copy-start.4 = (bf16[11,2,2,2,4096]{4,3,2,1,0:T(2,128)(2,1)S(1)}, bf16[11,2,2,2,4096]{4,3,2,1,0:T(2,128)(2,1)}, u32[]{:S(2)}) copy-start(bf16[11,2,2,2,4096]{4,3,2,1,0:T(2,128)(2,1)} %param.7) | copy-start | bytes 2162692
  17.4 32.8 %all-to-all-start = ((bf16[128,5,8,128]{3,2,1,0:T(8,128)(2,1)}), bf16[128,5,8,128]{3,2,1,0:T(8,128)(2,1)S(1)}, u32[]{:S(2)}, u32[]{:S(2)}) async-start(bf16[128,5,8,128]{3,2,1,0:T(8,128)(2,1)} %route.1), calls=%async_computation | async-start | bytes 2621440 | tf_op jit(solution)/shard_map/all_to_all | solution.py:425
  32.3 1.6 %copy-start.3 = (bf16[11,2,2,64,2,2,64]{6,3,4,1,0,5,2:T(8,128)(2,1)}, bf16[11,2,2,64,2,2,64]{6,3,4,1,0,5,2:T(8,128)(2,1)S(1)}, u32[]{:S(2)}) copy-start(bf16[11,2,2,64,2,2,64]{6,3,4,1,0,5,2:T(8,128)(2,1)S(1)} %maximum_bitcast_fusion) | copy-start | bytes 4325380
  95.9 3.7 %collective-permute-start = (bf16[2,2,4,256,128]{4,3,2,1,0:T(8,128)(2,1)}, bf16[2,2,4,256,128]{4,3,2,1,0:T(8,128)(2,1)S(1)}, u32[]{:S(2)}, u32[]{:S(2)}) collective-permute-start(bf16[2,2,4,256,128]{4,3,2,1,0:T(8,128)(2,1)} %inner.1.mine_ref), channel_id=1, source_target_pairs={{0,1},{1,0},{2,3},{3,2},{4,5},{5,4},{6,7},{7,6},{8,9},{9,8},{10,11... | collective-permute-start | bytes 3145736 | tf_op jit(solution)/shard_map/ppermute | solution.py:429

commit v2 on v1

v2 whole, which is shorter than its diff:
```python
import functools
import math

import jax
import jax.numpy as jnp
from jax import lax
from jax.experimental import pallas as pl
from jax.experimental.pallas import tpu as pltpu
from jax.sharding import PartitionSpec as P

QX = 8
R = 64
LEVX = 4
LB = 16
LAT = 16
CAP = 128

F32 = jnp.float32
BF16 = jnp.bfloat16
MODULUS = 61.0
MIB = 1024 * 1024

BLOCK = 256
HALF = 2
RANK_UNROLL = 8
ROUTE_UNROLL = 4
POINT_UNROLL = 8
LEAF_UNROLL = 16


def matmul_nt(lhs, rhs):
    return lax.dot_general(lhs, rhs, (((1,), (1,)), ((), ())), preferred_element_type=F32)


def unit_phase(product):
    rest = product - MODULUS * jnp.floor(product * (1.0 / MODULUS) + 0.5)
    x = rest * (math.pi / MODULUS)
    x2 = x * x
    s = x * (1.0 + x2 * (-1 / 6 + x2 * (1 / 120 + x2 * (-1 / 5040 + x2 * (1 / 362880 + x2 * (-1 / 39916800))))))
    c = 1.0 + x2 * (-1 / 2 + x2 * (1 / 24 + x2 * (-1 / 720 + x2 * (1 / 40320 + x2 * (-1 / 3628800)))))
    return 1.0 - 2.0 * s * s, 2.0 * s * c


def cost(micros):
    return pl.CostEstimate(flops=int(micros * 1.0e9), bytes_accessed=0, transcendentals=0)


def iota(shape, dim):
    return lax.broadcasted_iota(jnp.int32, shape, dim)


def reversed_bits(value, bits):
    out = 0
    for bit in range(bits):
        out |= (value >> bit & 1) << (bits - 1 - bit)
    return out


def nibble_reversed(value):
    return (value & 1) << 3 | (value & 2) << 1 | value >> 1 & 2 | value >> 3 & 1


def one_hot(cells, row):
    return jnp.where(cells == row, jnp.ones((), BF16), jnp.zeros((), BF16))


def rank_sources(own_ref, point_ref, value_ref, rows_ref, charge_ref, tri, accs):
    width = BLOCK
    earlier = iota((width, width), 0) < iota((width, width), 1)
    tri[...] = jnp.where(earlier, 1.0, 0.0).astype(BF16)
    owners = iota((128, width), 0).astype(F32).astype(BF16)
    before_accs, whole_accs = accs[0::2], accs[1::2]

    pltpu.matmul_push_rhs(tri[...], 0, 0)
    pltpu.matmul_acc_lhs(before_accs[0], jnp.zeros((128, width), BF16), load_staged_rhs=0)
    pltpu.matmul_push_rhs(jnp.ones((width, width), BF16), 0, 1)
    pltpu.matmul_acc_lhs(whole_accs[0], jnp.zeros((128, width), BF16), load_staged_rhs=0)
    start = pltpu.matmul_pop(before_accs[0]) + pltpu.matmul_pop(whole_accs[0])

    def several(step, held):
        spans = [
            pl.ds(pl.multiple_of((step * RANK_UNROLL + u) * width, width), width)
            for u in range(RANK_UNROLL)
        ]
        hits = []
        for u, span in enumerate(spans):
            own = own_ref[0:1, span]
            hits.append(one_hot(owners, own.astype(F32).astype(BF16)))
            pltpu.matmul_acc_lhs(before_accs[u], hits[u])
            pltpu.matmul_acc_lhs(whole_accs[u], hits[u])
        for u, span in enumerate(spans):
            own = own_ref[0:1, span]
            px = point_ref[0:1, span]
            py = point_ref[1:2, span]
            rows_ref[2:3, span] = ((own >> 6) * 16 + (own & 15)).astype(F32)
            box = nibble_reversed(px >> 4) * 16 + nibble_reversed(py >> 4)
            rows_ref[3:4, span] = box.astype(F32)
            rows_ref[4:5, span] = ((px & 15) * 16 + (py & 15)).astype(F32)
            big_x = (own >> 4) * (LB * LAT) + px
            big_y = (own & 15) * (LB * LAT) + py
            cosine, sine = unit_phase(big_x.astype(F32) * big_y.astype(F32))
            real = value_ref[0:16, span].astype(F32)
            imag = value_ref[16:32, span].astype(F32)
            turned_real = cosine * real - sine * imag
            turned_imag = sine * real + cosine * imag
            parts = []
            for group in range(4):
                parts.append(turned_real[4 * group : 4 * group + 4])
                parts.append(turned_imag[4 * group : 4 * group + 4])
            charge_ref[:, span] = jnp.concatenate(parts, axis=0).astype(BF16)
        for u, span in enumerate(spans):
            before = pltpu.matmul_pop(before_accs[u]) + held
            held = held + pltpu.matmul_pop(whole_accs[u])
            rank = jnp.sum(hits[u].astype(F32) * before, axis=0, keepdims=True)
            sibling = own_ref[0:1, span] >> 4 & 3
            key = rank + (128 * (sibling & 1)).astype(F32)
            rows_ref[0:1, span] = jnp.where(sibling < 2, key, -1.0)
            rows_ref[1:2, span] = jnp.where(sibling < 2, -1.0, key)
        return held

    lax.fori_loop(0, own_ref.shape[1] // width // RANK_UNROLL, several, start)


def place_charges(rows_ref, charge_ref, hold, accs):
    blocks = charge_ref.shape[1] // BLOCK
    cells = iota((256, BLOCK), 0).astype(F32).astype(BF16)
    none = jnp.zeros((), BF16)

    def one(step, carried):
        for u in range(ROUTE_UNROLL):
            span = pl.ds(pl.multiple_of((step * ROUTE_UNROLL + u) * BLOCK, BLOCK), BLOCK)
            low = jnp.broadcast_to(rows_ref[2:3, span].astype(BF16), (32, BLOCK))
            charge = charge_ref[:, span]
            slots = [one_hot(cells, rows_ref[side : side + 1, span].astype(BF16)) for side in range(2)]
            for m in range(2):
                parts = [jnp.where(low == float(m * 16 + n), charge, none) for n in range(16)]
                parts = jnp.concatenate(parts, axis=0)
                for side in range(2):
                    pltpu.matmul_push_rhs(slots[side], side, m, transpose=True)
                    pltpu.matmul_acc_lhs(accs[2 * side + m], parts, load_staged_rhs=side)
        return carried

    lax.fori_loop(0, blocks // ROUTE_UNROLL, one, 0)
    for side in range(2):
        for m in range(2):
            hold[side, m, 0:512] = pltpu.matmul_pop(accs[2 * side + m])


def place_points(rows_ref, hold, accs):
    blocks = rows_ref.shape[1] // BLOCK
    cells = iota((256, BLOCK), 0).astype(F32).astype(BF16)
    lows = iota((32, BLOCK), 0).astype(F32).astype(BF16)
    none = jnp.zeros((), BF16)

    def one(step, carried):
        for u in range(POINT_UNROLL):
            span = pl.ds(pl.multiple_of((step * POINT_UNROLL + u) * BLOCK, BLOCK), BLOCK)
            mine = lows == rows_ref[2:3, span].astype(BF16)
            places = [
                jnp.where(mine, rows_ref[3 + kind : 4 + kind, span].astype(BF16), none)
                for kind in range(2)
            ]
            places = jnp.concatenate(places, axis=0)
            for side in range(2):
                slots = one_hot(cells, rows_ref[side : side + 1, span].astype(BF16))
                pltpu.matmul_push_rhs(slots, u % 2, side, transpose=True)
                pltpu.matmul_acc_lhs(accs[side], places, load_staged_rhs=u % 2)
        return carried

    lax.fori_loop(0, blocks // POINT_UNROLL, one, 0)
    for side in range(2):
        hold[side, 0, 512:576] = pltpu.matmul_pop(accs[side])


def route_kernel(own_ref, point_ref, value_ref, send_ref, rows_ref, charge_ref, tri, hold):
    pl.run_scoped(
        lambda *accs: rank_sources(own_ref, point_ref, value_ref, rows_ref, charge_ref, tri, accs),
        *[pltpu.ACC(number % 2)((128, 256), F32) for number in range(2 * RANK_UNROLL)],
    )
    pl.run_scoped(
        lambda *accs: place_points(rows_ref, hold, accs),
        *[pltpu.ACC(number % 2)((64, 256), F32) for number in range(2)],
    )
    pl.run_scoped(
        lambda *accs: place_charges(rows_ref, charge_ref, hold, accs),
        *[pltpu.ACC(number % 2)((512, 256), F32) for number in range(4)],
    )
    for number in range(32):
        first = number // 16 * 64 + number % 16
        row = number % 16 * 32
        for group in range(4):
            for y in range(4):
                tile = hold[
                    y // 2,
                    number // 16,
                    row + group * 8 : row + group * 8 + 8,
                    y % 2 * 128 : y % 2 * 128 + 128,
                ]
                send_ref[first + group * 16, y] = tile.astype(BF16)
        tile = [
            hold[y // 2, 0, pl.ds(512 + 32 * kind + number, 1), y % 2 * 128 : y % 2 * 128 + 128]
            for kind in range(2)
            for y in range(4)
        ]
        tile = jnp.concatenate(tile, axis=0).astype(BF16)
        for group in range(4):
            send_ref[first + group * 16, 4] = tile


def route(owner, point, value):
    sources = owner.shape[1]
    vmem = pl.BlockSpec(memory_space=pltpu.VMEM)
    return pl.pallas_call(
        route_kernel,
        in_specs=[vmem] * 3,
        out_specs=vmem,
        out_shape=jax.ShapeDtypeStruct((128, 5, 8, 128), BF16),
        scratch_shapes=[
            pltpu.VMEM((8, sources), F32),
            pltpu.VMEM((32, sources), BF16),
            pltpu.VMEM((BLOCK, BLOCK), BF16),
            pltpu.VMEM((2, 2, 576, 256), F32),
        ],
        compiler_params=pltpu.CompilerParams(vmem_limit_bytes=40 * MIB),
        cost_estimate=cost(15),
        name="route",
    )(owner, point, value)


def nodes_and_scales():
    nodes = [0.5 + 0.5 * math.cos(math.pi * (2 * a + 1) / (2 * QX)) for a in range(QX)]
    scales = []
    for a in range(QX):
        scale = 1.0
        for c in range(QX):
            if c != a:
                scale /= nodes[a] - nodes[c]
        scales.append(scale)
    return nodes, scales


def column(values, shape):
    row = iota(shape, 0)
    out = jnp.full(shape, values[0], F32)
    for index in range(1, len(values)):
        out = jnp.where(row == index, values[index], out)
    return out


def interpolation(position, nodes, scales):
    gap = position - nodes
    one = pltpu.roll(gap, 7, axis=0)
    two = one * pltpu.roll(one, 7, axis=0)
    four = two * pltpu.roll(two, 6, axis=0)
    return scales * four * pltpu.roll(two, 4, axis=0) * pltpu.roll(one, 2, axis=0)


def turn(values, cosine, sine):
    return values * cosine + pltpu.roll(values, 64, axis=values.ndim - 1) * sine


def signs(shape):
    return jnp.where(iota(shape, len(shape) - 1) < 64, -1.0, 1.0)


def level_matrix(mats_ref, level):
    return jnp.concatenate(
        [
            jnp.concatenate([mats_ref[level, t, 0], mats_ref[level, t, 1]], axis=1)
            for t in range(2)
        ],
        axis=0,
    )


def leaves_kernel(got_ref, out_ref, points):
    points[...] = got_ref[:, 4].astype(F32)
    nodes, scales = nodes_and_scales()
    nodes = column(nodes, (8, 128))
    scales = column(scales, (8, 128))
    cells = iota((256, 128), 0).astype(F32).astype(BF16)

    def operands(source, y):
        charge = got_ref[source, y].astype(F32)
        box = points[source, y : y + 1, :]
        offset = points[source, 4 + y : 5 + y, :]
        coarse = jnp.floor(offset * (1.0 / LAT))
        fine = offset - LAT * coarse
        over_x = interpolation((coarse + 0.5) * (1.0 / LAT), nodes, scales)
        over_y = interpolation((fine + 0.5) * (1.0 / LAT), nodes, scales)
        both = jnp.concatenate([over_x[a : a + 1] * over_y for a in range(QX)], axis=0)
        both = both.astype(BF16)
        rows = []
        for h in range(4):
            for part in range(2):
                at = part * 4 + h
                rows.append(both * charge[at : at + 1].astype(BF16))
        return one_hot(cells, box.astype(BF16)), jnp.concatenate(rows, axis=0)

    def run(*accs):
        for y in range(4):

            def one(step, carried):
                for u in range(LEAF_UNROLL):
                    for m in range(2):
                        source = (step * LEAF_UNROLL + u) * 4 + m * 2
                        boxes0, spread0 = operands(source, y)
                        boxes1, spread1 = operands(source + 1, y)
                        boxes = jnp.concatenate([boxes0, boxes1], axis=1)
                        spread = jnp.concatenate([spread0, spread1], axis=1)
                        pltpu.matmul_push_rhs(boxes, u % 2, m, transpose=True)
                        pltpu.matmul_acc_lhs(accs[m], spread, load_staged_rhs=u % 2)
                return carried

            lax.fori_loop(0, 32 // LEAF_UNROLL, one, 0)
            total = pltpu.matmul_pop(accs[0]) + pltpu.matmul_pop(accs[1])
            for h in range(4):
                out_ref[h // 2, y, h % 2] = total[h * 128 : (h + 1) * 128].T.astype(BF16)

    pl.run_scoped(run, pltpu.ACC(0)((512, 256), F32), pltpu.ACC(1)((512, 256), F32))


def leaves(got):
    vmem = pl.BlockSpec(memory_space=pltpu.VMEM)
    return pl.pallas_call(
        leaves_kernel,
        in_specs=[vmem],
        out_specs=vmem,
        out_shape=jax.ShapeDtypeStruct((2, 4, HALF, 256, 128), BF16),
        scratch_shapes=[pltpu.VMEM((128, 8, 128), F32)],
        compiler_params=pltpu.CompilerParams(vmem_limit_bytes=40 * MIB),
        cost_estimate=cost(19),
        name="leaves",
    )(got)


def inner_kernel(where_ref, leaf_ref, mats_ref, after_ref, out_ref, work):
    del after_ref
    for y in range(4):
        for h in range(HALF):
            work[pl.ds(y * HALF + h, 256, stride=8), :] = leaf_ref[0, y, h].astype(F32)
    pl.run_scoped(
        lambda *accs: inner_levels(where_ref, mats_ref, out_ref, work, accs),
        *[pltpu.ACC(number % 2)((256, 256), F32) for number in range(4)],
    )


def four_products(accs, lefts, right):
    for number, left in enumerate(lefts):
        pltpu.matmul_push_rhs(right, number // 2, number % 2, transpose=True)
        pltpu.matmul_acc_lhs(accs[number], left, load_staged_rhs=number // 2)


def inner_levels(where_ref, mats_ref, out_ref, work, accs):
    row_high = where_ref[0].astype(F32)
    row_y = where_ref[1].astype(F32)
    sign8 = signs((8, 128))
    row_x = row_high * 4.0 + (iota((8, 128), 0) // HALF).astype(F32)

    def box_rows(x, y):
        return pl.ds((x * 16 + y) * 8, 8)

    def line(axis, at):
        if axis == 0:
            return work[pl.ds(at * 128, 128), :].astype(BF16)
        return jnp.concatenate([work[box_rows(x, at), :] for x in range(16)], axis=0).astype(BF16)

    for depth in range(LEVX):
        below = LEVX - 1 - depth
        count = 2**below
        starts = [(high, low) for high in range(2**depth) for low in range(count)]
        for axis in range(2):
            lefts = []
            for number in range(4):
                first = [high << below + 1 | low for high, low in starts[2 * number : 2 * number + 2]]
                lefts.append(
                    jnp.concatenate(
                        [
                            jnp.concatenate([line(axis, s) for s in first], axis=0),
                            jnp.concatenate([line(axis, s | 1 << below) for s in first], axis=0),
                        ],
                        axis=1,
                    )
                )
            four_products(accs, lefts, level_matrix(mats_ref, 2 * depth + axis))
            for number in range(4):
                made = pltpu.matmul_pop(accs[number])
                for place in range(2):
                    high, low = starts[2 * number + place]
                    parent = float(reversed_bits(low, below))
                    for t in range(2):
                        target = float(2 * high + t)
                        if axis == 0:
                            angle = (row_x * float(count) + parent) * target
                        else:
                            angle = jnp.full((8, 128), (row_y * float(count) + parent) * target)
                        cosine, sine = unit_phase(angle)
                        piece = made[place * 128 : (place + 1) * 128, t * 128 : (t + 1) * 128]
                        piece = turn(piece.reshape(16, 8, 128), cosine[None], (sine * sign8)[None])
                        end = high << below + 1 | low | t << below
                        if axis == 0:
                            work[pl.ds(end * 128, 128), :] = piece.reshape(128, 128)
                        else:
                            for x in range(16):
                                work[box_rows(x, end), :] = piece[x]

    key = iota((16, 8, 128), 0).astype(F32)
    sign = signs((16, 8, 128))
    lefts = []
    for pair in range(2):
        for h in range(HALF):
            both = [
                work[pl.ds((2 * pair + c) * HALF + h, 256, stride=8), :].astype(BF16)
                for c in range(2)
            ]
            lefts.append(jnp.concatenate(both, axis=1))
    four_products(accs, lefts, level_matrix(mats_ref, 2 * LEVX))
    for pair in range(2):
        tables = []
        for t in range(2):
            cosine, sine = unit_phase((row_high * 2.0 + float(pair)) * (2.0 * key + float(t)))
            tables.append((cosine[:, None], (sine * sign)[:, None]))
        for h in range(HALF):
            made = pltpu.matmul_pop(accs[pair * HALF + h])
            for t in range(2):
                piece = made[:, t * 128 : (t + 1) * 128].reshape(16, 2, 8, 128)
                piece = turn(piece, *tables[t]).reshape(256, 128)
                out_ref[pair, t, h] = piece.astype(BF16)


def inner(half, where, leaf, mats, after):
    vmem = pl.BlockSpec(memory_space=pltpu.VMEM)
    chosen = pl.BlockSpec((1, 4, HALF, 256, 128), lambda i: (half, 0, 0, 0, 0))
    return pl.pallas_call(
        inner_kernel,
        grid=(1,),
        in_specs=[
            pl.BlockSpec(memory_space=pltpu.SMEM),
            chosen,
            vmem,
            pl.BlockSpec(memory_space=pl.ANY),
        ],
        out_specs=vmem,
        out_shape=jax.ShapeDtypeStruct((2, 2, HALF, 256, 128), BF16),
        scratch_shapes=[pltpu.VMEM((2048, 128), F32)],
        compiler_params=pltpu.CompilerParams(vmem_limit_bytes=40 * MIB),
        cost_estimate=cost(4),
        name="inner",
    )(where, leaf, mats, after)


def outer_kernel(where_ref, mine_ref, other_ref, mats_ref, *refs):
    outs, held = refs[:4], refs[4]
    row_high = where_ref[0].astype(F32)
    row_y = where_ref[1]
    own = where_ref[2]
    core = row_y & 1
    target = 2.0 * iota((16, 128), 0).astype(F32) + core.astype(F32)
    cosine, sine = unit_phase((row_y >> 1).astype(F32) * target)
    table = (cosine[None], (sine * signs((16, 128)))[None])
    mats_y = jnp.concatenate([mats_ref[0, core, core], mats_ref[0, core, 1 - core]], axis=1)
    mats_x = level_matrix(mats_ref, 1)
    key = iota((16, 8, 128), 0).astype(F32)
    sign = signs((16, 8, 128))
    for t8 in range(2):
        tables = []
        for t in range(2):
            cosine, sine = unit_phase(row_high * (2.0 * (2.0 * key + float(t8)) + float(t)))
            tables.append((cosine[:, None], (sine * sign)[:, None]))
        for h in range(HALF):
            both = []
            for c in range(2):
                pair = jnp.concatenate([mine_ref[c, t8, h], other_ref[c, t8, h]], axis=1)
                made = matmul_nt(pair, mats_y).reshape(16, 16, 128)
                both.append(turn(made, *table).reshape(256, 128).astype(BF16))
            made = matmul_nt(jnp.concatenate(both, axis=1), mats_x)
            for t in range(2):
                piece = made[:, t * 128 : (t + 1) * 128].reshape(16, 2, 8, 128)
                piece = turn(piece, *tables[t]).reshape(256, 128)
                held[2 * t + t8, h] = piece.astype(BF16)
    for shift in range(4):
        outs[shift][...] = held[(own + shift) & 3]


def outer(where, mine, other, mats):
    vmem = pl.BlockSpec(memory_space=pltpu.VMEM)
    return pl.pallas_call(
        outer_kernel,
        in_specs=[pl.BlockSpec(memory_space=pltpu.SMEM), vmem, vmem, vmem],
        out_specs=[vmem] * 4,
        out_shape=[jax.ShapeDtypeStruct((HALF, 256, 128), BF16)] * 4,
        scratch_shapes=[pltpu.VMEM((4, HALF, 256, 128), BF16)],
        compiler_params=pltpu.CompilerParams(vmem_limit_bytes=40 * MIB),
        cost_estimate=cost(3),
        name="outer",
    )(where, mine, other, mats)


def finish_kernel(where_ref, *refs):
    got, out_ref, taken, held = refs[:8], refs[8], refs[9], refs[10]
    own = where_ref[2]
    for half in range(2):
        for shift in range(4):
            taken[half, shift] = got[half * 4 + shift][...]
    for half in range(2):
        for group in range(4):
            for h in range(HALF):
                row = group * 4 + half * HALF + h
                piece = taken[half, (own - group) & 3, h]
                held[pl.ds(row, 256, stride=16), :] = piece.astype(F32)
    for block in range(32):
        span = slice(block * 128, (block + 1) * 128)
        out_ref[:, span] = held[span].T.astype(BF16)


def finish(where, got):
    vmem = pl.BlockSpec(memory_space=pltpu.VMEM)
    return pl.pallas_call(
        finish_kernel,
        in_specs=[pl.BlockSpec(memory_space=pltpu.SMEM)] + [vmem] * 8,
        out_specs=vmem,
        out_shape=jax.ShapeDtypeStruct((128, 4096), BF16),
        scratch_shapes=[
            pltpu.VMEM((2, 4, HALF, 256, 128), BF16),
            pltpu.VMEM((4096, 128), F32),
        ],
        compiler_params=pltpu.CompilerParams(vmem_limit_bytes=40 * MIB),
        cost_estimate=cost(3),
        name="finish",
    )(where, *got)


def block_matrices(translation):
    parts = translation.reshape(-1, 2, 2, 2, R, R)
    real = parts[:, :, :, 0]
    imag = parts[:, :, :, 1]
    top = jnp.concatenate([real, -imag], axis=-1)
    bottom = jnp.concatenate([imag, real], axis=-1)
    return jnp.concatenate([top, bottom], axis=-2)


def body(src_value, src_point, src_owner, translation):
    row_x = lax.axis_index("gx")
    row_y = lax.axis_index("gy")
    where = jnp.stack([row_x >> 2, row_y, row_x & 3]).astype(jnp.int32)

    send = route(src_owner.reshape(1, -1), src_point, src_value)
    got = lax.all_to_all(send, ("gx", "gy"), split_axis=0, concat_axis=0, tiled=True)
    mats = block_matrices(translation)
    inner_mats = mats[: 2 * LEVX + 1]
    outer_mats = mats[2 * LEVX + 1 :]
    leaf = leaves(got)
    cores = [(i, i ^ 1) for i in range(lax.axis_size("gy"))]
    after = where
    got = []
    for half in range(2):
        mine = inner(half, where, leaf, inner_mats, after)
        after = mine
        other = lax.ppermute(mine, "gy", cores)
        outs = outer(where, mine, other, outer_mats)
        got.append(outs[0])
        for shift in range(1, 4):
            pairs = [(i, i // 4 * 4 + (i + shift) % 4) for i in range(lax.axis_size("gx"))]
            got.append(lax.ppermute(outs[shift], "gx", pairs))
    return finish(where, got).reshape(128, 1, 1, 4096)


def solution(mesh):
    return jax.shard_map(
        body,
        mesh=mesh,
        in_specs=(P(None, ("gx", "gy")), P(None, ("gx", "gy")), P(("gx", "gy"), None), P()),
        out_specs=P(None, "gx", "gy", None),
        check_vma=False,
    )
```

time: 123 us -> 103 us (0.84)
  waiting for transfers between devices: 6.39 us -> 26.4 us
  blocking collectives: 17.3 us -> 0 us
  Pallas kernels: 65.9 us -> 51.1 us
  local copies, waits for them, and re-layouts: 18.5 us -> 4.92 us
  starting transfers between devices: 12.7 us -> 18.6 us
    all_to_all x1 -> x0, blocking collectives: 17.3 us -> none  [body(): lax.all_to_all(out, 'gx', split_axis=0, concat_axis=0, axis_index_groups=...]
    pallas_call x3 -> x5, Pallas kernels: 62.3 us -> 47.2 us  [the longest x1 18.9 us: leaves(): pl.pallas_call(leaves_kernel, in_specs=[vmem], out_specs=vmem, out_shape=...]
    all_to_all x1, waiting for transfers between devices: 6.02 us -> 18 us  [body(): lax.all_to_all(send, ('gx', 'gy'), split_axis=0, concat_axis=0, tiled=True)]
    ppermute x1 -> x8, waiting for transfers between devices: 0.38 us -> 8.42 us  [the longest x6 7.14 us: body(): got.append(lax.ppermute(outs[shift], 'gx', pairs))]
    ppermute x1 -> x8, starting transfers between devices: 1.22 us -> 7.06 us  [the longest x6 5.71 us: body(): got.append(lax.ppermute(outs[shift], 'gx', pairs))]
    reshape x1 -> x0, local copies, waits for them, and re-layouts: 5.67 us -> none  [block_matrices(): return whole.reshape(-1, 4 * R, 4 * R)]
    transpose x1 -> x0, local copies, waits for them, and re-layouts: 4.58 us -> none  [block_matrices(): whole = jnp.transpose(whole, (0, 1, 2, 4, 3, 5, 6))]
    slice x4 -> x1, local copies, waits for them, and re-layouts: 1.63 us -> 0.08 us  [body(): inner_mats = mats[:2 * LEVX + 1]]
  transfers between devices with their start and end apart: 2 -> 9, of which waited for: 2 -> 5; matrix products, arithmetic and copies ran while one was open for 13% -> 3% of each run, Pallas kernels for 0% -> 4%
where the time goes in v2:
time: 103 us; the launch traced here: 102 us
  Pallas kernels  51.1 us (50%)
  waiting for transfers between devices  26.4 us (26%)
  starting transfers between devices  18.6 us (18%)
  local copies, waits for them, and re-layouts  4.92 us (5%)
  other arithmetic  1.15 us (1%)
    pallas_call x1, Pallas kernels, leaves(): pl.pallas_call(leaves_kernel, in_specs=[vmem], out_specs=vmem, out_shape=...  18.9 us
    all_to_all x1, waiting for transfers between devices, body(): lax.all_to_all(send, ('gx', 'gy'), split_axis=0, concat_axis=0, tiled=True)  18 us
    pallas_call x1, Pallas kernels, route(): pl.pallas_call(route_kernel, in_specs=[vmem] * 3, out_specs=vmem, out_sha...  15.9 us
    all_to_all x1, starting transfers between devices, body(): lax.all_to_all(send, ('gx', 'gy'), split_axis=0, concat_axis=0, tiled=True)  11.5 us
    pallas_call x2, Pallas kernels, inner(): pl.pallas_call(inner_kernel, grid=(1,), in_specs=[pl.BlockSpec(memory_spa...  9.73 us
    ppermute x6, waiting for transfers between devices, body(): got.append(lax.ppermute(outs[shift], 'gx', pairs))  7.14 us
    ppermute x6, starting transfers between devices, body(): got.append(lax.ppermute(outs[shift], 'gx', pairs))  5.71 us
    pallas_call x2, Pallas kernels, outer(): pl.pallas_call(outer_kernel, in_specs=[pl.BlockSpec(memory_space=pltpu.SM...  3.9 us
  transfers between devices with their start and end apart: 9, of which 5 were waited for; matrix products, arithmetic and copies ran while one was open for 3% of the time, Pallas kernels for 4%

profile of v2, /device:TPU:1, one launch (start us, length us, event | category | flops | bytes accessed | tf_op | source)
XLA Modules:
  0.0 102.3 jit_solution(5946273581223062729)
XLA Ops:
  0.0 1.0 %copy-done = bf16[32,8192]{1,0:T(8,128)(2,1)S(1)} copy-done((bf16[32,8192]{1,0:T(8,128)(2,1)S(1)}, bf16[32,8192]{1,0:T(8,128)(2,1)}, u32[]{:S(2)}) %copy-start) | copy-done | bytes 524312
  1.0 0.8 copy-done.1
  1.9 0.8 copy-done.2
  2.6 15.9 %route.1 = bf16[128,5,8,128]{3,2,1,0:T(8,128)(2,1)} custom-call(s32[1,8192]{1,0:T(1,128)S(1)} %bitcast.13, s32[2,8192]{1,0:T(2,128)S(1)} %copy-done.1, bf16[32,8192]{1,0:T(8,128)(2,1)S(1)} %copy-done), custom_call_target="tpu_custom_call" | custom-call | flops 15000000512 | tf_op jit(solution)/shard_map/route/pallas_call | solution.py:213
  18.6 11.5 %all-to-all-start = ((bf16[128,5,8,128]{3,2,1,0:T(8,128)(2,1)}), bf16[128,5,8,128]{3,2,1,0:T(8,128)(2,1)S(1)}, u32[]{:S(2)}, u32[]{:S(2)}) async-start(bf16[128,5,8,128]{3,2,1,0:T(8,128)(2,1)} %route.1), calls=%async_computation | async-start | bytes 2621440 | tf_op jit(solution)/shard_map/all_to_all | solution.py:548
  30.1 0.9 copy.5
  31.0 0.9 reshape.10
  31.9 0.1 fusion
  32.0 0.1 slice_bitcast_fusion
  32.2 0.8 maximum_maximum_fusion
  33.1 0.2 copy-done.5
  33.3 0.1 slice.18.mats_ref
  33.4 0.1 pad_add_fusion.where_ref.after_ref
  33.4 18.0 %all-to-all-done.got_ref = bf16[128,5,8,128]{3,2,1,0:T(8,128)(2,1)S(1)} async-done(((bf16[128,5,8,128]{3,2,1,0:T(8,128)(2,1)}), bf16[128,5,8,128]{3,2,1,0:T(8,128)(2,1)S(1)}, u32[]{:S(2)}, u32[]{:S(2)}) %all-to-all-start) | async-done | bytes 1310752 | tf_op jit(solution)/shard_map/all_to_all | solution.py:548
  51.4 18.9 %leaves.1.leaf_ref = bf16[2,4,2,256,128]{4,3,2,1,0:T(8,128)(2,1)S(1)} custom-call(bf16[128,5,8,128]{3,2,1,0:T(8,128)(2,1)S(1)} %all-to-all-done.got_ref), custom_call_target="tpu_custom_call" | custom-call | flops 19000000512 | tf_op jit(solution)/shard_map/leaves/pallas_call | solution.py:325
  70.4 4.9 %inner.2.mine_ref.after_ref = bf16[2,2,2,256,128]{4,3,2,1,0:T(8,128)(2,1)S(1)} custom-call(s32[3]{0:T(128)S(1)} %pad_add_fusion.where_ref.after_ref, bf16[2,4,2,256,128]{4,3,2,1,0:T(8,128)(2,1)S(1)} %leaves.1.leaf_ref, bf16[9,2,2,128,128]{4,3,2,1,0:T(8,128)(2,1)S(1)} %slice.18.mats_ref, s32[3]{0:T(128)S(1)} %pad_add_fusion.where_ref.after_ref), custom_call_target="tpu_custom_call" | custom-call | flops 4000000000 | tf_op jit(solution)/shard_map/inner/pallas_call | solution.py:434
  75.3 4.9 %inner.3.mine_ref = bf16[2,2,2,256,128]{4,3,2,1,0:T(8,128)(2,1)S(1)} custom-call(s32[3]{0:T(128)S(1)} %pad_add_fusion.where_ref.after_ref, bf16[2,4,2,256,128]{4,3,2,1,0:T(8,128)(2,1)S(1)} %leaves.1.leaf_ref, bf16[9,2,2,128,128]{4,3,2,1,0:T(8,128)(2,1)S(1)} %slice.18.mats_ref, bf16[2,2,2,256,128]{4,3,2,1,0:T(8,128)(2,1)S(1)} %inner.2.mine_ref.after_ref), custom_call_target="tpu_custom_call" | custom-call | flops 4000000000 | tf_op jit(solution)/shard_map/inner/pallas_call | solution.py:434
  80.1 1.3 %collective-permute-start.4 = (bf16[2,2,2,256,128]{4,3,2,1,0:T(8,128)(2,1)S(1)}, bf16[2,2,2,256,128]{4,3,2,1,0:T(8,128)(2,1)S(1)}, u32[]{:S(2)}, u32[]{:S(2)}) collective-permute-start(bf16[2,2,2,256,128]{4,3,2,1,0:T(8,128)(2,1)S(1)} %inner.3.mine_ref), channel_id=1, source_target_pairs={{0,1},{1,0},{2,3},{3,2},{4,5},{5,4},{6,7},{7,6},{8,9},{9,8},{10,11... | collective-permute-start | bytes 1572872 | tf_op jit(solution)/shard_map/ppermute | solution.py:559
  81.4 0.1 collective-permute-start
  81.5 0.2 maximum_maximum_fusion.1.mats_ref
  81.6 1.3 %collective-permute-done.4.other_ref = bf16[2,2,2,256,128]{4,3,2,1,0:T(8,128)(2,1)S(1)} collective-permute-done((bf16[2,2,2,256,128]{4,3,2,1,0:T(8,128)(2,1)S(1)}, bf16[2,2,2,256,128]{4,3,2,1,0:T(8,128)(2,1)S(1)}, u32[]{:S(2)}, u32[]{:S(2)}) %collective-permute-start.4) | collective-permute-done | bytes 524320 | tf_op jit(solution)/shard_map/ppermute | solution.py:559
  82.9 2.0 %outer.3 = (bf16[2,256,128]{2,1,0:T(8,128)(2,1)S(1)}, bf16[2,256,128]{2,1,0:T(8,128)(2,1)S(1)}, bf16[2,256,128]{2,1,0:T(8,128)(2,1)S(1)}, bf16[2,256,128]{2,1,0:T(8,128)(2,1)S(1)}) custom-call(s32[3]{0:T(128)S(1)} %pad_add_fusion.where_ref.after_ref, bf16[2,2,2,256,128]{4,3,2,1,0:T(8,128)(2,1)S(1)} %inner.3.mine_ref, ...), custom_call_target="tpu_custom_call" | custom-call | flops 3000000000 | tf_op jit(solution)/shard_map/outer/pallas_call | solution.py:487
  85.0 1.6 %collective-permute-start.6 = (bf16[2,256,128]{2,1,0:T(8,128)(2,1)S(1)}, bf16[2,256,128]{2,1,0:T(8,128)(2,1)S(1)}, u32[]{:S(2)}, u32[]{:S(2)}) collective-permute-start(bf16[2,256,128]{2,1,0:T(8,128)(2,1)S(1)} %get-tuple-element.19), channel_id=1, source_target_pairs={{0,32},{16,48},{32,0},{48,16},{64,96},{80,112},{96,64},{112,80},{1... | collective-permute-start | bytes 393224 | tf_op jit(solution)/shard_map/ppermute | solution.py:564
  86.6 1.3 %collective-permute-start.7 = (bf16[2,256,128]{2,1,0:T(8,128)(2,1)S(1)}, bf16[2,256,128]{2,1,0:T(8,128)(2,1)S(1)}, u32[]{:S(2)}, u32[]{:S(2)}) collective-permute-start(bf16[2,256,128]{2,1,0:T(8,128)(2,1)S(1)} %get-tuple-element.20), channel_id=1, source_target_pairs={{0,48},{16,0},{32,16},{48,32},{64,112},{80,64},{96,80},{112,96},{1... | collective-permute-start | bytes 393224 | tf_op jit(solution)/shard_map/ppermute | solution.py:564
  87.8 1.9 %outer.2 = (bf16[2,256,128]{2,1,0:T(8,128)(2,1)S(1)}, bf16[2,256,128]{2,1,0:T(8,128)(2,1)S(1)}, bf16[2,256,128]{2,1,0:T(8,128)(2,1)S(1)}, bf16[2,256,128]{2,1,0:T(8,128)(2,1)S(1)}) custom-call(s32[3]{0:T(128)S(1)} %pad_add_fusion.where_ref.after_ref, bf16[2,2,2,256,128]{4,3,2,1,0:T(8,128)(2,1)S(1)} %inner.2.mine_ref.after_ref, ...), custom_call_target="tpu_custom_call" | custom-call | flops 3000000000 | tf_op jit(solution)/shard_map/outer/pallas_call | solution.py:487
  89.8 0.5 collective-permute-start.1
  90.2 1.9 %collective-permute-start.2 = (bf16[2,256,128]{2,1,0:T(8,128)(2,1)S(1)}, bf16[2,256,128]{2,1,0:T(8,128)(2,1)S(1)}, u32[]{:S(2)}, u32[]{:S(2)}) collective-permute-start(bf16[2,256,128]{2,1,0:T(8,128)(2,1)S(1)} %get-tuple-element.15), channel_id=1, source_target_pairs={{0,32},{16,48},{32,0},{48,16},{64,96},{80,112},{96,64},{112,80},{1... | collective-permute-start | bytes 393224 | tf_op jit(solution)/shard_map/ppermute | solution.py:564
  92.1 1.6 %collective-permute-done.5.refs_5_ = bf16[2,256,128]{2,1,0:T(8,128)(2,1)S(1)} collective-permute-done((bf16[2,256,128]{2,1,0:T(8,128)(2,1)S(1)}, bf16[2,256,128]{2,1,0:T(8,128)(2,1)S(1)}, u32[]{:S(2)}, u32[]{:S(2)}) %collective-permute-start.5) | collective-permute-done | bytes 131104 | tf_op jit(solution)/shard_map/ppermute | solution.py:564
  93.7 0.4 collective-permute-start.3
  94.1 5.3 %collective-permute-done.1.refs_1_ = bf16[2,256,128]{2,1,0:T(8,128)(2,1)S(1)} collective-permute-done((bf16[2,256,128]{2,1,0:T(8,128)(2,1)S(1)}, bf16[2,256,128]{2,1,0:T(8,128)(2,1)S(1)}, u32[]{:S(2)}, u32[]{:S(2)}) %collective-permute-start.1) | collective-permute-done | bytes 131104 | tf_op jit(solution)/shard_map/ppermute | solution.py:564
  99.4 0.2 collective-permute-done.3.refs_3_
  99.7 2.6 %finish.1 = bf16[128,4096]{1,0:T(8,128)(2,1)} custom-call(s32[3]{0:T(128)S(1)} %pad_add_fusion.where_ref.after_ref, bf16[2,256,128]{2,1,0:T(8,128)(2,1)S(1)} %get-tuple-element.13.refs_0_, bf16[2,256,128]{2,1,0:T(8,128)(2,1)S(1)} %collective-permute-done.1.refs_1_, bf16[2,256,128]{2,1,0:T(8,128)(2,1)S(1)} %collective-permute-done.2.refs_2_, ...), custom_call_target="tpu_custom_call" | custom-call | flops 3000000000 | tf_op jit(solution)/shard_map/finish/pallas_call | solution.py:518
  (17 shorter events, 0.1 us)
Async XLA Ops:
  0.0 1.0 %copy-start = (bf16[32,8192]{1,0:T(8,128)(2,1)S(1)}, bf16[32,8192]{1,0:T(8,128)(2,1)}, u32[]{:S(2)}) copy-start(bf16[32,8192]{1,0:T(8,128)(2,1)} %value_ref.1) | copy-start | bytes 1572868
  1.0 0.8 copy-start.1
  1.9 0.8 copy-start.2
  18.6 11.5 %copy-start.7 = (bf16[11,2,2,2,4096]{4,3,2,1,0:T(2,128)(2,1)S(1)}, bf16[11,2,2,2,4096]{4,3,2,1,0:T(2,128)(2,1)}, u32[]{:S(2)}) copy-start(bf16[11,2,2,2,4096]{4,3,2,1,0:T(2,128)(2,1)} %param.7) | copy-start | bytes 2162692
  18.6 32.8 %all-to-all-start = ((bf16[128,5,8,128]{3,2,1,0:T(8,128)(2,1)}), bf16[128,5,8,128]{3,2,1,0:T(8,128)(2,1)S(1)}, u32[]{:S(2)}, u32[]{:S(2)}) async-start(bf16[128,5,8,128]{3,2,1,0:T(8,128)(2,1)} %route.1), calls=%async_computation | async-start | bytes 2621440 | tf_op jit(solution)/shard_map/all_to_all | solution.py:548
  32.2 0.9 copy-start.3
  32.2 1.1 %copy-start.5 = (bf16[11,2,2,64,64]{4,3,2,1,0:T(8,128)(2,1)}, bf16[11,2,2,64,64]{4,3,2,1,0:T(8,128)(2,1)S(1)}, u32[]{:S(2)}) copy-start(bf16[11,2,2,64,64]{4,3,2,1,0:T(8,128)(2,1)S(1)} %get-tuple-element.22) | copy-start | bytes 1081348
  75.2 6.2 %copy-start.4 = (bf16[11,2,2,64,64]{4,3,2,1,0:T(8,128)(2,1)S(1)}, bf16[11,2,2,64,64]{4,3,2,1,0:T(8,128)(2,1)}, u32[]{:S(2)}) copy-start(bf16[11,2,2,64,64]{4,3,2,1,0:T(8,128)(2,1)} %copy-done.3) | copy-start | bytes 1081348
  75.2 6.2 %copy-start.6 = (bf16[11,2,2,64,64]{4,3,2,1,0:T(8,128)(2,1)S(1)}, bf16[11,2,2,64,64]{4,3,2,1,0:T(8,128)(2,1)}, u32[]{:S(2)}) copy-start(bf16[11,2,2,64,64]{4,3,2,1,0:T(8,128)(2,1)} %copy-done.5) | copy-start | bytes 1081348
  80.1 2.8 %collective-permute-start.4 = (bf16[2,2,2,256,128]{4,3,2,1,0:T(8,128)(2,1)S(1)}, bf16[2,2,2,256,128]{4,3,2,1,0:T(8,128)(2,1)S(1)}, u32[]{:S(2)}, u32[]{:S(2)}) collective-permute-start(bf16[2,2,2,256,128]{4,3,2,1,0:T(8,128)(2,1)S(1)} %inner.3.mine_ref), channel_id=1, source_target_pairs={{0,1},{1,0},{2,3},{3,2},{4,5},{5,4},{6,7},{7,6},{8,9},{9,8},{10,11... | collective-permute-start | bytes 1572872 | tf_op jit(solution)/shard_map/ppermute | solution.py:559
  81.4 6.4 %collective-permute-start = (bf16[2,2,2,256,128]{4,3,2,1,0:T(8,128)(2,1)S(1)}, bf16[2,2,2,256,128]{4,3,2,1,0:T(8,128)(2,1)S(1)}, u32[]{:S(2)}, u32[]{:S(2)}) collective-permute-start(bf16[2,2,2,256,128]{4,3,2,1,0:T(8,128)(2,1)S(1)} %inner.2.mine_ref.after_ref), channel_id=1, source_target_pairs={{0,1},{1,0},{2,3},{3,2},{4,5},{5,4},{6,7},{7,6},{8,9},{9,8},{10,11... | collective-permute-start | bytes 1572872 | tf_op jit(solution)/shard_map/ppermute | solution.py:559
  84.9 8.8 %collective-permute-start.5 = (bf16[2,256,128]{2,1,0:T(8,128)(2,1)S(1)}, bf16[2,256,128]{2,1,0:T(8,128)(2,1)S(1)}, u32[]{:S(2)}, u32[]{:S(2)}) collective-permute-start(bf16[2,256,128]{2,1,0:T(8,128)(2,1)S(1)} %get-tuple-element.18), channel_id=1, source_target_pairs={{0,16},{16,32},{32,48},{48,0},{64,80},{80,96},{96,112},{112,64},{1... | collective-permute-start | bytes 393224 | tf_op jit(solution)/shard_map/ppermute | solution.py:564
  85.0 9.1 %collective-permute-start.6 = (bf16[2,256,128]{2,1,0:T(8,128)(2,1)S(1)}, bf16[2,256,128]{2,1,0:T(8,128)(2,1)S(1)}, u32[]{:S(2)}, u32[]{:S(2)}) collective-permute-start(bf16[2,256,128]{2,1,0:T(8,128)(2,1)S(1)} %get-tuple-element.19), channel_id=1, source_target_pairs={{0,32},{16,48},{32,0},{48,16},{64,96},{80,112},{96,64},{112,80},{1... | collective-permute-start | bytes 393224 | tf_op jit(solution)/shard_map/ppermute | solution.py:564
  86.6 7.5 %collective-permute-start.7 = (bf16[2,256,128]{2,1,0:T(8,128)(2,1)S(1)}, bf16[2,256,128]{2,1,0:T(8,128)(2,1)S(1)}, u32[]{:S(2)}, u32[]{:S(2)}) collective-permute-start(bf16[2,256,128]{2,1,0:T(8,128)(2,1)S(1)} %get-tuple-element.20), channel_id=1, source_target_pairs={{0,48},{16,0},{32,16},{48,32},{64,112},{80,64},{96,80},{112,96},{1... | collective-permute-start | bytes 393224 | tf_op jit(solution)/shard_map/ppermute | solution.py:564
  89.8 9.7 %collective-permute-start.1 = (bf16[2,256,128]{2,1,0:T(8,128)(2,1)S(1)}, bf16[2,256,128]{2,1,0:T(8,128)(2,1)S(1)}, u32[]{:S(2)}, u32[]{:S(2)}) collective-permute-start(bf16[2,256,128]{2,1,0:T(8,128)(2,1)S(1)} %get-tuple-element.14), channel_id=1, source_target_pairs={{0,16},{16,32},{32,48},{48,0},{64,80},{80,96},{96,112},{112,64},{1... | collective-permute-start | bytes 393224 | tf_op jit(solution)/shard_map/ppermute | solution.py:564
  90.2 9.2 %collective-permute-start.2 = (bf16[2,256,128]{2,1,0:T(8,128)(2,1)S(1)}, bf16[2,256,128]{2,1,0:T(8,128)(2,1)S(1)}, u32[]{:S(2)}, u32[]{:S(2)}) collective-permute-start(bf16[2,256,128]{2,1,0:T(8,128)(2,1)S(1)} %get-tuple-element.15), channel_id=1, source_target_pairs={{0,32},{16,48},{32,0},{48,16},{64,96},{80,112},{96,64},{112,80},{1... | collective-permute-start | bytes 393224 | tf_op jit(solution)/shard_map/ppermute | solution.py:564
  93.7 6.0 %collective-permute-start.3 = (bf16[2,256,128]{2,1,0:T(8,128)(2,1)S(1)}, bf16[2,256,128]{2,1,0:T(8,128)(2,1)S(1)}, u32[]{:S(2)}, u32[]{:S(2)}) collective-permute-start(bf16[2,256,128]{2,1,0:T(8,128)(2,1)S(1)} %get-tuple-element.16), channel_id=1, source_target_pairs={{0,48},{16,0},{32,16},{48,32},{64,112},{80,64},{96,80},{112,96},{1... | collective-permute-start | bytes 393224 | tf_op jit(solution)/shard_map/ppermute | solution.py:564

commit v3 on v2

v3 whole, which is shorter than its diff:
```python
import functools
import math

import jax
import jax.numpy as jnp
from jax import lax
from jax.experimental import pallas as pl
from jax.experimental.pallas import tpu as pltpu
from jax.sharding import PartitionSpec as P

QX = 8
R = 64
LEVX = 4
LB = 16
LAT = 16
CAP = 128

F32 = jnp.float32
BF16 = jnp.bfloat16
MODULUS = 61.0
MIB = 1024 * 1024

BLOCK = 256
HALF = 2
RANK_UNROLL = 8
ROUTE_UNROLL = 8
LEAF_UNROLL = 32


def matmul_nt(lhs, rhs):
    return lax.dot_general(lhs, rhs, (((1,), (1,)), ((), ())), preferred_element_type=F32)


def unit_phase(product):
    rest = product - MODULUS * jnp.floor(product * (1.0 / MODULUS) + 0.5)
    x = rest * (math.pi / MODULUS)
    x2 = x * x
    s = x * (1.0 + x2 * (-1 / 6 + x2 * (1 / 120 + x2 * (-1 / 5040 + x2 * (1 / 362880 + x2 * (-1 / 39916800))))))
    c = 1.0 + x2 * (-1 / 2 + x2 * (1 / 24 + x2 * (-1 / 720 + x2 * (1 / 40320 + x2 * (-1 / 3628800)))))
    return 1.0 - 2.0 * s * s, 2.0 * s * c


def cost(micros):
    return pl.CostEstimate(flops=int(micros * 1.0e9), bytes_accessed=0, transcendentals=0)


def iota(shape, dim):
    return lax.broadcasted_iota(jnp.int32, shape, dim)


def reversed_bits(value, bits):
    out = 0
    for bit in range(bits):
        out |= (value >> bit & 1) << (bits - 1 - bit)
    return out


def nibble_reversed(value):
    return (value & 1) << 3 | (value & 2) << 1 | value >> 1 & 2 | value >> 3 & 1


def one_hot(cells, row):
    return jnp.where(cells == row, jnp.ones((), BF16), jnp.zeros((), BF16))


def rank_sources(own_ref, point_ref, value_ref, rows_ref, charge_ref, tri, accs):
    width = BLOCK
    owners = iota((128, width), 0).astype(F32).astype(BF16)
    before_accs, whole_accs = accs[0::2], accs[1::2]

    pltpu.matmul_push_rhs(tri[...], 0, 0)
    pltpu.matmul_acc_lhs(before_accs[0], jnp.zeros((128, width), BF16), load_staged_rhs=0)
    pltpu.matmul_push_rhs(jnp.ones((width, width), BF16), 0, 1)
    pltpu.matmul_acc_lhs(whole_accs[0], jnp.zeros((128, width), BF16), load_staged_rhs=0)
    start = pltpu.matmul_pop(before_accs[0]) + pltpu.matmul_pop(whole_accs[0])

    def several(step, held):
        spans = [
            pl.ds(pl.multiple_of((step * RANK_UNROLL + u) * width, width), width)
            for u in range(RANK_UNROLL)
        ]
        hits = []
        for u, span in enumerate(spans):
            own = own_ref[0:1, span]
            hits.append(one_hot(owners, own.astype(F32).astype(BF16)))
            pltpu.matmul_acc_lhs(before_accs[u], hits[u])
            pltpu.matmul_acc_lhs(whole_accs[u], hits[u])
        for u, span in enumerate(spans):
            own = own_ref[0:1, span]
            px = point_ref[0:1, span]
            py = point_ref[1:2, span]
            rows_ref[2:3, span] = ((own >> 6) * 16 + (own & 15)).astype(F32)
            box = nibble_reversed(px >> 4) * 16 + nibble_reversed(py >> 4)
            rows_ref[3:4, span] = box.astype(F32)
            rows_ref[4:5, span] = ((px & 15) * 16 + (py & 15)).astype(F32)
            big_x = (own >> 4) * (LB * LAT) + px
            big_y = (own & 15) * (LB * LAT) + py
            cosine, sine = unit_phase(big_x.astype(F32) * big_y.astype(F32))
            real = value_ref[0:16, span].astype(F32)
            imag = value_ref[16:32, span].astype(F32)
            turned_real = cosine * real - sine * imag
            turned_imag = sine * real + cosine * imag
            parts = []
            for group in range(4):
                parts.append(turned_real[4 * group : 4 * group + 4])
                parts.append(turned_imag[4 * group : 4 * group + 4])
            charge_ref[:, span] = jnp.concatenate(parts, axis=0).astype(BF16)
        for u, span in enumerate(spans):
            before = pltpu.matmul_pop(before_accs[u]) + held
            held = held + pltpu.matmul_pop(whole_accs[u])
            rank = jnp.sum(hits[u].astype(F32) * before, axis=0, keepdims=True)
            sibling = own_ref[0:1, span] >> 4 & 3
            key = rank + (128 * (sibling & 1)).astype(F32)
            rows_ref[0:1, span] = jnp.where(sibling < 2, key, -1.0)
            rows_ref[1:2, span] = jnp.where(sibling < 2, -1.0, key)
        return held

    lax.fori_loop(0, own_ref.shape[1] // width // RANK_UNROLL, several, start)


def place_sources(high, rows_ref, charge_ref, hold, accs):
    blocks = charge_ref.shape[1] // BLOCK
    cells = iota((256, BLOCK), 0).astype(F32).astype(BF16)
    lows = (iota((16, BLOCK), 0) + 16 * high).astype(F32).astype(BF16)
    none = jnp.zeros((), BF16)

    def one(step, carried):
        for u in range(ROUTE_UNROLL):
            span = pl.ds(pl.multiple_of((step * ROUTE_UNROLL + u) * BLOCK, BLOCK), BLOCK)
            row = rows_ref[2:3, span].astype(BF16)
            low = jnp.broadcast_to(row, (32, BLOCK))
            charge = charge_ref[:, span]
            parts = [jnp.where(low == float(high * 16 + n), charge, none) for n in range(16)]
            mine = lows == row
            for kind in range(2):
                parts.append(jnp.where(mine, rows_ref[3 + kind : 4 + kind, span].astype(BF16), none))
            parts = jnp.concatenate(parts, axis=0)
            for side in range(2):
                slots = one_hot(cells, rows_ref[side : side + 1, span].astype(BF16))
                pltpu.matmul_push_rhs(slots, u % 2, side, transpose=True)
                pltpu.matmul_acc_lhs(accs[side], parts, load_staged_rhs=u % 2)
        return carried

    lax.fori_loop(0, blocks // ROUTE_UNROLL, one, 0)
    for side in range(2):
        hold[high, side] = pltpu.matmul_pop(accs[side])


def route_kernel(
    own_hbm, point_hbm, value_hbm, send_ref, own, point, value, rows, charge, tri, hold, sems
):
    copies = [
        pltpu.make_async_copy(source, target, sems.at[number])
        for number, (source, target) in enumerate(
            ((own_hbm, own), (point_hbm, point), (value_hbm, value))
        )
    ]
    for copy in copies:
        copy.start()
    earlier = iota((BLOCK, BLOCK), 0) < iota((BLOCK, BLOCK), 1)
    tri[...] = jnp.where(earlier, 1.0, 0.0).astype(BF16)
    for copy in copies:
        copy.wait()
    pl.run_scoped(
        lambda *accs: rank_sources(own, point, value, rows, charge, tri, accs),
        *[pltpu.ACC(number % 2)((128, 256), F32) for number in range(2 * RANK_UNROLL)],
    )
    for high in range(2):
        pl.run_scoped(
            lambda *accs, high=high: place_sources(high, rows, charge, hold, accs),
            *[pltpu.ACC(number)((544, 256), F32) for number in range(2)],
        )
    for number in range(32):
        high, low = number // 16, number % 16
        first = high * 64 + low
        for group in range(4):
            at = low * 32 + group * 8
            for y in range(4):
                tile = hold[high, y // 2, at : at + 8, y % 2 * 128 : y % 2 * 128 + 128]
                send_ref[first + group * 16, y] = tile.astype(BF16)
        tile = [
            hold[high, y // 2, pl.ds(512 + 16 * kind + low, 1), y % 2 * 128 : y % 2 * 128 + 128]
            for kind in range(2)
            for y in range(4)
        ]
        tile = jnp.concatenate(tile, axis=0).astype(BF16)
        for group in range(4):
            send_ref[first + group * 16, 4] = tile


def route(owner, point, value):
    sources = owner.shape[1]
    vmem = pl.BlockSpec(memory_space=pltpu.VMEM)
    return pl.pallas_call(
        route_kernel,
        in_specs=[pl.BlockSpec(memory_space=pltpu.HBM)] * 3,
        out_specs=vmem,
        out_shape=jax.ShapeDtypeStruct((128, 5, 8, 128), BF16),
        scratch_shapes=[
            pltpu.VMEM((1, sources), jnp.int32),
            pltpu.VMEM((2, sources), jnp.int32),
            pltpu.VMEM((32, sources), BF16),
            pltpu.VMEM((8, sources), F32),
            pltpu.VMEM((32, sources), BF16),
            pltpu.VMEM((BLOCK, BLOCK), BF16),
            pltpu.VMEM((2, 2, 544, 256), F32),
            pltpu.SemaphoreType.DMA((3,)),
        ],
        compiler_params=pltpu.CompilerParams(vmem_limit_bytes=40 * MIB),
        cost_estimate=cost(15),
        name="route",
    )(owner, point, value)


def level_starts(depth):
    return [(high, low) for high in range(2**depth) for low in range(2 ** (LEVX - 1 - depth))]


def phases_kernel(
    where_ref, level_c, level_s, eight_c, eight_s, nine_c, nine_s, ten_c, ten_s
):
    row_high = where_ref[0].astype(F32)
    row_y = where_ref[1]
    sign = signs((8, 128))
    row_x = row_high * 4.0 + (iota((8, 128), 0) // HALF).astype(F32)
    flat_y = jnp.full((8, 128), row_y.astype(F32))
    for depth in range(LEVX):
        below = LEVX - 1 - depth
        for axis in range(2):
            row = (row_x, flat_y)[axis]
            for place, (high, low) in enumerate(level_starts(depth)):
                parent = row * float(2**below) + float(reversed_bits(low, below))
                for t in range(2):
                    cosine, sine = unit_phase(parent * float(2 * high + t))
                    level_c[2 * depth + axis, 2 * place + t] = cosine
                    level_s[2 * depth + axis, 2 * place + t] = sine * sign

    key = iota((16, 8, 128), 0).astype(F32)
    sign = signs((16, 8, 128))
    for pair in range(2):
        for t in range(2):
            cosine, sine = unit_phase((row_high * 2.0 + float(pair)) * (2.0 * key + float(t)))
            eight_c[pair, t] = cosine
            eight_s[pair, t] = sine * sign
            cosine, sine = unit_phase(row_high * (2.0 * (2.0 * key + float(pair)) + float(t)))
            ten_c[pair, t] = cosine
            ten_s[pair, t] = sine * sign

    core = (row_y & 1).astype(F32)
    target = 2.0 * iota((16, 128), 0).astype(F32) + core
    cosine, sine = unit_phase((row_y >> 1).astype(F32) * target)
    nine_c[...] = cosine
    nine_s[...] = sine * signs((16, 128))


def phases(where):
    shapes = [(8, 16, 8, 128), (2, 2, 16, 8, 128), (16, 128), (2, 2, 16, 8, 128)]
    return pl.pallas_call(
        phases_kernel,
        in_specs=[pl.BlockSpec(memory_space=pltpu.SMEM)],
        out_specs=[pl.BlockSpec(memory_space=pltpu.VMEM)] * 8,
        out_shape=[jax.ShapeDtypeStruct(shape, F32) for shape in shapes for _ in range(2)],
        compiler_params=pltpu.CompilerParams(vmem_limit_bytes=40 * MIB),
        cost_estimate=cost(2),
        name="phases",
    )(where)


def nodes_and_scales():
    nodes = [0.5 + 0.5 * math.cos(math.pi * (2 * a + 1) / (2 * QX)) for a in range(QX)]
    scales = []
    for a in range(QX):
        scale = 1.0
        for c in range(QX):
            if c != a:
                scale /= nodes[a] - nodes[c]
        scales.append(scale)
    return nodes, scales


def column(values, shape):
    row = iota(shape, 0)
    out = jnp.full(shape, values[0], F32)
    for index in range(1, len(values)):
        out = jnp.where(row == index, values[index], out)
    return out


def interpolation(position, nodes, scales):
    gap = position - nodes
    one = pltpu.roll(gap, 7, axis=0)
    two = one * pltpu.roll(one, 7, axis=0)
    four = two * pltpu.roll(two, 6, axis=0)
    return scales * four * pltpu.roll(two, 4, axis=0) * pltpu.roll(one, 2, axis=0)


def turn(values, cosine, sine):
    return values * cosine + pltpu.roll(values, 64, axis=values.ndim - 1) * sine


def signs(shape):
    return jnp.where(iota(shape, len(shape) - 1) < 64, -1.0, 1.0)


def level_matrix(mats_ref, level):
    return jnp.concatenate(
        [
            jnp.concatenate([mats_ref[level, t, 0], mats_ref[level, t, 1]], axis=1)
            for t in range(2)
        ],
        axis=0,
    )


def leaves_kernel(got_ref, out_ref, points):
    points[...] = got_ref[:, 4].astype(F32)
    nodes, scales = nodes_and_scales()
    nodes = column(nodes, (8, 128))
    scales = column(scales, (8, 128))
    cells = iota((256, 128), 0).astype(F32).astype(BF16)

    def operands(source, y):
        charge = got_ref[source, y].astype(F32)
        box = points[source, y : y + 1, :]
        offset = points[source, 4 + y : 5 + y, :]
        coarse = jnp.floor(offset * (1.0 / LAT))
        fine = offset - LAT * coarse
        over_x = interpolation((coarse + 0.5) * (1.0 / LAT), nodes, scales)
        over_y = interpolation((fine + 0.5) * (1.0 / LAT), nodes, scales)
        both = jnp.concatenate([over_x[a : a + 1] * over_y for a in range(QX)], axis=0)
        both = both.astype(BF16)
        rows = []
        for h in range(4):
            for part in range(2):
                at = part * 4 + h
                rows.append(both * charge[at : at + 1].astype(BF16))
        return one_hot(cells, box.astype(BF16)), jnp.concatenate(rows, axis=0)

    def run(*accs):
        for y in range(4):

            def one(step, carried):
                for u in range(LEAF_UNROLL):
                    for m in range(2):
                        source = (step * LEAF_UNROLL + u) * 4 + m * 2
                        boxes0, spread0 = operands(source, y)
                        boxes1, spread1 = operands(source + 1, y)
                        boxes = jnp.concatenate([boxes0, boxes1], axis=1)
                        spread = jnp.concatenate([spread0, spread1], axis=1)
                        pltpu.matmul_push_rhs(boxes, u % 2, m, transpose=True)
                        pltpu.matmul_acc_lhs(accs[m], spread, load_staged_rhs=u % 2)
                return carried

            lax.fori_loop(0, 32 // LEAF_UNROLL, one, 0)
            total = pltpu.matmul_pop(accs[0]) + pltpu.matmul_pop(accs[1])
            for h in range(4):
                out_ref[h // 2, y, h % 2] = total[h * 128 : (h + 1) * 128].T.astype(BF16)

    pl.run_scoped(run, pltpu.ACC(0)((512, 256), F32), pltpu.ACC(1)((512, 256), F32))


def leaves(got):
    vmem = pl.BlockSpec(memory_space=pltpu.VMEM)
    return pl.pallas_call(
        leaves_kernel,
        in_specs=[vmem],
        out_specs=vmem,
        out_shape=jax.ShapeDtypeStruct((2, 4, HALF, 256, 128), BF16),
        scratch_shapes=[pltpu.VMEM((128, 8, 128), F32)],
        compiler_params=pltpu.CompilerParams(vmem_limit_bytes=40 * MIB),
        cost_estimate=cost(19),
        name="leaves",
    )(got)


def inner_kernel(leaf_ref, mats_ref, level_c, level_s, eight_c, eight_s, out0, out1, work0, work1):
    works = (work0, work1)
    for half in range(2):
        for y in range(4):
            for h in range(HALF):
                piece = leaf_ref[half, y, h].astype(F32)
                works[half][pl.ds(y * HALF + h, 256, stride=8), :] = piece
    pl.run_scoped(
        lambda *accs: inner_levels(
            mats_ref, level_c, level_s, eight_c, eight_s, (out0, out1), works, accs
        ),
        *[pltpu.ACC(number % 2)((256, 256), F32) for number in range(8)],
    )


def four_products(accs, lefts, right, load):
    for number, left in enumerate(lefts):
        if load and number < 2:
            pltpu.matmul_push_rhs(right, 0, number, transpose=True)
            pltpu.matmul_acc_lhs(accs[number], left, load_staged_rhs=0)
        else:
            pltpu.matmul_acc_lhs(accs[number], left)


def box_rows(x, y):
    return pl.ds((x * 16 + y) * 8, 8)


def line(work, axis, at):
    if axis == 0:
        return work[pl.ds(at * 128, 128), :].astype(BF16)
    return jnp.concatenate([work[box_rows(x, at), :] for x in range(16)], axis=0).astype(BF16)


def inner_levels(mats_ref, level_c, level_s, eight_c, eight_s, outs, works, accs):
    for depth in range(LEVX):
        below = LEVX - 1 - depth
        starts = level_starts(depth)
        for axis in range(2):
            level = 2 * depth + axis
            right = level_matrix(mats_ref, level)
            for half, work in enumerate(works):
                lefts = []
                for number in range(4):
                    pair = starts[2 * number : 2 * number + 2]
                    first = [high << below + 1 | low for high, low in pair]
                    ends = [[line(work, axis, s | t << below) for s in first] for t in range(2)]
                    ends = [jnp.concatenate(end, axis=0) for end in ends]
                    lefts.append(jnp.concatenate(ends, axis=1))
                four_products(accs[4 * half : 4 * half + 4], lefts, right, half == 0)
            for half, work in enumerate(works):
                for number in range(4):
                    made = pltpu.matmul_pop(accs[4 * half + number])
                    for place in range(2):
                        high, low = starts[2 * number + place]
                        for t in range(2):
                            cosine = level_c[level, 4 * number + 2 * place + t]
                            sine = level_s[level, 4 * number + 2 * place + t]
                            piece = made[place * 128 : (place + 1) * 128, t * 128 : (t + 1) * 128]
                            piece = turn(piece.reshape(16, 8, 128), cosine[None], sine[None])
                            end = high << below + 1 | low | t << below
                            if axis == 0:
                                work[pl.ds(end * 128, 128), :] = piece.reshape(128, 128)
                            else:
                                for x in range(16):
                                    work[box_rows(x, end), :] = piece[x]

    right = level_matrix(mats_ref, 2 * LEVX)
    for half, work in enumerate(works):
        lefts = []
        for pair in range(2):
            for h in range(HALF):
                both = [
                    work[pl.ds((2 * pair + c) * HALF + h, 256, stride=8), :].astype(BF16)
                    for c in range(2)
                ]
                lefts.append(jnp.concatenate(both, axis=1))
        four_products(accs[4 * half : 4 * half + 4], lefts, right, half == 0)
    for half, out_ref in enumerate(outs):
        for pair in range(2):
            tables = [(eight_c[pair, t][:, None], eight_s[pair, t][:, None]) for t in range(2)]
            for h in range(HALF):
                made = pltpu.matmul_pop(accs[4 * half + pair * HALF + h])
                for t in range(2):
                    piece = made[:, t * 128 : (t + 1) * 128].reshape(16, 2, 8, 128)
                    piece = turn(piece, *tables[t]).reshape(256, 128)
                    out_ref[pair, t, h] = piece.astype(BF16)


def inner(leaf, mats, tables):
    vmem = pl.BlockSpec(memory_space=pltpu.VMEM)
    return pl.pallas_call(
        inner_kernel,
        in_specs=[vmem] * 6,
        out_specs=[vmem] * 2,
        out_shape=[jax.ShapeDtypeStruct((2, 2, HALF, 256, 128), BF16)] * 2,
        scratch_shapes=[pltpu.VMEM((2048, 128), F32)] * 2,
        compiler_params=pltpu.CompilerParams(vmem_limit_bytes=40 * MIB),
        cost_estimate=cost(6),
        name="inner",
    )(leaf, mats, *tables[:4])


def outer_kernel(
    where_ref, mine_ref, other_ref, mats_ref, nine_c, nine_s, ten_c, ten_s, after_ref, *refs
):
    del after_ref
    outs, held = refs[:4], refs[4]
    row_y = where_ref[1]
    own = where_ref[2]
    core = row_y & 1
    table = (nine_c[...][None], nine_s[...][None])
    mats_y = jnp.concatenate([mats_ref[0, core, core], mats_ref[0, core, 1 - core]], axis=1)
    mats_x = level_matrix(mats_ref, 1)
    for t8 in range(2):
        tables = [(ten_c[t8, t][:, None], ten_s[t8, t][:, None]) for t in range(2)]
        for h in range(HALF):
            both = []
            for c in range(2):
                pair = jnp.concatenate([mine_ref[c, t8, h], other_ref[c, t8, h]], axis=1)
                made = matmul_nt(pair, mats_y).reshape(16, 16, 128)
                both.append(turn(made, *table).reshape(256, 128).astype(BF16))
            made = matmul_nt(jnp.concatenate(both, axis=1), mats_x)
            for t in range(2):
                piece = made[:, t * 128 : (t + 1) * 128].reshape(16, 2, 8, 128)
                piece = turn(piece, *tables[t]).reshape(256, 128)
                held[2 * t + t8, h] = piece.astype(BF16)
    for shift in range(4):
        outs[shift][...] = held[(own + shift) & 3]


def outer(where, mine, other, mats, tables, after):
    vmem = pl.BlockSpec(memory_space=pltpu.VMEM)
    return pl.pallas_call(
        outer_kernel,
        in_specs=[pl.BlockSpec(memory_space=pltpu.SMEM)]
        + [vmem] * 7
        + [pl.BlockSpec(memory_space=pl.ANY)],
        out_specs=[vmem] * 4,
        out_shape=[jax.ShapeDtypeStruct((HALF, 256, 128), BF16)] * 4,
        scratch_shapes=[pltpu.VMEM((4, HALF, 256, 128), BF16)],
        compiler_params=pltpu.CompilerParams(vmem_limit_bytes=40 * MIB),
        cost_estimate=cost(3),
        name="outer",
    )(where, mine, other, mats, *tables[4:], after)


def finish_kernel(where_ref, *refs):
    got, out_ref, held = refs[:8], refs[8], refs[9]
    own = where_ref[2]
    for half in range(2):
        for shift in range(4):
            group = (own - shift) & 3
            for h in range(HALF):
                row = group * 4 + (half * HALF + h)
                held[pl.ds(row, 256, stride=16), :] = got[half * 4 + shift][h].astype(F32)
    for block in range(32):
        span = slice(block * 128, (block + 1) * 128)
        out_ref[:, span] = held[span].astype(BF16).T


def finish(where, got):
    vmem = pl.BlockSpec(memory_space=pltpu.VMEM)
    return pl.pallas_call(
        finish_kernel,
        in_specs=[pl.BlockSpec(memory_space=pltpu.SMEM)] + [vmem] * 8,
        out_specs=vmem,
        out_shape=jax.ShapeDtypeStruct((128, 4096), BF16),
        scratch_shapes=[pltpu.VMEM((4096, 128), F32)],
        compiler_params=pltpu.CompilerParams(vmem_limit_bytes=40 * MIB),
        cost_estimate=cost(3),
        name="finish",
    )(where, *got)


def block_matrices(translation):
    parts = translation.reshape(-1, 2, 2, 2, R, R)
    real = parts[:, :, :, 0]
    imag = parts[:, :, :, 1]
    top = jnp.concatenate([real, -imag], axis=-1)
    bottom = jnp.concatenate([imag, real], axis=-1)
    return jnp.concatenate([top, bottom], axis=-2)


def body(src_value, src_point, src_owner, translation):
    row_x = lax.axis_index("gx")
    row_y = lax.axis_index("gy")
    where = jnp.stack([row_x >> 2, row_y, row_x & 3]).astype(jnp.int32)

    send = route(src_owner.reshape(1, -1), src_point, src_value)
    got = lax.all_to_all(send, ("gx", "gy"), split_axis=0, concat_axis=0, tiled=True)
    mats = block_matrices(translation)
    inner_mats = mats[: 2 * LEVX + 1]
    outer_mats = mats[2 * LEVX + 1 :]
    leaf = leaves(got)
    cores = [(i, i ^ 1) for i in range(lax.axis_size("gy"))]
    tables = phases(where)
    last = where
    got = []
    for mine in inner(leaf, inner_mats, tables):
        other = lax.ppermute(mine, "gy", cores)
        outs = outer(where, mine, other, outer_mats, tables, last)
        last = outs[0]
        got.append(outs[0])
        for shift in range(1, 4):
            pairs = [(i, i // 4 * 4 + (i + shift) % 4) for i in range(lax.axis_size("gx"))]
            got.append(lax.ppermute(outs[shift], "gx", pairs))
    return finish(where, got).reshape(128, 1, 1, 4096)


def solution(mesh):
    return jax.shard_map(
        body,
        mesh=mesh,
        in_specs=(P(None, ("gx", "gy")), P(None, ("gx", "gy")), P(("gx", "gy"), None), P()),
        out_specs=P(None, "gx", "gy", None),
        check_vma=False,
    )
```

time: 103 us -> 95.9 us (0.931)
  waiting for transfers between devices: 26.4 us -> 20.3 us
  Pallas kernels: 51.1 us -> 46 us
  local copies, waits for them, and re-layouts: 4.92 us -> 8.99 us
    all_to_all x1, waiting for transfers between devices: 18 us -> 12.2 us  [body(): lax.all_to_all(send, ('gx', 'gy'), split_axis=0, concat_axis=0, tiled=True)]
    unnamed x17 -> x41, local copies, waits for them, and re-layouts: 3.76 us -> 7.65 us
    pallas_call x3, Pallas kernels: 25.7 us -> 21.9 us  [the longest x1 13.8 us: route(): pl.pallas_call(route_kernel, in_specs=[pl.BlockSpec(memory_space=pltpu.HB...]
    pallas_call x1, Pallas kernels: 18.9 us -> 17.8 us  [leaves(): pl.pallas_call(leaves_kernel, in_specs=[vmem], out_specs=vmem, out_shape=...]
  transfers between devices with their start and end apart: 9 -> 9, of which waited for: 5 -> 5; matrix products, arithmetic and copies ran while one was open for 3% -> 4% of each run, Pallas kernels for 4% -> 6%
where the time goes in v3:
time: 95.9 us; the launch traced here: 95.5 us
  Pallas kernels  46 us (48%)
  waiting for transfers between devices  20.3 us (21%)
  starting transfers between devices  18.8 us (20%)
  local copies, waits for them, and re-layouts  8.99 us (9%)
  other arithmetic  1.13 us (1%)
    pallas_call x1, Pallas kernels, leaves(): pl.pallas_call(leaves_kernel, in_specs=[vmem], out_specs=vmem, out_shape=...  17.8 us
    pallas_call x1, Pallas kernels, route(): pl.pallas_call(route_kernel, in_specs=[pl.BlockSpec(memory_space=pltpu.HB...  13.8 us
    all_to_all x1, waiting for transfers between devices, body(): lax.all_to_all(send, ('gx', 'gy'), split_axis=0, concat_axis=0, tiled=True)  12.2 us
    all_to_all x1, starting transfers between devices, body(): lax.all_to_all(send, ('gx', 'gy'), split_axis=0, concat_axis=0, tiled=True)  11.5 us
    unnamed x41, local copies, waits for them, and re-layouts  7.65 us
    ppermute x6, waiting for transfers between devices, body(): got.append(lax.ppermute(outs[shift], 'gx', pairs))  7.12 us
    pallas_call x1, Pallas kernels, inner(): pl.pallas_call(inner_kernel, in_specs=[vmem] * 6, out_specs=[vmem] * 2, o...  6.42 us
    ppermute x6, starting transfers between devices, body(): got.append(lax.ppermute(outs[shift], 'gx', pairs))  5.67 us
  transfers between devices with their start and end apart: 9, of which 5 were waited for; matrix products, arithmetic and copies ran while one was open for 4% of the time, Pallas kernels for 6%

profile of v3, /device:TPU:1, one launch (start us, length us, event | category | flops | bytes accessed | tf_op | source)
XLA Modules:
  0.0 95.5 jit_solution(6242546711989042277)
XLA Ops:
  0.0 1.0 %copy-done = bf16[32,8192]{1,0:T(8,128)(2,1)S(1)} copy-done((bf16[32,8192]{1,0:T(8,128)(2,1)S(1)}, bf16[32,8192]{1,0:T(8,128)(2,1)}, u32[]{:S(2)}) %copy-start) | copy-done | bytes 524312
  1.0 0.8 copy-done.1
  1.9 0.8 copy-done.2
  2.6 13.8 %route.1 = bf16[128,5,8,128]{3,2,1,0:T(8,128)(2,1)} custom-call(s32[1,8192]{1,0:T(1,128)S(1)} %bitcast.13, s32[2,8192]{1,0:T(2,128)S(1)} %copy-done.1, bf16[32,8192]{1,0:T(8,128)(2,1)S(1)} %copy-done), custom_call_target="tpu_custom_call" | custom-call | flops 15000000512 | tf_op jit(solution)/shard_map/route/pallas_call | solution.py:194
  16.4 11.5 %all-to-all-start = ((bf16[128,5,8,128]{3,2,1,0:T(8,128)(2,1)}), bf16[128,5,8,128]{3,2,1,0:T(8,128)(2,1)S(1)}, u32[]{:S(2)}, u32[]{:S(2)}) async-start(bf16[128,5,8,128]{3,2,1,0:T(8,128)(2,1)} %route.1), calls=%async_computation | async-start | bytes 2621440 | tf_op jit(solution)/shard_map/all_to_all | solution.py:566
  27.9 0.9 copy.5
  28.8 1.1 %reshape.10 = bf16[11,2,2,2,64,64]{5,4,2,1,0,3:T(8,128)(2,1)S(1)} reshape(bf16[11,2,2,2,4096]{4,2,1,0,3:T(2,128)(2,1)S(1)} %copy.5) | data formatting | bytes 1441792 | tf_op jit(solution)/shard_map/reshape | solution.py:552
  30.2 0.7 copy-done.13
  30.9 0.8 maximum_maximum_fusion
  31.9 1.7 %phases.1 = (f32[8,16,8,128]{3,2,1,0:T(8,128)S(1)}, f32[8,16,8,128]{3,2,1,0:T(8,128)S(1)}, f32[2,2,16,8,128]{4,3,2,1,0:T(8,128)S(1)}, f32[2,2,16,8,128]{4,3,2,1,...) custom-call(s32[3]{0:T(128)S(1)} %pad_add_fusion.where_ref.after_ref), custom_call_target="tpu_custom_call" | custom-call | flops 2000000000 | tf_op jit(solution)/shard_map/phases/pallas_call | solution.py:258
  33.7 0.7 copy-done.3
  34.4 0.7 copy-done.5
  35.1 0.7 copy-done.7
  35.8 0.7 copy-done.9
  36.5 0.6 copy-done.11
  37.1 12.2 %all-to-all-done.got_ref = bf16[128,5,8,128]{3,2,1,0:T(8,128)(2,1)S(1)} async-done(((bf16[128,5,8,128]{3,2,1,0:T(8,128)(2,1)}), bf16[128,5,8,128]{3,2,1,0:T(8,128)(2,1)S(1)}, u32[]{:S(2)}, u32[]{:S(2)}) %all-to-all-start) | async-done | bytes 1310752 | tf_op jit(solution)/shard_map/all_to_all | solution.py:566
  49.3 17.8 %leaves.1.leaf_ref = bf16[2,4,2,256,128]{4,3,2,1,0:T(8,128)(2,1)S(1)} custom-call(bf16[128,5,8,128]{3,2,1,0:T(8,128)(2,1)S(1)} %all-to-all-done.got_ref), custom_call_target="tpu_custom_call" | custom-call | flops 19000000512 | tf_op jit(solution)/shard_map/leaves/pallas_call | solution.py:364
  67.1 6.4 %inner.1 = (bf16[2,2,2,256,128]{4,3,2,1,0:T(8,128)(2,1)S(1)}, bf16[2,2,2,256,128]{4,3,2,1,0:T(8,128)(2,1)S(1)}) custom-call(bf16[2,4,2,256,128]{4,3,2,1,0:T(8,128)(2,1)S(1)} %leaves.1.leaf_ref, bf16[9,2,2,128,128]{4,3,2,1,0:T(8,128)(2,1)S(1)} %slice.18.mats_ref, f32[8,16,8,128]{3,2,1,0:T(8,128)S(1)} %get-tuple-element.23.level_c, ...), custom_call_target="tpu_custom_call" | custom-call | flops 6000000000 | tf_op jit(solution)/shard_map/inner/pallas_call | solution.py:467
  73.6 1.3 %collective-permute-start = (bf16[2,2,2,256,128]{4,3,2,1,0:T(8,128)(2,1)S(1)}, bf16[2,2,2,256,128]{4,3,2,1,0:T(8,128)(2,1)S(1)}, u32[]{:S(2)}, u32[]{:S(2)}) collective-permute-start(bf16[2,2,2,256,128]{4,3,2,1,0:T(8,128)(2,1)S(1)} %get-tuple-element.27.mine_ref), channel_id=1, source_target_pairs={{0,1},{1,0},{2,3},{3,2},{4,5},{5,4},{6,7},{7,6},{8,9},{9,8},{10,11... | collective-permute-start | bytes 1572872 | tf_op jit(solution)/shard_map/ppermute | solution.py:576
  74.8 0.4 collective-permute-start.4
  75.4 1.0 %collective-permute-done.other_ref = bf16[2,2,2,256,128]{4,3,2,1,0:T(8,128)(2,1)S(1)} collective-permute-done((bf16[2,2,2,256,128]{4,3,2,1,0:T(8,128)(2,1)S(1)}, bf16[2,2,2,256,128]{4,3,2,1,0:T(8,128)(2,1)S(1)}, u32[]{:S(2)}, u32[]{:S(2)}) %collective-permute-start) | collective-permute-done | bytes 524320 | tf_op jit(solution)/shard_map/ppermute | solution.py:576
  76.4 1.9 %outer.2 = (bf16[2,256,128]{2,1,0:T(8,128)(2,1)S(1)}, bf16[2,256,128]{2,1,0:T(8,128)(2,1)S(1)}, bf16[2,256,128]{2,1,0:T(8,128)(2,1)S(1)}, bf16[2,256,128]{2,1,0:T(8,128)(2,1)S(1)}) custom-call(s32[3]{0:T(128)S(1)} %pad_add_fusion.where_ref.after_ref, bf16[2,2,2,256,128]{4,3,2,1,0:T(8,128)(2,1)S(1)} %get-tuple-element.27.mine_ref, ...), custom_call_target="tpu_custom_call" | custom-call | flops 3000000000 | tf_op jit(solution)/shard_map/outer/pallas_call | solution.py:509
  78.4 1.6 %collective-permute-start.2 = (bf16[2,256,128]{2,1,0:T(8,128)(2,1)S(1)}, bf16[2,256,128]{2,1,0:T(8,128)(2,1)S(1)}, u32[]{:S(2)}, u32[]{:S(2)}) collective-permute-start(bf16[2,256,128]{2,1,0:T(8,128)(2,1)S(1)} %get-tuple-element.34), channel_id=1, source_target_pairs={{0,32},{16,48},{32,0},{48,16},{64,96},{80,112},{96,64},{112,80},{1... | collective-permute-start | bytes 393224 | tf_op jit(solution)/shard_map/ppermute | solution.py:582
  80.0 1.2 %collective-permute-start.3 = (bf16[2,256,128]{2,1,0:T(8,128)(2,1)S(1)}, bf16[2,256,128]{2,1,0:T(8,128)(2,1)S(1)}, u32[]{:S(2)}, u32[]{:S(2)}) collective-permute-start(bf16[2,256,128]{2,1,0:T(8,128)(2,1)S(1)} %get-tuple-element.35), channel_id=1, source_target_pairs={{0,48},{16,0},{32,16},{48,32},{64,112},{80,64},{96,80},{112,96},{1... | collective-permute-start | bytes 393224 | tf_op jit(solution)/shard_map/ppermute | solution.py:582
  81.2 1.9 %outer.3 = (bf16[2,256,128]{2,1,0:T(8,128)(2,1)S(1)}, bf16[2,256,128]{2,1,0:T(8,128)(2,1)S(1)}, bf16[2,256,128]{2,1,0:T(8,128)(2,1)S(1)}, bf16[2,256,128]{2,1,0:T(8,128)(2,1)S(1)}) custom-call(s32[3]{0:T(128)S(1)} %pad_add_fusion.where_ref.after_ref, bf16[2,2,2,256,128]{4,3,2,1,0:T(8,128)(2,1)S(1)} %get-tuple-element.36.mine_ref, ...), custom_call_target="tpu_custom_call" | custom-call | flops 3000000000 | tf_op jit(solution)/shard_map/outer/pallas_call | solution.py:509
  83.2 0.5 collective-permute-start.5
  83.7 1.9 %collective-permute-start.6 = (bf16[2,256,128]{2,1,0:T(8,128)(2,1)S(1)}, bf16[2,256,128]{2,1,0:T(8,128)(2,1)S(1)}, u32[]{:S(2)}, u32[]{:S(2)}) collective-permute-start(bf16[2,256,128]{2,1,0:T(8,128)(2,1)S(1)} %get-tuple-element.39), channel_id=1, source_target_pairs={{0,32},{16,48},{32,0},{48,16},{64,96},{80,112},{96,64},{112,80},{1... | collective-permute-start | bytes 393224 | tf_op jit(solution)/shard_map/ppermute | solution.py:582
  85.5 1.6 %collective-permute-done.1.refs_1_ = bf16[2,256,128]{2,1,0:T(8,128)(2,1)S(1)} collective-permute-done((bf16[2,256,128]{2,1,0:T(8,128)(2,1)S(1)}, bf16[2,256,128]{2,1,0:T(8,128)(2,1)S(1)}, u32[]{:S(2)}, u32[]{:S(2)}) %collective-permute-start.1) | collective-permute-done | bytes 131104 | tf_op jit(solution)/shard_map/ppermute | solution.py:582
  87.1 0.4 collective-permute-start.7
  87.5 5.3 %collective-permute-done.5.refs_5_ = bf16[2,256,128]{2,1,0:T(8,128)(2,1)S(1)} collective-permute-done((bf16[2,256,128]{2,1,0:T(8,128)(2,1)S(1)}, bf16[2,256,128]{2,1,0:T(8,128)(2,1)S(1)}, u32[]{:S(2)}, u32[]{:S(2)}) %collective-permute-start.5) | collective-permute-done | bytes 131104 | tf_op jit(solution)/shard_map/ppermute | solution.py:582
  92.8 0.2 collective-permute-done.7.refs_7_
  93.1 2.4 %finish.1 = bf16[128,4096]{1,0:T(8,128)(2,1)} custom-call(s32[3]{0:T(128)S(1)} %pad_add_fusion.where_ref.after_ref, bf16[2,256,128]{2,1,0:T(8,128)(2,1)S(1)} %get-tuple-element.32.after_ref.refs_0_, bf16[2,256,128]{2,1,0:T(8,128)(2,1)S(1)} %collective-permute-done.1.refs_1_, bf16[2,256,128]{2,1,0:T(8,128)(2,1)S(1)} %collective-permute-done.2.refs_2_, ...), custom_call_target="tpu_custom_call" | custom-call | flops 3000000000 | tf_op jit(solution)/shard_map/finish/pallas_call | solution.py:539
  (41 shorter events, 0.7 us)
Async XLA Ops:
  0.0 1.0 %copy-start = (bf16[32,8192]{1,0:T(8,128)(2,1)S(1)}, bf16[32,8192]{1,0:T(8,128)(2,1)}, u32[]{:S(2)}) copy-start(bf16[32,8192]{1,0:T(8,128)(2,1)} %value_hbm.1) | copy-start | bytes 1572868
  1.0 0.8 copy-start.1
  1.9 0.8 copy-start.2
  16.4 11.5 %copy-start.19 = (bf16[11,2,2,2,4096]{4,3,2,1,0:T(2,128)(2,1)S(1)}, bf16[11,2,2,2,4096]{4,3,2,1,0:T(2,128)(2,1)}, u32[]{:S(2)}) copy-start(bf16[11,2,2,2,4096]{4,3,2,1,0:T(2,128)(2,1)} %param.7) | copy-start | bytes 2162692
  16.4 32.8 %all-to-all-start = ((bf16[128,5,8,128]{3,2,1,0:T(8,128)(2,1)}), bf16[128,5,8,128]{3,2,1,0:T(8,128)(2,1)S(1)}, u32[]{:S(2)}, u32[]{:S(2)}) async-start(bf16[128,5,8,128]{3,2,1,0:T(8,128)(2,1)} %route.1), calls=%async_computation | async-start | bytes 2621440 | tf_op jit(solution)/shard_map/all_to_all | solution.py:566
  30.1 0.9 copy-start.13
  30.2 1.5 %copy-start.15 = (bf16[11,2,2,64,64]{4,3,2,1,0:T(8,128)(2,1)}, bf16[11,2,2,64,64]{4,3,2,1,0:T(8,128)(2,1)S(1)}, u32[]{:S(2)}) copy-start(bf16[11,2,2,64,64]{4,3,2,1,0:T(8,128)(2,1)S(1)} %get-tuple-element.41) | copy-start | bytes 1081348
  30.2 1.5 %copy-start.17 = (bf16[11,2,2,64,64]{4,3,2,1,0:T(8,128)(2,1)}, bf16[11,2,2,64,64]{4,3,2,1,0:T(8,128)(2,1)S(1)}, u32[]{:S(2)}) copy-start(bf16[11,2,2,64,64]{4,3,2,1,0:T(8,128)(2,1)S(1)} %get-tuple-element.42) | copy-start | bytes 1081348
  33.7 0.7 copy-start.3
  34.4 0.7 copy-start.5
  35.1 0.7 copy-start.7
  35.8 0.7 copy-start.9
  36.5 0.6 copy-start.11
  49.3 17.8 %copy-start.8 = (f32[2,2,16,8,128]{4,3,2,1,0:T(8,128)S(1)}, f32[2,2,16,8,128]{4,3,2,1,0:T(8,128)}, u32[]{:S(2)}) copy-start(f32[2,2,16,8,128]{4,3,2,1,0:T(8,128)} %copy-done.7) | copy-start | bytes 786436
  49.3 17.8 %copy-start.10 = (f32[2,2,16,8,128]{4,3,2,1,0:T(8,128)S(1)}, f32[2,2,16,8,128]{4,3,2,1,0:T(8,128)}, u32[]{:S(2)}) copy-start(f32[2,2,16,8,128]{4,3,2,1,0:T(8,128)} %copy-done.9) | copy-start | bytes 786436
  67.1 8.1 %copy-start.14 = (bf16[11,2,2,64,64]{4,3,2,1,0:T(8,128)(2,1)S(1)}, bf16[11,2,2,64,64]{4,3,2,1,0:T(8,128)(2,1)}, u32[]{:S(2)}) copy-start(bf16[11,2,2,64,64]{4,3,2,1,0:T(8,128)(2,1)} %copy-done.13) | copy-start | bytes 1081348
  67.1 8.1 %copy-start.16 = (bf16[11,2,2,64,64]{4,3,2,1,0:T(8,128)(2,1)S(1)}, bf16[11,2,2,64,64]{4,3,2,1,0:T(8,128)(2,1)}, u32[]{:S(2)}) copy-start(bf16[11,2,2,64,64]{4,3,2,1,0:T(8,128)(2,1)} %copy-done.15) | copy-start | bytes 1081348
  67.1 8.1 %copy-start.18 = (bf16[11,2,2,64,64]{4,3,2,1,0:T(8,128)(2,1)S(1)}, bf16[11,2,2,64,64]{4,3,2,1,0:T(8,128)(2,1)}, u32[]{:S(2)}) copy-start(bf16[11,2,2,64,64]{4,3,2,1,0:T(8,128)(2,1)} %copy-done.17) | copy-start | bytes 1081348
  73.5 2.9 %copy-start.4 = (f32[2,2,16,8,128]{4,3,2,1,0:T(8,128)S(1)}, f32[2,2,16,8,128]{4,3,2,1,0:T(8,128)}, u32[]{:S(2)}) copy-start(f32[2,2,16,8,128]{4,3,2,1,0:T(8,128)} %copy-done.3) | copy-start | bytes 786436
  73.5 2.8 %copy-start.6 = (f32[2,2,16,8,128]{4,3,2,1,0:T(8,128)S(1)}, f32[2,2,16,8,128]{4,3,2,1,0:T(8,128)}, u32[]{:S(2)}) copy-start(f32[2,2,16,8,128]{4,3,2,1,0:T(8,128)} %copy-done.5) | copy-start | bytes 786436
  73.5 2.8 %copy-start.12 = (f32[16,128]{1,0:T(8,128)S(1)}, f32[16,128]{1,0:T(8,128)}, u32[]{:S(2)}) copy-start(f32[16,128]{1,0:T(8,128)} %copy-done.11) | copy-start | bytes 24580
  73.6 2.8 %collective-permute-start = (bf16[2,2,2,256,128]{4,3,2,1,0:T(8,128)(2,1)S(1)}, bf16[2,2,2,256,128]{4,3,2,1,0:T(8,128)(2,1)S(1)}, u32[]{:S(2)}, u32[]{:S(2)}) collective-permute-start(bf16[2,2,2,256,128]{4,3,2,1,0:T(8,128)(2,1)S(1)} %get-tuple-element.27.mine_ref), channel_id=1, source_target_pairs={{0,1},{1,0},{2,3},{3,2},{4,5},{5,4},{6,7},{7,6},{8,9},{9,8},{10,11... | collective-permute-start | bytes 1572872 | tf_op jit(solution)/shard_map/ppermute | solution.py:576
  74.8 6.4 %collective-permute-start.4 = (bf16[2,2,2,256,128]{4,3,2,1,0:T(8,128)(2,1)S(1)}, bf16[2,2,2,256,128]{4,3,2,1,0:T(8,128)(2,1)S(1)}, u32[]{:S(2)}, u32[]{:S(2)}) collective-permute-start(bf16[2,2,2,256,128]{4,3,2,1,0:T(8,128)(2,1)S(1)} %get-tuple-element.36.mine_ref), channel_id=1, source_target_pairs={{0,1},{1,0},{2,3},{3,2},{4,5},{5,4},{6,7},{7,6},{8,9},{9,8},{10,11... | collective-permute-start | bytes 1572872 | tf_op jit(solution)/shard_map/ppermute | solution.py:576
  78.3 8.8 %collective-permute-start.1 = (bf16[2,256,128]{2,1,0:T(8,128)(2,1)S(1)}, bf16[2,256,128]{2,1,0:T(8,128)(2,1)S(1)}, u32[]{:S(2)}, u32[]{:S(2)}) collective-permute-start(bf16[2,256,128]{2,1,0:T(8,128)(2,1)S(1)} %get-tuple-element.33), channel_id=1, source_target_pairs={{0,16},{16,32},{32,48},{48,0},{64,80},{80,96},{96,112},{112,64},{1... | collective-permute-start | bytes 393224 | tf_op jit(solution)/shard_map/ppermute | solution.py:582
  78.4 9.1 %collective-permute-start.2 = (bf16[2,256,128]{2,1,0:T(8,128)(2,1)S(1)}, bf16[2,256,128]{2,1,0:T(8,128)(2,1)S(1)}, u32[]{:S(2)}, u32[]{:S(2)}) collective-permute-start(bf16[2,256,128]{2,1,0:T(8,128)(2,1)S(1)} %get-tuple-element.34), channel_id=1, source_target_pairs={{0,32},{16,48},{32,0},{48,16},{64,96},{80,112},{96,64},{112,80},{1... | collective-permute-start | bytes 393224 | tf_op jit(solution)/shard_map/ppermute | solution.py:582
  80.0 7.5 %collective-permute-start.3 = (bf16[2,256,128]{2,1,0:T(8,128)(2,1)S(1)}, bf16[2,256,128]{2,1,0:T(8,128)(2,1)S(1)}, u32[]{:S(2)}, u32[]{:S(2)}) collective-permute-start(bf16[2,256,128]{2,1,0:T(8,128)(2,1)S(1)} %get-tuple-element.35), channel_id=1, source_target_pairs={{0,48},{16,0},{32,16},{48,32},{64,112},{80,64},{96,80},{112,96},{1... | collective-permute-start | bytes 393224 | tf_op jit(solution)/shard_map/ppermute | solution.py:582
  83.2 9.7 %collective-permute-start.5 = (bf16[2,256,128]{2,1,0:T(8,128)(2,1)S(1)}, bf16[2,256,128]{2,1,0:T(8,128)(2,1)S(1)}, u32[]{:S(2)}, u32[]{:S(2)}) collective-permute-start(bf16[2,256,128]{2,1,0:T(8,128)(2,1)S(1)} %get-tuple-element.38), channel_id=1, source_target_pairs={{0,16},{16,32},{32,48},{48,0},{64,80},{80,96},{96,112},{112,64},{1... | collective-permute-start | bytes 393224 | tf_op jit(solution)/shard_map/ppermute | solution.py:582
  83.7 9.2 %collective-permute-start.6 = (bf16[2,256,128]{2,1,0:T(8,128)(2,1)S(1)}, bf16[2,256,128]{2,1,0:T(8,128)(2,1)S(1)}, u32[]{:S(2)}, u32[]{:S(2)}) collective-permute-start(bf16[2,256,128]{2,1,0:T(8,128)(2,1)S(1)} %get-tuple-element.39), channel_id=1, source_target_pairs={{0,32},{16,48},{32,0},{48,16},{64,96},{80,112},{96,64},{112,80},{1... | collective-permute-start | bytes 393224 | tf_op jit(solution)/shard_map/ppermute | solution.py:582
  87.1 6.0 %collective-permute-start.7 = (bf16[2,256,128]{2,1,0:T(8,128)(2,1)S(1)}, bf16[2,256,128]{2,1,0:T(8,128)(2,1)S(1)}, u32[]{:S(2)}, u32[]{:S(2)}) collective-permute-start(bf16[2,256,128]{2,1,0:T(8,128)(2,1)S(1)} %get-tuple-element.40), channel_id=1, source_target_pairs={{0,48},{16,0},{32,16},{48,32},{64,112},{80,64},{96,80},{112,96},{1... | collective-permute-start | bytes 393224 | tf_op jit(solution)/shard_map/ppermute | solution.py:582

commit v4 on v3

--- a/solution.py
+++ b/solution.py
@@ -24,7 +24,6 @@
 HALF = 2
 RANK_UNROLL = 8
 ROUTE_UNROLL = 8
-LEAF_UNROLL = 32
 
 
 def matmul_nt(lhs, rhs):
@@ -206,7 +205,7 @@
             pltpu.VMEM((2, 2, 544, 256), F32),
             pltpu.SemaphoreType.DMA((3,)),
         ],
-        compiler_params=pltpu.CompilerParams(vmem_limit_bytes=40 * MIB),
+        compiler_params=pltpu.CompilerParams(vmem_limit_bytes=60 * MIB),
         cost_estimate=cost(15),
         name="route",
     )(owner, point, value)
@@ -339,22 +338,19 @@
     def run(*accs):
         for y in range(4):
 
-            def one(step, carried):
-                for u in range(LEAF_UNROLL):
-                    for m in range(2):
-                        source = (step * LEAF_UNROLL + u) * 4 + m * 2
-                        boxes0, spread0 = operands(source, y)
-                        boxes1, spread1 = operands(source + 1, y)
-                        boxes = jnp.concatenate([boxes0, boxes1], axis=1)
-                        spread = jnp.concatenate([spread0, spread1], axis=1)
-                        pltpu.matmul_push_rhs(boxes, u % 2, m, transpose=True)
-                        pltpu.matmul_acc_lhs(accs[m], spread, load_staged_rhs=u % 2)
-                return carried
-
-            lax.fori_loop(0, 32 // LEAF_UNROLL, one, 0)
+            for step in range(32):
+                for m in range(2):
+                    source = step * 4 + m * 2
+                    boxes0, spread0 = operands(source, y)
+                    boxes1, spread1 = operands(source + 1, y)
+                    boxes = jnp.concatenate([boxes0, boxes1], axis=1)
+                    spread = jnp.concatenate([spread0, spread1], axis=1)
+                    pltpu.matmul_push_rhs(boxes, step % 2, m, transpose=True)
+                    pltpu.matmul_acc_lhs(accs[m], spread, load_staged_rhs=step % 2)
             total = pltpu.matmul_pop(accs[0]) + pltpu.matmul_pop(accs[1])
             for h in range(4):
-                out_ref[h // 2, y, h % 2] = total[h * 128 : (h + 1) * 128].T.astype(BF16)
+                rows = pl.ds(y * HALF + h % HALF, 256, stride=8)
+                out_ref[h // HALF, rows, :] = total[h * 128 : (h + 1) * 128].T
 
     pl.run_scoped(run, pltpu.ACC(0)((512, 256), F32), pltpu.ACC(1)((512, 256), F32))
 
@@ -365,7 +361,7 @@
         leaves_kernel,
         in_specs=[vmem],
         out_specs=vmem,
-        out_shape=jax.ShapeDtypeStruct((2, 4, HALF, 256, 128), BF16),
+        out_shape=jax.ShapeDtypeStruct((2, 2048, 128), F32),
         scratch_shapes=[pltpu.VMEM((128, 8, 128), F32)],
         compiler_params=pltpu.CompilerParams(vmem_limit_bytes=40 * MIB),
         cost_estimate=cost(19),
@@ -374,25 +370,34 @@
 
 
 def inner_kernel(leaf_ref, mats_ref, level_c, level_s, eight_c, eight_s, out0, out1, work0, work1):
-    works = (work0, work1)
-    for half in range(2):
-        for y in range(4):
-            for h in range(HALF):
-                piece = leaf_ref[half, y, h].astype(F32)
-                works[half][pl.ds(y * HALF + h, 256, stride=8), :] = piece
-    pl.run_scoped(
-        lambda *accs: inner_levels(
-            mats_ref, level_c, level_s, eight_c, eight_s, (out0, out1), works, accs
-        ),
-        *[pltpu.ACC(number % 2)((256, 256), F32) for number in range(8)],
-    )
-
-
-def four_products(accs, lefts, right, load):
+    tables = (level_c, level_s, eight_c, eight_s)
+
+    def run(*accs):
+        halves = [
+            (leaf_ref.at[0], work0, out0, accs[:4]),
+            (leaf_ref.at[1], work1, out1, accs[4:]),
+        ]
+        for number, (leaf, _, _, own) in enumerate(halves):
+            level_products(0, mats_ref, leaf, own, number == 0)
+        for level in range(2 * LEVX):
+            for number, (_, work, _, own) in enumerate(halves):
+                level_turns(level, tables, work, own)
+                if level < 2 * LEVX - 1:
+                    level_products(level + 1, mats_ref, work, own, number == 0)
+                else:
+                    eighth_products(mats_ref, work, own, number == 0)
+        for _, _, out, own in halves:
+            eighth_turns(tables, out, own)
+
+    pl.run_scoped(run, *[pltpu.ACC(number % 2)((256, 256), F32) for number in range(8)])
+
+
+def four_products(accs, lefts, level, mats_ref, load):
     for number, left in enumerate(lefts):
         if load and number < 2:
-            pltpu.matmul_push_rhs(right, 0, number, transpose=True)
-            pltpu.matmul_acc_lhs(accs[number], left, load_staged_rhs=0)
+            right = level_matrix(mats_ref, level)
+            pltpu.matmul_push_rhs(right, level % 2, number, transpose=True)
+            pltpu.matmul_acc_lhs(accs[number], left, load_staged_rhs=level % 2)
         else:
             pltpu.matmul_acc_lhs(accs[number], left)
 
@@ -401,65 +406,65 @@
     return pl.ds((x * 16 + y) * 8, 8)
 
 
-def line(work, axis, at):
-    if axis == 0:
+def line(work, level, at):
+    if level % 2 == 0:
         return work[pl.ds(at * 128, 128), :].astype(BF16)
     return jnp.concatenate([work[box_rows(x, at), :] for x in range(16)], axis=0).astype(BF16)
 
 
-def inner_levels(mats_ref, level_c, level_s, eight_c, eight_s, outs, works, accs):
-    for depth in range(LEVX):
-        below = LEVX - 1 - depth
-        starts = level_starts(depth)
-        for axis in range(2):
-            level = 2 * depth + axis
-            right = level_matrix(mats_ref, level)
-            for half, work in enumerate(works):
-                lefts = []
-                for number in range(4):
-                    pair = starts[2 * number : 2 * number + 2]
-                    first = [high << below + 1 | low for high, low in pair]
-                    ends = [[line(work, axis, s | t << below) for s in first] for t in range(2)]
-                    ends = [jnp.concatenate(end, axis=0) for end in ends]
-                    lefts.append(jnp.concatenate(ends, axis=1))
-                four_products(accs[4 * half : 4 * half + 4], lefts, right, half == 0)
-            for half, work in enumerate(works):
-                for number in range(4):
-                    made = pltpu.matmul_pop(accs[4 * half + number])
-                    for place in range(2):
-                        high, low = starts[2 * number + place]
-                        for t in range(2):
-                            cosine = level_c[level, 4 * number + 2 * place + t]
-                            sine = level_s[level, 4 * number + 2 * place + t]
-                            piece = made[place * 128 : (place + 1) * 128, t * 128 : (t + 1) * 128]
-                            piece = turn(piece.reshape(16, 8, 128), cosine[None], sine[None])
-                            end = high << below + 1 | low | t << below
-                            if axis == 0:
-                                work[pl.ds(end * 128, 128), :] = piece.reshape(128, 128)
-                            else:
-                                for x in range(16):
-                                    work[box_rows(x, end), :] = piece[x]
-
-    right = level_matrix(mats_ref, 2 * LEVX)
-    for half, work in enumerate(works):
-        lefts = []
-        for pair in range(2):
-            for h in range(HALF):
-                both = [
-                    work[pl.ds((2 * pair + c) * HALF + h, 256, stride=8), :].astype(BF16)
-                    for c in range(2)
-                ]
-                lefts.append(jnp.concatenate(both, axis=1))
-        four_products(accs[4 * half : 4 * half + 4], lefts, right, half == 0)
-    for half, out_ref in enumerate(outs):
-        for pair in range(2):
-            tables = [(eight_c[pair, t][:, None], eight_s[pair, t][:, None]) for t in range(2)]
-            for h in range(HALF):
-                made = pltpu.matmul_pop(accs[4 * half + pair * HALF + h])
-                for t in range(2):
-                    piece = made[:, t * 128 : (t + 1) * 128].reshape(16, 2, 8, 128)
-                    piece = turn(piece, *tables[t]).reshape(256, 128)
-                    out_ref[pair, t, h] = piece.astype(BF16)
+def level_products(level, mats_ref, work, accs, load):
+    below = LEVX - 1 - level // 2
+    starts = [high << below + 1 | low for high, low in level_starts(level // 2)]
+    lefts = []
+    for number in range(4):
+        first = starts[2 * number : 2 * number + 2]
+        ends = [[line(work, level, s | t << below) for s in first] for t in range(2)]
+        ends = [jnp.concatenate(end, axis=0) for end in ends]
+        lefts.append(jnp.concatenate(ends, axis=1))
+    four_products(accs, lefts, level, mats_ref, load)
+
+
+def level_turns(level, tables, work, accs):
+    level_c, level_s = tables[:2]
+    below = LEVX - 1 - level // 2
+    starts = [high << below + 1 | low for high, low in level_starts(level // 2)]
+    for number in range(4):
+        made = pltpu.matmul_pop(accs[number])
+        for place in range(2):
+            at = 2 * number + place
+            for t in range(2):
+                piece = made[place * 128 : (place + 1) * 128, t * 128 : (t + 1) * 128]
+                cosine, sine = level_c[level, 2 * at + t], level_s[level, 2 * at + t]
+                piece = turn(piece.reshape(16, 8, 128), cosine[None], sine[None])
+                end = starts[at] | t << below
+                if level % 2 == 0:
+                    work[pl.ds(end * 128, 128), :] = piece.reshape(128, 128)
+                else:
+                    for x in range(16):
+                        work[box_rows(x, end), :] = piece[x]
+
+
+def eighth_products(mats_ref, work, accs, load):
+    lefts = []
+    for pair in range(2):
+        for h in range(HALF):
+            both = [
+                work[pl.ds((2 * pair + c) * HALF + h, 256, stride=8), :].astype(BF16)
+                for c in range(2)
+            ]
+            lefts.append(jnp.concatenate(both, axis=1))
+    four_products(accs, lefts, 2 * LEVX, mats_ref, load)
+
+
+def eighth_turns(tables, out_ref, accs):
+    eight_c, eight_s = tables[2:]
+    for pair in range(2):
+        for h in range(HALF):
+            made = pltpu.matmul_pop(accs[pair * HALF + h])
+            for t in range(2):
+                piece = made[:, t * 128 : (t + 1) * 128].reshape(16, 2, 8, 128)
+                piece = turn(piece, eight_c[pair, t][:, None], eight_s[pair, t][:, None])
+                out_ref[pair, t, h] = piece.reshape(256, 128).astype(BF16)
 
 
 def inner(leaf, mats, tables):
@@ -471,7 +476,7 @@
         out_shape=[jax.ShapeDtypeStruct((2, 2, HALF, 256, 128), BF16)] * 2,
         scratch_shapes=[pltpu.VMEM((2048, 128), F32)] * 2,
         compiler_params=pltpu.CompilerParams(vmem_limit_bytes=40 * MIB),
-        cost_estimate=cost(6),
+        cost_estimate=cost(5),
         name="inner",
     )(leaf, mats, *tables[:4])
 

time: 95.9 us -> 94 us (0.980)
  local copies, waits for them, and re-layouts: 8.99 us -> 6.31 us
    unnamed x41 -> x35, local copies, waits for them, and re-layouts: 7.65 us -> 4.98 us
where the time goes in v4:
time: 94 us; the launch traced here: 93.7 us
  Pallas kernels  46.9 us (50%)
  waiting for transfers between devices  20.3 us (22%)
  starting transfers between devices  18.8 us (20%)
  local copies, waits for them, and re-layouts  6.31 us (7%)
  other arithmetic  1.13 us (1%)
    pallas_call x1, Pallas kernels, leaves(): pl.pallas_call(leaves_kernel, in_specs=[vmem], out_specs=vmem, out_shape=...  17.8 us
    pallas_call x1, Pallas kernels, route(): pl.pallas_call(route_kernel, in_specs=[pl.BlockSpec(memory_space=pltpu.HB...  14.7 us
    all_to_all x1, waiting for transfers between devices, body(): lax.all_to_all(send, ('gx', 'gy'), split_axis=0, concat_axis=0, tiled=True)  12.2 us
    all_to_all x1, starting transfers between devices, body(): lax.all_to_all(send, ('gx', 'gy'), split_axis=0, concat_axis=0, tiled=True)  11.5 us
    ppermute x6, waiting for transfers between devices, body(): got.append(lax.ppermute(outs[shift], 'gx', pairs))  7.07 us
    pallas_call x1, Pallas kernels, inner(): pl.pallas_call(inner_kernel, in_specs=[vmem] * 6, out_specs=[vmem] * 2, o...  6.33 us
    ppermute x6, starting transfers between devices, body(): got.append(lax.ppermute(outs[shift], 'gx', pairs))  5.67 us
    unnamed x35, local copies, waits for them, and re-layouts  4.98 us
  transfers between devices with their start and end apart: 9, of which 5 were waited for; matrix products, arithmetic and copies ran while one was open for 4% of the time, Pallas kernels for 6%

profile of v4, /device:TPU:1, one launch (start us, length us, event | category | flops | bytes accessed | tf_op | source)
XLA Modules:
  0.0 93.7 jit_solution(4667355000654302191)
XLA Ops:
  0.0 14.7 %route.1 = bf16[128,5,8,128]{3,2,1,0:T(8,128)(2,1)} custom-call(s32[1,8192]{1,0:T(1,128)} %bitcast.13, s32[2,8192]{1,0:T(2,128)} %point_hbm.1, bf16[32,8192]{1,0:T(8,128)(2,1)} %value_hbm.1), custom_call_target="tpu_custom_call" | custom-call | flops 15000000512 | tf_op jit(solution)/shard_map/route/pallas_call | solution.py:193
  14.7 11.5 %all-to-all-start = ((bf16[128,5,8,128]{3,2,1,0:T(8,128)(2,1)}), bf16[128,5,8,128]{3,2,1,0:T(8,128)(2,1)S(1)}, u32[]{:S(2)}, u32[]{:S(2)}) async-start(bf16[128,5,8,128]{3,2,1,0:T(8,128)(2,1)} %route.1), calls=%async_computation | async-start | bytes 2621440 | tf_op jit(solution)/shard_map/all_to_all | solution.py:571
  26.3 0.9 copy.5
  27.1 1.1 %reshape.10 = bf16[11,2,2,2,64,64]{5,4,2,1,0,3:T(8,128)(2,1)S(1)} reshape(bf16[11,2,2,2,4096]{4,2,1,0,3:T(2,128)(2,1)S(1)} %copy.5) | data formatting | bytes 1441792 | tf_op jit(solution)/shard_map/reshape | solution.py:557
  28.3 0.1 fusion
  28.4 0.1 slice_bitcast_fusion
  28.5 0.7 copy-done.10
  29.3 0.8 maximum_maximum_fusion
  30.3 1.7 %phases.1 = (f32[8,16,8,128]{3,2,1,0:T(8,128)S(1)}, f32[8,16,8,128]{3,2,1,0:T(8,128)S(1)}, f32[2,2,16,8,128]{4,3,2,1,0:T(8,128)S(1)}, f32[2,2,16,8,128]{4,3,2,1,...) custom-call(s32[3]{0:T(128)S(1)} %pad_add_fusion.where_ref.after_ref), custom_call_target="tpu_custom_call" | custom-call | flops 2000000000 | tf_op jit(solution)/shard_map/phases/pallas_call | solution.py:257
  32.0 0.7 copy-done
  32.7 0.7 copy-done.2
  33.4 0.7 copy-done.4
  34.1 0.7 copy-done.6
  34.7 0.6 copy-done.8
  35.3 12.2 %all-to-all-done.got_ref = bf16[128,5,8,128]{3,2,1,0:T(8,128)(2,1)S(1)} async-done(((bf16[128,5,8,128]{3,2,1,0:T(8,128)(2,1)}), bf16[128,5,8,128]{3,2,1,0:T(8,128)(2,1)S(1)}, u32[]{:S(2)}, u32[]{:S(2)}) %all-to-all-start) | async-done | bytes 1310752 | tf_op jit(solution)/shard_map/all_to_all | solution.py:571
  47.6 17.8 %leaves.1.leaf_ref = f32[2,2048,128]{2,1,0:T(8,128)S(1)} custom-call(bf16[128,5,8,128]{3,2,1,0:T(8,128)(2,1)S(1)} %all-to-all-done.got_ref), custom_call_target="tpu_custom_call" | custom-call | flops 19000000512 | tf_op jit(solution)/shard_map/leaves/pallas_call | solution.py:360
  65.5 6.3 %inner.1 = (bf16[2,2,2,256,128]{4,3,2,1,0:T(8,128)(2,1)S(1)}, bf16[2,2,2,256,128]{4,3,2,1,0:T(8,128)(2,1)S(1)}) custom-call(f32[2,2048,128]{2,1,0:T(8,128)S(1)} %leaves.1.leaf_ref, bf16[9,2,2,128,128]{4,3,2,1,0:T(8,128)(2,1)S(1)} %slice.18.mats_ref, f32[8,16,8,128]{3,2,1,0:T(8,128)S(1)} %get-tuple-element.23.level_c, ...), custom_call_target="tpu_custom_call" | custom-call | flops 5000000000 | tf_op jit(solution)/shard_map/inner/pallas_call | solution.py:472
  71.8 1.3 %collective-permute-start = (bf16[2,2,2,256,128]{4,3,2,1,0:T(8,128)(2,1)S(1)}, bf16[2,2,2,256,128]{4,3,2,1,0:T(8,128)(2,1)S(1)}, u32[]{:S(2)}, u32[]{:S(2)}) collective-permute-start(bf16[2,2,2,256,128]{4,3,2,1,0:T(8,128)(2,1)S(1)} %get-tuple-element.27.mine_ref), channel_id=1, source_target_pairs={{0,1},{1,0},{2,3},{3,2},{4,5},{5,4},{6,7},{7,6},{8,9},{9,8},{10,11... | collective-permute-start | bytes 1572872 | tf_op jit(solution)/shard_map/ppermute | solution.py:581
  73.1 0.4 collective-permute-start.4
  73.5 0.2 maximum_maximum_fusion.1.mats_ref
  73.6 1.0 %collective-permute-done.other_ref = bf16[2,2,2,256,128]{4,3,2,1,0:T(8,128)(2,1)S(1)} collective-permute-done((bf16[2,2,2,256,128]{4,3,2,1,0:T(8,128)(2,1)S(1)}, bf16[2,2,2,256,128]{4,3,2,1,0:T(8,128)(2,1)S(1)}, u32[]{:S(2)}, u32[]{:S(2)}) %collective-permute-start) | collective-permute-done | bytes 524320 | tf_op jit(solution)/shard_map/ppermute | solution.py:581
  74.7 1.9 %outer.2 = (bf16[2,256,128]{2,1,0:T(8,128)(2,1)S(1)}, bf16[2,256,128]{2,1,0:T(8,128)(2,1)S(1)}, bf16[2,256,128]{2,1,0:T(8,128)(2,1)S(1)}, bf16[2,256,128]{2,1,0:T(8,128)(2,1)S(1)}) custom-call(s32[3]{0:T(128)S(1)} %pad_add_fusion.where_ref.after_ref, bf16[2,2,2,256,128]{4,3,2,1,0:T(8,128)(2,1)S(1)} %get-tuple-element.27.mine_ref, ...), custom_call_target="tpu_custom_call" | custom-call | flops 3000000000 | tf_op jit(solution)/shard_map/outer/pallas_call | solution.py:514
  76.7 1.6 %collective-permute-start.2 = (bf16[2,256,128]{2,1,0:T(8,128)(2,1)S(1)}, bf16[2,256,128]{2,1,0:T(8,128)(2,1)S(1)}, u32[]{:S(2)}, u32[]{:S(2)}) collective-permute-start(bf16[2,256,128]{2,1,0:T(8,128)(2,1)S(1)} %get-tuple-element.34), channel_id=1, source_target_pairs={{0,32},{16,48},{32,0},{48,16},{64,96},{80,112},{96,64},{112,80},{1... | collective-permute-start | bytes 393224 | tf_op jit(solution)/shard_map/ppermute | solution.py:587
  78.3 1.2 %collective-permute-start.3 = (bf16[2,256,128]{2,1,0:T(8,128)(2,1)S(1)}, bf16[2,256,128]{2,1,0:T(8,128)(2,1)S(1)}, u32[]{:S(2)}, u32[]{:S(2)}) collective-permute-start(bf16[2,256,128]{2,1,0:T(8,128)(2,1)S(1)} %get-tuple-element.35), channel_id=1, source_target_pairs={{0,48},{16,0},{32,16},{48,32},{64,112},{80,64},{96,80},{112,96},{1... | collective-permute-start | bytes 393224 | tf_op jit(solution)/shard_map/ppermute | solution.py:587
  79.5 1.9 %outer.3 = (bf16[2,256,128]{2,1,0:T(8,128)(2,1)S(1)}, bf16[2,256,128]{2,1,0:T(8,128)(2,1)S(1)}, bf16[2,256,128]{2,1,0:T(8,128)(2,1)S(1)}, bf16[2,256,128]{2,1,0:T(8,128)(2,1)S(1)}) custom-call(s32[3]{0:T(128)S(1)} %pad_add_fusion.where_ref.after_ref, bf16[2,2,2,256,128]{4,3,2,1,0:T(8,128)(2,1)S(1)} %get-tuple-element.36.mine_ref, ...), custom_call_target="tpu_custom_call" | custom-call | flops 3000000000 | tf_op jit(solution)/shard_map/outer/pallas_call | solution.py:514
  81.4 0.5 collective-permute-start.5
  81.9 1.9 %collective-permute-start.6 = (bf16[2,256,128]{2,1,0:T(8,128)(2,1)S(1)}, bf16[2,256,128]{2,1,0:T(8,128)(2,1)S(1)}, u32[]{:S(2)}, u32[]{:S(2)}) collective-permute-start(bf16[2,256,128]{2,1,0:T(8,128)(2,1)S(1)} %get-tuple-element.39), channel_id=1, source_target_pairs={{0,32},{16,48},{32,0},{48,16},{64,96},{80,112},{96,64},{112,80},{1... | collective-permute-start | bytes 393224 | tf_op jit(solution)/shard_map/ppermute | solution.py:587
  83.8 1.6 %collective-permute-done.1.refs_1_ = bf16[2,256,128]{2,1,0:T(8,128)(2,1)S(1)} collective-permute-done((bf16[2,256,128]{2,1,0:T(8,128)(2,1)S(1)}, bf16[2,256,128]{2,1,0:T(8,128)(2,1)S(1)}, u32[]{:S(2)}, u32[]{:S(2)}) %collective-permute-start.1) | collective-permute-done | bytes 131104 | tf_op jit(solution)/shard_map/ppermute | solution.py:587
  85.4 0.4 collective-permute-start.7
  85.8 5.3 %collective-permute-done.5.refs_5_ = bf16[2,256,128]{2,1,0:T(8,128)(2,1)S(1)} collective-permute-done((bf16[2,256,128]{2,1,0:T(8,128)(2,1)S(1)}, bf16[2,256,128]{2,1,0:T(8,128)(2,1)S(1)}, u32[]{:S(2)}, u32[]{:S(2)}) %collective-permute-start.5) | collective-permute-done | bytes 131104 | tf_op jit(solution)/shard_map/ppermute | solution.py:587
  91.1 0.2 collective-permute-done.7.refs_7_
  91.3 2.4 %finish.1 = bf16[128,4096]{1,0:T(8,128)(2,1)} custom-call(s32[3]{0:T(128)S(1)} %pad_add_fusion.where_ref.after_ref, bf16[2,256,128]{2,1,0:T(8,128)(2,1)S(1)} %get-tuple-element.32.after_ref.refs_0_, bf16[2,256,128]{2,1,0:T(8,128)(2,1)S(1)} %collective-permute-done.1.refs_1_, bf16[2,256,128]{2,1,0:T(8,128)(2,1)S(1)} %collective-permute-done.2.refs_2_, ...), custom_call_target="tpu_custom_call" | custom-call | flops 3000000000 | tf_op jit(solution)/shard_map/finish/pallas_call | solution.py:544
  (35 shorter events, 0.3 us)
Async XLA Ops:
  14.7 11.5 %copy-start.16 = (bf16[11,2,2,2,4096]{4,3,2,1,0:T(2,128)(2,1)S(1)}, bf16[11,2,2,2,4096]{4,3,2,1,0:T(2,128)(2,1)}, u32[]{:S(2)}) copy-start(bf16[11,2,2,2,4096]{4,3,2,1,0:T(2,128)(2,1)} %param.7) | copy-start | bytes 2162692
  14.7 32.8 %all-to-all-start = ((bf16[128,5,8,128]{3,2,1,0:T(8,128)(2,1)}), bf16[128,5,8,128]{3,2,1,0:T(8,128)(2,1)S(1)}, u32[]{:S(2)}, u32[]{:S(2)}) async-start(bf16[128,5,8,128]{3,2,1,0:T(8,128)(2,1)} %route.1), calls=%async_computation | async-start | bytes 2621440 | tf_op jit(solution)/shard_map/all_to_all | solution.py:571
  28.4 0.9 copy-start.10
  28.5 1.6 %copy-start.12 = (bf16[11,2,2,64,64]{4,3,2,1,0:T(8,128)(2,1)}, bf16[11,2,2,64,64]{4,3,2,1,0:T(8,128)(2,1)S(1)}, u32[]{:S(2)}) copy-start(bf16[11,2,2,64,64]{4,3,2,1,0:T(8,128)(2,1)S(1)} %get-tuple-element.41) | copy-start | bytes 1081348
  28.5 1.6 %copy-start.14 = (bf16[11,2,2,64,64]{4,3,2,1,0:T(8,128)(2,1)}, bf16[11,2,2,64,64]{4,3,2,1,0:T(8,128)(2,1)S(1)}, u32[]{:S(2)}) copy-start(bf16[11,2,2,64,64]{4,3,2,1,0:T(8,128)(2,1)S(1)} %get-tuple-element.42) | copy-start | bytes 1081348
  32.0 0.7 copy-start
  32.7 0.7 copy-start.2
  33.4 0.7 copy-start.4
  34.1 0.7 copy-start.6
  34.7 0.6 copy-start.8
  47.6 17.8 %copy-start.5 = (f32[2,2,16,8,128]{4,3,2,1,0:T(8,128)S(1)}, f32[2,2,16,8,128]{4,3,2,1,0:T(8,128)}, u32[]{:S(2)}) copy-start(f32[2,2,16,8,128]{4,3,2,1,0:T(8,128)} %copy-done.4) | copy-start | bytes 786436
  47.6 17.8 %copy-start.7 = (f32[2,2,16,8,128]{4,3,2,1,0:T(8,128)S(1)}, f32[2,2,16,8,128]{4,3,2,1,0:T(8,128)}, u32[]{:S(2)}) copy-start(f32[2,2,16,8,128]{4,3,2,1,0:T(8,128)} %copy-done.6) | copy-start | bytes 786436
  65.4 8.1 %copy-start.11 = (bf16[11,2,2,64,64]{4,3,2,1,0:T(8,128)(2,1)S(1)}, bf16[11,2,2,64,64]{4,3,2,1,0:T(8,128)(2,1)}, u32[]{:S(2)}) copy-start(bf16[11,2,2,64,64]{4,3,2,1,0:T(8,128)(2,1)} %copy-done.10) | copy-start | bytes 1081348
  65.4 8.0 %copy-start.13 = (bf16[11,2,2,64,64]{4,3,2,1,0:T(8,128)(2,1)S(1)}, bf16[11,2,2,64,64]{4,3,2,1,0:T(8,128)(2,1)}, u32[]{:S(2)}) copy-start(bf16[11,2,2,64,64]{4,3,2,1,0:T(8,128)(2,1)} %copy-done.12) | copy-start | bytes 1081348
  65.4 8.0 %copy-start.15 = (bf16[11,2,2,64,64]{4,3,2,1,0:T(8,128)(2,1)S(1)}, bf16[11,2,2,64,64]{4,3,2,1,0:T(8,128)(2,1)}, u32[]{:S(2)}) copy-start(bf16[11,2,2,64,64]{4,3,2,1,0:T(8,128)(2,1)} %copy-done.14) | copy-start | bytes 1081348
  71.8 2.9 %copy-start.1 = (f32[2,2,16,8,128]{4,3,2,1,0:T(8,128)S(1)}, f32[2,2,16,8,128]{4,3,2,1,0:T(8,128)}, u32[]{:S(2)}) copy-start(f32[2,2,16,8,128]{4,3,2,1,0:T(8,128)} %copy-done) | copy-start | bytes 786436
  71.8 2.9 %copy-start.3 = (f32[2,2,16,8,128]{4,3,2,1,0:T(8,128)S(1)}, f32[2,2,16,8,128]{4,3,2,1,0:T(8,128)}, u32[]{:S(2)}) copy-start(f32[2,2,16,8,128]{4,3,2,1,0:T(8,128)} %copy-done.2) | copy-start | bytes 786436
  71.8 2.9 %copy-start.9 = (f32[16,128]{1,0:T(8,128)S(1)}, f32[16,128]{1,0:T(8,128)}, u32[]{:S(2)}) copy-start(f32[16,128]{1,0:T(8,128)} %copy-done.8) | copy-start | bytes 24580
  71.8 2.8 %collective-permute-start = (bf16[2,2,2,256,128]{4,3,2,1,0:T(8,128)(2,1)S(1)}, bf16[2,2,2,256,128]{4,3,2,1,0:T(8,128)(2,1)S(1)}, u32[]{:S(2)}, u32[]{:S(2)}) collective-permute-start(bf16[2,2,2,256,128]{4,3,2,1,0:T(8,128)(2,1)S(1)} %get-tuple-element.27.mine_ref), channel_id=1, source_target_pairs={{0,1},{1,0},{2,3},{3,2},{4,5},{5,4},{6,7},{7,6},{8,9},{9,8},{10,11... | collective-permute-start | bytes 1572872 | tf_op jit(solution)/shard_map/ppermute | solution.py:581
  73.1 6.4 %collective-permute-start.4 = (bf16[2,2,2,256,128]{4,3,2,1,0:T(8,128)(2,1)S(1)}, bf16[2,2,2,256,128]{4,3,2,1,0:T(8,128)(2,1)S(1)}, u32[]{:S(2)}, u32[]{:S(2)}) collective-permute-start(bf16[2,2,2,256,128]{4,3,2,1,0:T(8,128)(2,1)S(1)} %get-tuple-element.36.mine_ref), channel_id=1, source_target_pairs={{0,1},{1,0},{2,3},{3,2},{4,5},{5,4},{6,7},{7,6},{8,9},{9,8},{10,11... | collective-permute-start | bytes 1572872 | tf_op jit(solution)/shard_map/ppermute | solution.py:581
  76.6 8.8 %collective-permute-start.1 = (bf16[2,256,128]{2,1,0:T(8,128)(2,1)S(1)}, bf16[2,256,128]{2,1,0:T(8,128)(2,1)S(1)}, u32[]{:S(2)}, u32[]{:S(2)}) collective-permute-start(bf16[2,256,128]{2,1,0:T(8,128)(2,1)S(1)} %get-tuple-element.33), channel_id=1, source_target_pairs={{0,16},{16,32},{32,48},{48,0},{64,80},{80,96},{96,112},{112,64},{1... | collective-permute-start | bytes 393224 | tf_op jit(solution)/shard_map/ppermute | solution.py:587
  76.7 9.1 %collective-permute-start.2 = (bf16[2,256,128]{2,1,0:T(8,128)(2,1)S(1)}, bf16[2,256,128]{2,1,0:T(8,128)(2,1)S(1)}, u32[]{:S(2)}, u32[]{:S(2)}) collective-permute-start(bf16[2,256,128]{2,1,0:T(8,128)(2,1)S(1)} %get-tuple-element.34), channel_id=1, source_target_pairs={{0,32},{16,48},{32,0},{48,16},{64,96},{80,112},{96,64},{112,80},{1... | collective-permute-start | bytes 393224 | tf_op jit(solution)/shard_map/ppermute | solution.py:587
  78.3 7.5 %collective-permute-start.3 = (bf16[2,256,128]{2,1,0:T(8,128)(2,1)S(1)}, bf16[2,256,128]{2,1,0:T(8,128)(2,1)S(1)}, u32[]{:S(2)}, u32[]{:S(2)}) collective-permute-start(bf16[2,256,128]{2,1,0:T(8,128)(2,1)S(1)} %get-tuple-element.35), channel_id=1, source_target_pairs={{0,48},{16,0},{32,16},{48,32},{64,112},{80,64},{96,80},{112,96},{1... | collective-permute-start | bytes 393224 | tf_op jit(solution)/shard_map/ppermute | solution.py:587
  81.4 9.7 %collective-permute-start.5 = (bf16[2,256,128]{2,1,0:T(8,128)(2,1)S(1)}, bf16[2,256,128]{2,1,0:T(8,128)(2,1)S(1)}, u32[]{:S(2)}, u32[]{:S(2)}) collective-permute-start(bf16[2,256,128]{2,1,0:T(8,128)(2,1)S(1)} %get-tuple-element.38), channel_id=1, source_target_pairs={{0,16},{16,32},{32,48},{48,0},{64,80},{80,96},{96,112},{112,64},{1... | collective-permute-start | bytes 393224 | tf_op jit(solution)/shard_map/ppermute | solution.py:587
  81.9 9.2 %collective-permute-start.6 = (bf16[2,256,128]{2,1,0:T(8,128)(2,1)S(1)}, bf16[2,256,128]{2,1,0:T(8,128)(2,1)S(1)}, u32[]{:S(2)}, u32[]{:S(2)}) collective-permute-start(bf16[2,256,128]{2,1,0:T(8,128)(2,1)S(1)} %get-tuple-element.39), channel_id=1, source_target_pairs={{0,32},{16,48},{32,0},{48,16},{64,96},{80,112},{96,64},{112,80},{1... | collective-permute-start | bytes 393224 | tf_op jit(solution)/shard_map/ppermute | solution.py:587
  85.4 5.9 %collective-permute-start.7 = (bf16[2,256,128]{2,1,0:T(8,128)(2,1)S(1)}, bf16[2,256,128]{2,1,0:T(8,128)(2,1)S(1)}, u32[]{:S(2)}, u32[]{:S(2)}) collective-permute-start(bf16[2,256,128]{2,1,0:T(8,128)(2,1)S(1)} %get-tuple-element.40), channel_id=1, source_target_pairs={{0,48},{16,0},{32,16},{48,32},{64,112},{80,64},{96,80},{112,96},{1... | collective-permute-start | bytes 393224 | tf_op jit(solution)/shard_map/ppermute | solution.py:587

commit v5 on v4

--- a/solution.py
+++ b/solution.py
@@ -293,8 +293,10 @@
     return scales * four * pltpu.roll(two, 4, axis=0) * pltpu.roll(one, 2, axis=0)
 
 
-def turn(values, cosine, sine):
-    return values * cosine + pltpu.roll(values, 64, axis=values.ndim - 1) * sine
+def swapped_parts(matrix):
+    blocks = [matrix[row : row + 64] for row in range(0, matrix.shape[0], 64)]
+    order = [number ^ 1 for number in range(len(blocks))]
+    return jnp.concatenate([blocks[number] for number in order], axis=0)
 
 
 def signs(shape):
@@ -371,35 +373,54 @@
 
 def inner_kernel(leaf_ref, mats_ref, level_c, level_s, eight_c, eight_s, out0, out1, work0, work1):
     tables = (level_c, level_s, eight_c, eight_s)
+    works, outs = (work0, work1), (out0, out1)
+    stages = [
+        (level, half, number)
+        for level in range(2 * LEVX + 1)
+        for half in range(2)
+        for number in range(2)
+    ]
 
     def run(*accs):
-        halves = [
-            (leaf_ref.at[0], work0, out0, accs[:4]),
-            (leaf_ref.at[1], work1, out1, accs[4:]),
-        ]
-        for number, (leaf, _, _, own) in enumerate(halves):
-            level_products(0, mats_ref, leaf, own, number == 0)
-        for level in range(2 * LEVX):
-            for number, (_, work, _, own) in enumerate(halves):
-                level_turns(level, tables, work, own)
-                if level < 2 * LEVX - 1:
-                    level_products(level + 1, mats_ref, work, own, number == 0)
+        def start(at):
+            level, half, number = stages[at]
+            work = leaf_ref.at[half] if level == 0 else works[half]
+            if level < 2 * LEVX:
+                lefts = level_lefts(level, work, number)
+            else:
+                lefts = eighth_lefts(work, number)
+            own = accs[at % 2 * 4 : at % 2 * 4 + 4]
+            first = half == 0 and number == 0
+            if first:
+                right = level_matrix(mats_ref, level)
+                pltpu.matmul_push_rhs(right, level % 2, 0, transpose=True)
+                pltpu.matmul_push_rhs(swapped_parts(right), level % 2, 1, transpose=True)
+            for place, left in enumerate(lefts):
+                for m in range(2):
+                    if place == 0 or m == at % 2:
+                        load = level % 2 if first and place == 0 else None
+                        pltpu.matmul_acc_lhs(own[2 * place + m], left, load_staged_rhs=load)
+
+        def finish(at):
+            level, half, number = stages[at]
+            own = accs[at % 2 * 4 : at % 2 * 4 + 4]
+            for place in range(2):
+                both = place == 0
+                made = pltpu.matmul_pop(own[2 * place]) if both or at % 2 == 0 else None
+                other = pltpu.matmul_pop(own[2 * place + 1]) if both or at % 2 == 1 else None
+                if level < 2 * LEVX:
+                    level_turns(level, tables, works[half], 2 * number + place, made, other)
                 else:
-                    eighth_products(mats_ref, work, own, number == 0)
-        for _, _, out, own in halves:
-            eighth_turns(tables, out, own)
+                    eighth_turns(tables, outs[half], number, place, made, other)
+
+        start(0)
+        start(1)
+        for at in range(len(stages)):
+            finish(at)
+            if at + 2 < len(stages):
+                start(at + 2)
 
     pl.run_scoped(run, *[pltpu.ACC(number % 2)((256, 256), F32) for number in range(8)])
-
-
-def four_products(accs, lefts, level, mats_ref, load):
-    for number, left in enumerate(lefts):
-        if load and number < 2:
-            right = level_matrix(mats_ref, level)
-            pltpu.matmul_push_rhs(right, level % 2, number, transpose=True)
-            pltpu.matmul_acc_lhs(accs[number], left, load_staged_rhs=level % 2)
-        else:
-            pltpu.matmul_acc_lhs(accs[number], left)
 
 
 def box_rows(x, y):
@@ -412,59 +433,64 @@
     return jnp.concatenate([work[box_rows(x, at), :] for x in range(16)], axis=0).astype(BF16)
 
 
-def level_products(level, mats_ref, work, accs, load):
+def level_lefts(level, work, half):
     below = LEVX - 1 - level // 2
     starts = [high << below + 1 | low for high, low in level_starts(level // 2)]
     lefts = []
-    for number in range(4):
+    for number in range(2 * half, 2 * half + 2):
         first = starts[2 * number : 2 * number + 2]
         ends = [[line(work, level, s | t << below) for s in first] for t in range(2)]
         ends = [jnp.concatenate(end, axis=0) for end in ends]
         lefts.append(jnp.concatenate(ends, axis=1))
-    four_products(accs, lefts, level, mats_ref, load)
-
-
-def level_turns(level, tables, work, accs):
+    return lefts
+
+
+def two_forms(made, other, chosen):
+    if made is None:
+        other = other[chosen]
+        return pltpu.roll(other, 64, axis=1), other
+    made = made[chosen]
+    return made, pltpu.roll(made, 64, axis=1) if other is None else other[chosen]
+
+
+def level_turns(level, tables, work, number, made, other):
     level_c, level_s = tables[:2]
     below = LEVX - 1 - level // 2
     starts = [high << below + 1 | low for high, low in level_starts(level // 2)]
-    for number in range(4):
-        made = pltpu.matmul_pop(accs[number])
-        for place in range(2):
-            at = 2 * number + place
-            for t in range(2):
-                piece = made[place * 128 : (place + 1) * 128, t * 128 : (t + 1) * 128]
-                cosine, sine = level_c[level, 2 * at + t], level_s[level, 2 * at + t]
-                piece = turn(piece.reshape(16, 8, 128), cosine[None], sine[None])
-                end = starts[at] | t << below
-                if level % 2 == 0:
-                    work[pl.ds(end * 128, 128), :] = piece.reshape(128, 128)
-                else:
-                    for x in range(16):
-                        work[box_rows(x, end), :] = piece[x]
-
-
-def eighth_products(mats_ref, work, accs, load):
+    for place in range(2):
+        at = 2 * number + place
+        for t in range(2):
+            chosen = (slice(place * 128, place * 128 + 128), slice(t * 128, t * 128 + 128))
+            cosine, sine = level_c[level, 2 * at + t], level_s[level, 2 * at + t]
+            plain, swapped = two_forms(made, other, chosen)
+            piece = plain.reshape(16, 8, 128) * cosine[None]
+            piece = piece + swapped.reshape(16, 8, 128) * sine[None]
+            end = starts[at] | t << below
+            if level % 2 == 0:
+                work[pl.ds(end * 128, 128), :] = piece.reshape(128, 128)
+            else:
+                for x in range(16):
+                    work[box_rows(x, end), :] = piece[x]
+
+
+def eighth_lefts(work, pair):
     lefts = []
-    for pair in range(2):
-        for h in range(HALF):
-            both = [
-                work[pl.ds((2 * pair + c) * HALF + h, 256, stride=8), :].astype(BF16)
-                for c in range(2)
-            ]
-            lefts.append(jnp.concatenate(both, axis=1))
-    four_products(accs, lefts, 2 * LEVX, mats_ref, load)
-
-
-def eighth_turns(tables, out_ref, accs):
+    for h in range(HALF):
+        both = [
+            work[pl.ds((2 * pair + c) * HALF + h, 256, stride=8), :].astype(BF16) for c in range(2)
+        ]
+        lefts.append(jnp.concatenate(both, axis=1))
+    return lefts
+
+
+def eighth_turns(tables, out_ref, pair, h, made, other):
     eight_c, eight_s = tables[2:]
-    for pair in range(2):
-        for h in range(HALF):
-            made = pltpu.matmul_pop(accs[pair * HALF + h])
-            for t in range(2):
-                piece = made[:, t * 128 : (t + 1) * 128].reshape(16, 2, 8, 128)
-                piece = turn(piece, eight_c[pair, t][:, None], eight_s[pair, t][:, None])
-                out_ref[pair, t, h] = piece.reshape(256, 128).astype(BF16)
+    for t in range(2):
+        chosen = (slice(None), slice(t * 128, t * 128 + 128))
+        plain, swapped = two_forms(made, other, chosen)
+        piece = plain.reshape(16, 2, 8, 128) * eight_c[pair, t][:, None]
+        piece = piece + swapped.reshape(16, 2, 8, 128) * eight_s[pair, t][:, None]
+        out_ref[pair, t, h] = piece.reshape(256, 128).astype(BF16)
 
 
 def inner(leaf, mats, tables):
@@ -491,20 +517,25 @@
     core = row_y & 1
     table = (nine_c[...][None], nine_s[...][None])
     mats_y = jnp.concatenate([mats_ref[0, core, core], mats_ref[0, core, 1 - core]], axis=1)
+    mats_y = jnp.concatenate([mats_y, swapped_parts(mats_y)], axis=0)
     mats_x = level_matrix(mats_ref, 1)
+    mats_x = jnp.concatenate([mats_x, swapped_parts(mats_x)], axis=0)
     for t8 in range(2):
         tables = [(ten_c[t8, t][:, None], ten_s[t8, t][:, None]) for t in range(2)]
         for h in range(HALF):
             both = []
             for c in range(2):
                 pair = jnp.concatenate([mine_ref[c, t8, h], other_ref[c, t8, h]], axis=1)
-                made = matmul_nt(pair, mats_y).reshape(16, 16, 128)
-                both.append(turn(made, *table).reshape(256, 128).astype(BF16))
+                made = matmul_nt(pair, mats_y)
+                piece = made[:, :128].reshape(16, 16, 128) * table[0]
+                piece = piece + made[:, 128:].reshape(16, 16, 128) * table[1]
+                both.append(piece.reshape(256, 128).astype(BF16))
             made = matmul_nt(jnp.concatenate(both, axis=1), mats_x)
             for t in range(2):
-                piece = made[:, t * 128 : (t + 1) * 128].reshape(16, 2, 8, 128)
-                piece = turn(piece, *tables[t]).reshape(256, 128)
-                held[2 * t + t8, h] = piece.astype(BF16)
+                plain = made[:, t * 128 : t * 128 + 128].reshape(16, 2, 8, 128)
+                other = made[:, t * 128 + 256 : t * 128 + 384].reshape(16, 2, 8, 128)
+                piece = plain * tables[t][0] + other * tables[t][1]
+                held[2 * t + t8, h] = piece.reshape(256, 128).astype(BF16)
     for shift in range(4):
         outs[shift][...] = held[(own + shift) & 3]
 

time: 94 us -> 92.3 us (0.982)
  Pallas kernels: 46.9 us -> 44.9 us
    pallas_call x1, Pallas kernels: 6.33 us -> 4.73 us  [inner(): pl.pallas_call(inner_kernel, in_specs=[vmem] * 6, out_specs=[vmem] * 2, o...]
  transfers between devices with their start and end apart: 9 -> 9, of which waited for: 5 -> 6; matrix products, arithmetic and copies ran while one was open for 4% -> 4% of each run, Pallas kernels for 6% -> 6%
where the time goes in v5:
time: 92.3 us; the launch traced here: 92.1 us
  Pallas kernels  44.9 us (49%)
  waiting for transfers between devices  21 us (23%)
  starting transfers between devices  18.6 us (20%)
  local copies, waits for them, and re-layouts  6.31 us (7%)
  other arithmetic  1.13 us (1%)
    pallas_call x1, Pallas kernels, leaves(): pl.pallas_call(leaves_kernel, in_specs=[vmem], out_specs=vmem, out_shape=...  17.8 us
    pallas_call x1, Pallas kernels, route(): pl.pallas_call(route_kernel, in_specs=[pl.BlockSpec(memory_space=pltpu.HB...  14.7 us
    all_to_all x1, waiting for transfers between devices, body(): lax.all_to_all(send, ('gx', 'gy'), split_axis=0, concat_axis=0, tiled=True)  12.2 us
    all_to_all x1, starting transfers between devices, body(): lax.all_to_all(send, ('gx', 'gy'), split_axis=0, concat_axis=0, tiled=True)  11.5 us
    ppermute x6, waiting for transfers between devices, body(): got.append(lax.ppermute(outs[shift], 'gx', pairs))  7.46 us
    ppermute x6, starting transfers between devices, body(): got.append(lax.ppermute(outs[shift], 'gx', pairs))  5.71 us
    unnamed x35, local copies, waits for them, and re-layouts  4.98 us
    pallas_call x1, Pallas kernels, inner(): pl.pallas_call(inner_kernel, in_specs=[vmem] * 6, out_specs=[vmem] * 2, o...  4.73 us
  transfers between devices with their start and end apart: 9, of which 6 were waited for; matrix products, arithmetic and copies ran while one was open for 4% of the time, Pallas kernels for 6%

profile of v5, /device:TPU:1, one launch (start us, length us, event | category | flops | bytes accessed | tf_op | source)
XLA Modules:
  0.0 92.1 jit_solution(14781453268828287369)
XLA Ops:
  0.0 14.7 %route.1 = bf16[128,5,8,128]{3,2,1,0:T(8,128)(2,1)} custom-call(s32[1,8192]{1,0:T(1,128)} %bitcast.13, s32[2,8192]{1,0:T(2,128)} %point_hbm.1, bf16[32,8192]{1,0:T(8,128)(2,1)} %value_hbm.1), custom_call_target="tpu_custom_call" | custom-call | flops 15000000512 | tf_op jit(solution)/shard_map/route/pallas_call | solution.py:193
  14.7 11.5 %all-to-all-start = ((bf16[128,5,8,128]{3,2,1,0:T(8,128)(2,1)}), bf16[128,5,8,128]{3,2,1,0:T(8,128)(2,1)S(1)}, u32[]{:S(2)}, u32[]{:S(2)}) async-start(bf16[128,5,8,128]{3,2,1,0:T(8,128)(2,1)} %route.1), calls=%async_computation | async-start | bytes 2621440 | tf_op jit(solution)/shard_map/all_to_all | solution.py:602
  26.3 0.9 copy.5
  27.1 1.1 %reshape.10 = bf16[11,2,2,2,64,64]{5,4,2,1,0,3:T(8,128)(2,1)S(1)} reshape(bf16[11,2,2,2,4096]{4,2,1,0,3:T(2,128)(2,1)S(1)} %copy.5) | data formatting | bytes 1441792 | tf_op jit(solution)/shard_map/reshape | solution.py:588
  28.3 0.1 fusion
  28.4 0.1 slice_bitcast_fusion
  28.5 0.7 copy-done.10
  29.3 0.8 maximum_maximum_fusion
  30.3 1.7 %phases.1 = (f32[8,16,8,128]{3,2,1,0:T(8,128)S(1)}, f32[8,16,8,128]{3,2,1,0:T(8,128)S(1)}, f32[2,2,16,8,128]{4,3,2,1,0:T(8,128)S(1)}, f32[2,2,16,8,128]{4,3,2,1,...) custom-call(s32[3]{0:T(128)S(1)} %pad_add_fusion.where_ref.after_ref), custom_call_target="tpu_custom_call" | custom-call | flops 2000000000 | tf_op jit(solution)/shard_map/phases/pallas_call | solution.py:257
  32.0 0.7 copy-done
  32.7 0.7 copy-done.2
  33.4 0.7 copy-done.4
  34.1 0.7 copy-done.6
  34.7 0.6 copy-done.8
  35.3 12.2 %all-to-all-done.got_ref = bf16[128,5,8,128]{3,2,1,0:T(8,128)(2,1)S(1)} async-done(((bf16[128,5,8,128]{3,2,1,0:T(8,128)(2,1)}), bf16[128,5,8,128]{3,2,1,0:T(8,128)(2,1)S(1)}, u32[]{:S(2)}, u32[]{:S(2)}) %all-to-all-start) | async-done | bytes 1310752 | tf_op jit(solution)/shard_map/all_to_all | solution.py:602
  47.6 17.8 %leaves.1.leaf_ref = f32[2,2048,128]{2,1,0:T(8,128)S(1)} custom-call(bf16[128,5,8,128]{3,2,1,0:T(8,128)(2,1)S(1)} %all-to-all-done.got_ref), custom_call_target="tpu_custom_call" | custom-call | flops 19000000512 | tf_op jit(solution)/shard_map/leaves/pallas_call | solution.py:362
  65.5 4.7 %inner.1 = (bf16[2,2,2,256,128]{4,3,2,1,0:T(8,128)(2,1)S(1)}, bf16[2,2,2,256,128]{4,3,2,1,0:T(8,128)(2,1)S(1)}) custom-call(f32[2,2048,128]{2,1,0:T(8,128)S(1)} %leaves.1.leaf_ref, bf16[9,2,2,128,128]{4,3,2,1,0:T(8,128)(2,1)S(1)} %slice.18.mats_ref, f32[8,16,8,128]{3,2,1,0:T(8,128)S(1)} %get-tuple-element.23.level_c, ...), custom_call_target="tpu_custom_call" | custom-call | flops 5000000000 | tf_op jit(solution)/shard_map/inner/pallas_call | solution.py:498
  70.2 1.3 %collective-permute-start = (bf16[2,2,2,256,128]{4,3,2,1,0:T(8,128)(2,1)S(1)}, bf16[2,2,2,256,128]{4,3,2,1,0:T(8,128)(2,1)S(1)}, u32[]{:S(2)}, u32[]{:S(2)}) collective-permute-start(bf16[2,2,2,256,128]{4,3,2,1,0:T(8,128)(2,1)S(1)} %get-tuple-element.27.mine_ref), channel_id=1, source_target_pairs={{0,1},{1,0},{2,3},{3,2},{4,5},{5,4},{6,7},{7,6},{8,9},{9,8},{10,11... | collective-permute-start | bytes 1572872 | tf_op jit(solution)/shard_map/ppermute | solution.py:612
  71.6 0.2 maximum_maximum_fusion.1.mats_ref
  71.8 1.3 %collective-permute-done.other_ref = bf16[2,2,2,256,128]{4,3,2,1,0:T(8,128)(2,1)S(1)} collective-permute-done((bf16[2,2,2,256,128]{4,3,2,1,0:T(8,128)(2,1)S(1)}, bf16[2,2,2,256,128]{4,3,2,1,0:T(8,128)(2,1)S(1)}, u32[]{:S(2)}, u32[]{:S(2)}) %collective-permute-start) | collective-permute-done | bytes 524320 | tf_op jit(solution)/shard_map/ppermute | solution.py:612
  73.0 1.7 %outer.2 = (bf16[2,256,128]{2,1,0:T(8,128)(2,1)S(1)}, bf16[2,256,128]{2,1,0:T(8,128)(2,1)S(1)}, bf16[2,256,128]{2,1,0:T(8,128)(2,1)S(1)}, bf16[2,256,128]{2,1,0:T(8,128)(2,1)S(1)}) custom-call(s32[3]{0:T(128)S(1)} %pad_add_fusion.where_ref.after_ref, bf16[2,2,2,256,128]{4,3,2,1,0:T(8,128)(2,1)S(1)} %get-tuple-element.27.mine_ref, ...), custom_call_target="tpu_custom_call" | custom-call | flops 3000000000 | tf_op jit(solution)/shard_map/outer/pallas_call | solution.py:545
  74.9 1.6 %collective-permute-start.2 = (bf16[2,256,128]{2,1,0:T(8,128)(2,1)S(1)}, bf16[2,256,128]{2,1,0:T(8,128)(2,1)S(1)}, u32[]{:S(2)}, u32[]{:S(2)}) collective-permute-start(bf16[2,256,128]{2,1,0:T(8,128)(2,1)S(1)} %get-tuple-element.34), channel_id=1, source_target_pairs={{0,32},{16,48},{32,0},{48,16},{64,96},{80,112},{96,64},{112,80},{1... | collective-permute-start | bytes 393224 | tf_op jit(solution)/shard_map/ppermute | solution.py:618
  76.5 1.2 %collective-permute-start.3 = (bf16[2,256,128]{2,1,0:T(8,128)(2,1)S(1)}, bf16[2,256,128]{2,1,0:T(8,128)(2,1)S(1)}, u32[]{:S(2)}, u32[]{:S(2)}) collective-permute-start(bf16[2,256,128]{2,1,0:T(8,128)(2,1)S(1)} %get-tuple-element.35), channel_id=1, source_target_pairs={{0,48},{16,0},{32,16},{48,32},{64,112},{80,64},{96,80},{112,96},{1... | collective-permute-start | bytes 393224 | tf_op jit(solution)/shard_map/ppermute | solution.py:618
  77.7 1.7 %outer.3 = (bf16[2,256,128]{2,1,0:T(8,128)(2,1)S(1)}, bf16[2,256,128]{2,1,0:T(8,128)(2,1)S(1)}, bf16[2,256,128]{2,1,0:T(8,128)(2,1)S(1)}, bf16[2,256,128]{2,1,0:T(8,128)(2,1)S(1)}) custom-call(s32[3]{0:T(128)S(1)} %pad_add_fusion.where_ref.after_ref, bf16[2,2,2,256,128]{4,3,2,1,0:T(8,128)(2,1)S(1)} %get-tuple-element.36.mine_ref, ...), custom_call_target="tpu_custom_call" | custom-call | flops 3000000000 | tf_op jit(solution)/shard_map/outer/pallas_call | solution.py:545
  79.4 0.5 collective-permute-start.5
  79.9 1.9 %collective-permute-start.6 = (bf16[2,256,128]{2,1,0:T(8,128)(2,1)S(1)}, bf16[2,256,128]{2,1,0:T(8,128)(2,1)S(1)}, u32[]{:S(2)}, u32[]{:S(2)}) collective-permute-start(bf16[2,256,128]{2,1,0:T(8,128)(2,1)S(1)} %get-tuple-element.39), channel_id=1, source_target_pairs={{0,32},{16,48},{32,0},{48,16},{64,96},{80,112},{96,64},{112,80},{1... | collective-permute-start | bytes 393224 | tf_op jit(solution)/shard_map/ppermute | solution.py:618
  81.8 1.6 %collective-permute-done.1.refs_1_ = bf16[2,256,128]{2,1,0:T(8,128)(2,1)S(1)} collective-permute-done((bf16[2,256,128]{2,1,0:T(8,128)(2,1)S(1)}, bf16[2,256,128]{2,1,0:T(8,128)(2,1)S(1)}, u32[]{:S(2)}, u32[]{:S(2)}) %collective-permute-start.1) | collective-permute-done | bytes 131104 | tf_op jit(solution)/shard_map/ppermute | solution.py:618
  83.4 0.4 collective-permute-start.7
  83.8 0.1 collective-permute-done.3.refs_3_
  83.9 5.4 %collective-permute-done.5.refs_5_ = bf16[2,256,128]{2,1,0:T(8,128)(2,1)S(1)} collective-permute-done((bf16[2,256,128]{2,1,0:T(8,128)(2,1)S(1)}, bf16[2,256,128]{2,1,0:T(8,128)(2,1)S(1)}, u32[]{:S(2)}, u32[]{:S(2)}) %collective-permute-start.5) | collective-permute-done | bytes 131104 | tf_op jit(solution)/shard_map/ppermute | solution.py:618
  89.3 0.4 collective-permute-done.7.refs_7_
  89.7 2.4 %finish.1 = bf16[128,4096]{1,0:T(8,128)(2,1)} custom-call(s32[3]{0:T(128)S(1)} %pad_add_fusion.where_ref.after_ref, bf16[2,256,128]{2,1,0:T(8,128)(2,1)S(1)} %get-tuple-element.32.after_ref.refs_0_, bf16[2,256,128]{2,1,0:T(8,128)(2,1)S(1)} %collective-permute-done.1.refs_1_, bf16[2,256,128]{2,1,0:T(8,128)(2,1)S(1)} %collective-permute-done.2.refs_2_, ...), custom_call_target="tpu_custom_call" | custom-call | flops 3000000000 | tf_op jit(solution)/shard_map/finish/pallas_call | solution.py:575
  (35 shorter events, 0.4 us)
Async XLA Ops:
  14.7 11.5 %copy-start.16 = (bf16[11,2,2,2,4096]{4,3,2,1,0:T(2,128)(2,1)S(1)}, bf16[11,2,2,2,4096]{4,3,2,1,0:T(2,128)(2,1)}, u32[]{:S(2)}) copy-start(bf16[11,2,2,2,4096]{4,3,2,1,0:T(2,128)(2,1)} %param.7) | copy-start | bytes 2162692
  14.7 32.8 %all-to-all-start = ((bf16[128,5,8,128]{3,2,1,0:T(8,128)(2,1)}), bf16[128,5,8,128]{3,2,1,0:T(8,128)(2,1)S(1)}, u32[]{:S(2)}, u32[]{:S(2)}) async-start(bf16[128,5,8,128]{3,2,1,0:T(8,128)(2,1)} %route.1), calls=%async_computation | async-start | bytes 2621440 | tf_op jit(solution)/shard_map/all_to_all | solution.py:602
  28.4 0.9 copy-start.10
  28.5 1.6 %copy-start.12 = (bf16[11,2,2,64,64]{4,3,2,1,0:T(8,128)(2,1)}, bf16[11,2,2,64,64]{4,3,2,1,0:T(8,128)(2,1)S(1)}, u32[]{:S(2)}) copy-start(bf16[11,2,2,64,64]{4,3,2,1,0:T(8,128)(2,1)S(1)} %get-tuple-element.41) | copy-start | bytes 1081348
  28.5 1.6 %copy-start.14 = (bf16[11,2,2,64,64]{4,3,2,1,0:T(8,128)(2,1)}, bf16[11,2,2,64,64]{4,3,2,1,0:T(8,128)(2,1)S(1)}, u32[]{:S(2)}) copy-start(bf16[11,2,2,64,64]{4,3,2,1,0:T(8,128)(2,1)S(1)} %get-tuple-element.42) | copy-start | bytes 1081348
  32.0 0.7 copy-start
  32.7 0.7 copy-start.2
  33.4 0.7 copy-start.4
  34.1 0.7 copy-start.6
  34.7 0.6 copy-start.8
  47.6 17.8 %copy-start.5 = (f32[2,2,16,8,128]{4,3,2,1,0:T(8,128)S(1)}, f32[2,2,16,8,128]{4,3,2,1,0:T(8,128)}, u32[]{:S(2)}) copy-start(f32[2,2,16,8,128]{4,3,2,1,0:T(8,128)} %copy-done.4) | copy-start | bytes 786436
  47.6 17.8 %copy-start.7 = (f32[2,2,16,8,128]{4,3,2,1,0:T(8,128)S(1)}, f32[2,2,16,8,128]{4,3,2,1,0:T(8,128)}, u32[]{:S(2)}) copy-start(f32[2,2,16,8,128]{4,3,2,1,0:T(8,128)} %copy-done.6) | copy-start | bytes 786436
  65.4 6.2 %copy-start.11 = (bf16[11,2,2,64,64]{4,3,2,1,0:T(8,128)(2,1)S(1)}, bf16[11,2,2,64,64]{4,3,2,1,0:T(8,128)(2,1)}, u32[]{:S(2)}) copy-start(bf16[11,2,2,64,64]{4,3,2,1,0:T(8,128)(2,1)} %copy-done.10) | copy-start | bytes 1081348
  65.4 6.2 %copy-start.13 = (bf16[11,2,2,64,64]{4,3,2,1,0:T(8,128)(2,1)S(1)}, bf16[11,2,2,64,64]{4,3,2,1,0:T(8,128)(2,1)}, u32[]{:S(2)}) copy-start(bf16[11,2,2,64,64]{4,3,2,1,0:T(8,128)(2,1)} %copy-done.12) | copy-start | bytes 1081348
  65.4 6.2 %copy-start.15 = (bf16[11,2,2,64,64]{4,3,2,1,0:T(8,128)(2,1)S(1)}, bf16[11,2,2,64,64]{4,3,2,1,0:T(8,128)(2,1)}, u32[]{:S(2)}) copy-start(bf16[11,2,2,64,64]{4,3,2,1,0:T(8,128)(2,1)} %copy-done.14) | copy-start | bytes 1081348
  70.2 2.8 %copy-start.1 = (f32[2,2,16,8,128]{4,3,2,1,0:T(8,128)S(1)}, f32[2,2,16,8,128]{4,3,2,1,0:T(8,128)}, u32[]{:S(2)}) copy-start(f32[2,2,16,8,128]{4,3,2,1,0:T(8,128)} %copy-done) | copy-start | bytes 786436
  70.2 2.8 %copy-start.3 = (f32[2,2,16,8,128]{4,3,2,1,0:T(8,128)S(1)}, f32[2,2,16,8,128]{4,3,2,1,0:T(8,128)}, u32[]{:S(2)}) copy-start(f32[2,2,16,8,128]{4,3,2,1,0:T(8,128)} %copy-done.2) | copy-start | bytes 786436
  70.2 2.8 %copy-start.9 = (f32[16,128]{1,0:T(8,128)S(1)}, f32[16,128]{1,0:T(8,128)}, u32[]{:S(2)}) copy-start(f32[16,128]{1,0:T(8,128)} %copy-done.8) | copy-start | bytes 24580
  70.2 2.8 %collective-permute-start = (bf16[2,2,2,256,128]{4,3,2,1,0:T(8,128)(2,1)S(1)}, bf16[2,2,2,256,128]{4,3,2,1,0:T(8,128)(2,1)S(1)}, u32[]{:S(2)}, u32[]{:S(2)}) collective-permute-start(bf16[2,2,2,256,128]{4,3,2,1,0:T(8,128)(2,1)S(1)} %get-tuple-element.27.mine_ref), channel_id=1, source_target_pairs={{0,1},{1,0},{2,3},{3,2},{4,5},{5,4},{6,7},{7,6},{8,9},{9,8},{10,11... | collective-permute-start | bytes 1572872 | tf_op jit(solution)/shard_map/ppermute | solution.py:612
  71.5 6.2 %collective-permute-start.4 = (bf16[2,2,2,256,128]{4,3,2,1,0:T(8,128)(2,1)S(1)}, bf16[2,2,2,256,128]{4,3,2,1,0:T(8,128)(2,1)S(1)}, u32[]{:S(2)}, u32[]{:S(2)}) collective-permute-start(bf16[2,2,2,256,128]{4,3,2,1,0:T(8,128)(2,1)S(1)} %get-tuple-element.36.mine_ref), channel_id=1, source_target_pairs={{0,1},{1,0},{2,3},{3,2},{4,5},{5,4},{6,7},{7,6},{8,9},{9,8},{10,11... | collective-permute-start | bytes 1572872 | tf_op jit(solution)/shard_map/ppermute | solution.py:612
  74.8 8.6 %collective-permute-start.1 = (bf16[2,256,128]{2,1,0:T(8,128)(2,1)S(1)}, bf16[2,256,128]{2,1,0:T(8,128)(2,1)S(1)}, u32[]{:S(2)}, u32[]{:S(2)}) collective-permute-start(bf16[2,256,128]{2,1,0:T(8,128)(2,1)S(1)} %get-tuple-element.33), channel_id=1, source_target_pairs={{0,16},{16,32},{32,48},{48,0},{64,80},{80,96},{96,112},{112,64},{1... | collective-permute-start | bytes 393224 | tf_op jit(solution)/shard_map/ppermute | solution.py:618
  74.9 8.9 %collective-permute-start.2 = (bf16[2,256,128]{2,1,0:T(8,128)(2,1)S(1)}, bf16[2,256,128]{2,1,0:T(8,128)(2,1)S(1)}, u32[]{:S(2)}, u32[]{:S(2)}) collective-permute-start(bf16[2,256,128]{2,1,0:T(8,128)(2,1)S(1)} %get-tuple-element.34), channel_id=1, source_target_pairs={{0,32},{16,48},{32,0},{48,16},{64,96},{80,112},{96,64},{112,80},{1... | collective-permute-start | bytes 393224 | tf_op jit(solution)/shard_map/ppermute | solution.py:618
  76.5 7.4 %collective-permute-start.3 = (bf16[2,256,128]{2,1,0:T(8,128)(2,1)S(1)}, bf16[2,256,128]{2,1,0:T(8,128)(2,1)S(1)}, u32[]{:S(2)}, u32[]{:S(2)}) collective-permute-start(bf16[2,256,128]{2,1,0:T(8,128)(2,1)S(1)} %get-tuple-element.35), channel_id=1, source_target_pairs={{0,48},{16,0},{32,16},{48,32},{64,112},{80,64},{96,80},{112,96},{1... | collective-permute-start | bytes 393224 | tf_op jit(solution)/shard_map/ppermute | solution.py:618
  79.4 9.8 %collective-permute-start.5 = (bf16[2,256,128]{2,1,0:T(8,128)(2,1)S(1)}, bf16[2,256,128]{2,1,0:T(8,128)(2,1)S(1)}, u32[]{:S(2)}, u32[]{:S(2)}) collective-permute-start(bf16[2,256,128]{2,1,0:T(8,128)(2,1)S(1)} %get-tuple-element.38), channel_id=1, source_target_pairs={{0,16},{16,32},{32,48},{48,0},{64,80},{80,96},{96,112},{112,64},{1... | collective-permute-start | bytes 393224 | tf_op jit(solution)/shard_map/ppermute | solution.py:618
  79.9 9.3 %collective-permute-start.6 = (bf16[2,256,128]{2,1,0:T(8,128)(2,1)S(1)}, bf16[2,256,128]{2,1,0:T(8,128)(2,1)S(1)}, u32[]{:S(2)}, u32[]{:S(2)}) collective-permute-start(bf16[2,256,128]{2,1,0:T(8,128)(2,1)S(1)} %get-tuple-element.39), channel_id=1, source_target_pairs={{0,32},{16,48},{32,0},{48,16},{64,96},{80,112},{96,64},{112,80},{1... | collective-permute-start | bytes 393224 | tf_op jit(solution)/shard_map/ppermute | solution.py:618
  83.4 6.3 %collective-permute-start.7 = (bf16[2,256,128]{2,1,0:T(8,128)(2,1)S(1)}, bf16[2,256,128]{2,1,0:T(8,128)(2,1)S(1)}, u32[]{:S(2)}, u32[]{:S(2)}) collective-permute-start(bf16[2,256,128]{2,1,0:T(8,128)(2,1)S(1)} %get-tuple-element.40), channel_id=1, source_target_pairs={{0,48},{16,0},{32,16},{48,32},{64,112},{80,64},{96,80},{112,96},{1... | collective-permute-start | bytes 393224 | tf_op jit(solution)/shard_map/ppermute | solution.py:618

commit v6 on v5

--- a/solution.py
+++ b/solution.py
@@ -23,7 +23,7 @@
 BLOCK = 256
 HALF = 2
 RANK_UNROLL = 8
-ROUTE_UNROLL = 8
+ROUTE_UNROLL = 32
 
 
 def matmul_nt(lhs, rhs):
@@ -557,17 +557,41 @@
 
 
 def finish_kernel(where_ref, *refs):
-    got, out_ref, held = refs[:8], refs[8], refs[9]
+    got, out_ref, held, sems = refs[:8], *refs[8:]
     own = where_ref[2]
-    for half in range(2):
-        for shift in range(4):
-            group = (own - shift) & 3
-            for h in range(HALF):
-                row = group * 4 + (half * HALF + h)
-                held[pl.ds(row, 256, stride=16), :] = got[half * 4 + shift][h].astype(F32)
-    for block in range(32):
-        span = slice(block * 128, (block + 1) * 128)
-        out_ref[:, span] = held[span].astype(BF16).T
+    row = iota((256, 256), 1)
+    place = row >> 4
+    group = (own - (place >> 1)) & 3
+    target = (row & 15) * 16 + group * 4 + (place >> 3) * HALF + (place & 1)
+    order = jnp.where(iota((256, 256), 0) == target, 1.0, 0.0).astype(BF16)
+
+    def run(*accs):
+        for number, acc in enumerate(accs):
+            blocks = []
+            for block in (2 * number, 2 * number + 1):
+                span = slice(block * 16, block * 16 + 16)
+                pieces = [got[at // 2][at % 2, span] for at in range(16)]
+                blocks.append(jnp.concatenate(pieces, axis=0))
+            m, register = number % 2, number // 2 % 2
+            pltpu.matmul_push_rhs(jnp.concatenate(blocks, axis=1), register, m)
+            pltpu.matmul_acc_lhs(acc, order, load_staged_rhs=register)
+        for number, acc in enumerate(accs):
+            made = pltpu.matmul_pop(acc).astype(BF16)
+            for side in range(2):
+                start = (2 * number + side) * 256
+                held[:, start : start + 256] = made[:, side * 128 : side * 128 + 128].T
+            if number % 2 == 1:
+                copies[number // 2].start()
+
+    copies = []
+    for number in range(4):
+        span = pl.ds(number * 1024, 1024)
+        copies.append(
+            pltpu.make_async_copy(held.at[:, span], out_ref.at[:, span], sems.at[number])
+        )
+    pl.run_scoped(run, *[pltpu.ACC(number % 2)((256, 256), F32) for number in range(8)])
+    for copy in copies:
+        copy.wait()
 
 
 def finish(where, got):
@@ -575,9 +599,9 @@
     return pl.pallas_call(
         finish_kernel,
         in_specs=[pl.BlockSpec(memory_space=pltpu.SMEM)] + [vmem] * 8,
-        out_specs=vmem,
+        out_specs=pl.BlockSpec(memory_space=pltpu.HBM),
         out_shape=jax.ShapeDtypeStruct((128, 4096), BF16),
-        scratch_shapes=[pltpu.VMEM((4096, 128), F32)],
+        scratch_shapes=[pltpu.VMEM((128, 4096), BF16), pltpu.SemaphoreType.DMA((4,))],
         compiler_params=pltpu.CompilerParams(vmem_limit_bytes=40 * MIB),
         cost_estimate=cost(3),
         name="finish",

time: 92.3 us -> 91.2 us (0.988)
  Pallas kernels: 44.9 us -> 43.6 us
where the time goes in v6:
time: 91.2 us; the launch traced here: 91 us
  Pallas kernels  43.6 us (48%)
  waiting for transfers between devices  21 us (23%)
  starting transfers between devices  18.6 us (20%)
  local copies, waits for them, and re-layouts  6.31 us (7%)
  other arithmetic  1.13 us (1%)
    pallas_call x1, Pallas kernels, leaves(): pl.pallas_call(leaves_kernel, in_specs=[vmem], out_specs=vmem, out_shape=...  17.8 us
    pallas_call x1, Pallas kernels, route(): pl.pallas_call(route_kernel, in_specs=[pl.BlockSpec(memory_space=pltpu.HB...  14 us
    all_to_all x1, waiting for transfers between devices, body(): lax.all_to_all(send, ('gx', 'gy'), split_axis=0, concat_axis=0, tiled=True)  12.2 us
    all_to_all x1, starting transfers between devices, body(): lax.all_to_all(send, ('gx', 'gy'), split_axis=0, concat_axis=0, tiled=True)  11.5 us
    ppermute x6, waiting for transfers between devices, body(): got.append(lax.ppermute(outs[shift], 'gx', pairs))  7.45 us
    ppermute x6, starting transfers between devices, body(): got.append(lax.ppermute(outs[shift], 'gx', pairs))  5.69 us
    unnamed x35, local copies, waits for them, and re-layouts  4.98 us
    pallas_call x1, Pallas kernels, inner(): pl.pallas_call(inner_kernel, in_specs=[vmem] * 6, out_specs=[vmem] * 2, o...  4.71 us
  transfers between devices with their start and end apart: 9, of which 6 were waited for; matrix products, arithmetic and copies ran while one was open for 4% of the time, Pallas kernels for 6%

profile of v6, /device:TPU:1, one launch (start us, length us, event | category | flops | bytes accessed | tf_op | source)
XLA Modules:
  0.0 91.0 jit_solution(8277361138738709114)
XLA Ops:
  0.0 14.0 %route.1 = bf16[128,5,8,128]{3,2,1,0:T(8,128)(2,1)} custom-call(s32[1,8192]{1,0:T(1,128)} %bitcast.13, s32[2,8192]{1,0:T(2,128)} %point_hbm.1, bf16[32,8192]{1,0:T(8,128)(2,1)} %value_hbm.1), custom_call_target="tpu_custom_call" | custom-call | flops 15000000512 | tf_op jit(solution)/shard_map/route/pallas_call | solution.py:193
  14.0 11.5 %all-to-all-start = ((bf16[128,5,8,128]{3,2,1,0:T(8,128)(2,1)}), bf16[128,5,8,128]{3,2,1,0:T(8,128)(2,1)S(1)}, u32[]{:S(2)}, u32[]{:S(2)}) async-start(bf16[128,5,8,128]{3,2,1,0:T(8,128)(2,1)} %route.1), calls=%async_computation | async-start | bytes 2621440 | tf_op jit(solution)/shard_map/all_to_all | solution.py:626
  25.5 0.9 copy.5
  26.4 1.1 %reshape.10 = bf16[11,2,2,2,64,64]{5,4,2,1,0,3:T(8,128)(2,1)S(1)} reshape(bf16[11,2,2,2,4096]{4,2,1,0,3:T(2,128)(2,1)S(1)} %copy.5) | data formatting | bytes 1441792 | tf_op jit(solution)/shard_map/reshape | solution.py:612
  27.5 0.1 fusion
  27.7 0.1 slice_bitcast_fusion
  27.8 0.7 copy-done.10
  28.5 0.8 maximum_maximum_fusion
  29.5 1.7 %phases.1 = (f32[8,16,8,128]{3,2,1,0:T(8,128)S(1)}, f32[8,16,8,128]{3,2,1,0:T(8,128)S(1)}, f32[2,2,16,8,128]{4,3,2,1,0:T(8,128)S(1)}, f32[2,2,16,8,128]{4,3,2,1,...) custom-call(s32[3]{0:T(128)S(1)} %pad_add_fusion.where_ref.after_ref), custom_call_target="tpu_custom_call" | custom-call | flops 2000000000 | tf_op jit(solution)/shard_map/phases/pallas_call | solution.py:257
  31.3 0.7 copy-done
  31.9 0.7 copy-done.2
  32.6 0.7 copy-done.4
  33.3 0.7 copy-done.6
  34.0 0.6 copy-done.8
  34.6 12.2 %all-to-all-done.got_ref = bf16[128,5,8,128]{3,2,1,0:T(8,128)(2,1)S(1)} async-done(((bf16[128,5,8,128]{3,2,1,0:T(8,128)(2,1)}), bf16[128,5,8,128]{3,2,1,0:T(8,128)(2,1)S(1)}, u32[]{:S(2)}, u32[]{:S(2)}) %all-to-all-start) | async-done | bytes 1310752 | tf_op jit(solution)/shard_map/all_to_all | solution.py:626
  46.8 17.8 %leaves.1.leaf_ref = f32[2,2048,128]{2,1,0:T(8,128)S(1)} custom-call(bf16[128,5,8,128]{3,2,1,0:T(8,128)(2,1)S(1)} %all-to-all-done.got_ref), custom_call_target="tpu_custom_call" | custom-call | flops 19000000512 | tf_op jit(solution)/shard_map/leaves/pallas_call | solution.py:362
  64.7 4.7 %inner.1 = (bf16[2,2,2,256,128]{4,3,2,1,0:T(8,128)(2,1)S(1)}, bf16[2,2,2,256,128]{4,3,2,1,0:T(8,128)(2,1)S(1)}) custom-call(f32[2,2048,128]{2,1,0:T(8,128)S(1)} %leaves.1.leaf_ref, bf16[9,2,2,128,128]{4,3,2,1,0:T(8,128)(2,1)S(1)} %slice.18.mats_ref, f32[8,16,8,128]{3,2,1,0:T(8,128)S(1)} %get-tuple-element.23.level_c, ...), custom_call_target="tpu_custom_call" | custom-call | flops 5000000000 | tf_op jit(solution)/shard_map/inner/pallas_call | solution.py:498
  69.5 1.3 %collective-permute-start = (bf16[2,2,2,256,128]{4,3,2,1,0:T(8,128)(2,1)S(1)}, bf16[2,2,2,256,128]{4,3,2,1,0:T(8,128)(2,1)S(1)}, u32[]{:S(2)}, u32[]{:S(2)}) collective-permute-start(bf16[2,2,2,256,128]{4,3,2,1,0:T(8,128)(2,1)S(1)} %get-tuple-element.27.mine_ref), channel_id=1, source_target_pairs={{0,1},{1,0},{2,3},{3,2},{4,5},{5,4},{6,7},{7,6},{8,9},{9,8},{10,11... | collective-permute-start | bytes 1572872 | tf_op jit(solution)/shard_map/ppermute | solution.py:636
  70.9 0.2 maximum_maximum_fusion.1.mats_ref
  71.0 1.3 %collective-permute-done.other_ref = bf16[2,2,2,256,128]{4,3,2,1,0:T(8,128)(2,1)S(1)} collective-permute-done((bf16[2,2,2,256,128]{4,3,2,1,0:T(8,128)(2,1)S(1)}, bf16[2,2,2,256,128]{4,3,2,1,0:T(8,128)(2,1)S(1)}, u32[]{:S(2)}, u32[]{:S(2)}) %collective-permute-start) | collective-permute-done | bytes 524320 | tf_op jit(solution)/shard_map/ppermute | solution.py:636
  72.3 1.7 %outer.2 = (bf16[2,256,128]{2,1,0:T(8,128)(2,1)S(1)}, bf16[2,256,128]{2,1,0:T(8,128)(2,1)S(1)}, bf16[2,256,128]{2,1,0:T(8,128)(2,1)S(1)}, bf16[2,256,128]{2,1,0:T(8,128)(2,1)S(1)}) custom-call(s32[3]{0:T(128)S(1)} %pad_add_fusion.where_ref.after_ref, bf16[2,2,2,256,128]{4,3,2,1,0:T(8,128)(2,1)S(1)} %get-tuple-element.27.mine_ref, ...), custom_call_target="tpu_custom_call" | custom-call | flops 3000000000 | tf_op jit(solution)/shard_map/outer/pallas_call | solution.py:545
  74.1 1.6 %collective-permute-start.2 = (bf16[2,256,128]{2,1,0:T(8,128)(2,1)S(1)}, bf16[2,256,128]{2,1,0:T(8,128)(2,1)S(1)}, u32[]{:S(2)}, u32[]{:S(2)}) collective-permute-start(bf16[2,256,128]{2,1,0:T(8,128)(2,1)S(1)} %get-tuple-element.34), channel_id=1, source_target_pairs={{0,32},{16,48},{32,0},{48,16},{64,96},{80,112},{96,64},{112,80},{1... | collective-permute-start | bytes 393224 | tf_op jit(solution)/shard_map/ppermute | solution.py:642
  75.7 1.2 %collective-permute-start.3 = (bf16[2,256,128]{2,1,0:T(8,128)(2,1)S(1)}, bf16[2,256,128]{2,1,0:T(8,128)(2,1)S(1)}, u32[]{:S(2)}, u32[]{:S(2)}) collective-permute-start(bf16[2,256,128]{2,1,0:T(8,128)(2,1)S(1)} %get-tuple-element.35), channel_id=1, source_target_pairs={{0,48},{16,0},{32,16},{48,32},{64,112},{80,64},{96,80},{112,96},{1... | collective-permute-start | bytes 393224 | tf_op jit(solution)/shard_map/ppermute | solution.py:642
  77.0 1.7 %outer.3 = (bf16[2,256,128]{2,1,0:T(8,128)(2,1)S(1)}, bf16[2,256,128]{2,1,0:T(8,128)(2,1)S(1)}, bf16[2,256,128]{2,1,0:T(8,128)(2,1)S(1)}, bf16[2,256,128]{2,1,0:T(8,128)(2,1)S(1)}) custom-call(s32[3]{0:T(128)S(1)} %pad_add_fusion.where_ref.after_ref, bf16[2,2,2,256,128]{4,3,2,1,0:T(8,128)(2,1)S(1)} %get-tuple-element.36.mine_ref, ...), custom_call_target="tpu_custom_call" | custom-call | flops 3000000000 | tf_op jit(solution)/shard_map/outer/pallas_call | solution.py:545
  78.7 0.5 collective-permute-start.5
  79.2 1.9 %collective-permute-start.6 = (bf16[2,256,128]{2,1,0:T(8,128)(2,1)S(1)}, bf16[2,256,128]{2,1,0:T(8,128)(2,1)S(1)}, u32[]{:S(2)}, u32[]{:S(2)}) collective-permute-start(bf16[2,256,128]{2,1,0:T(8,128)(2,1)S(1)} %get-tuple-element.39), channel_id=1, source_target_pairs={{0,32},{16,48},{32,0},{48,16},{64,96},{80,112},{96,64},{112,80},{1... | collective-permute-start | bytes 393224 | tf_op jit(solution)/shard_map/ppermute | solution.py:642
  81.1 1.6 %collective-permute-done.1.refs_1_ = bf16[2,256,128]{2,1,0:T(8,128)(2,1)S(1)} collective-permute-done((bf16[2,256,128]{2,1,0:T(8,128)(2,1)S(1)}, bf16[2,256,128]{2,1,0:T(8,128)(2,1)S(1)}, u32[]{:S(2)}, u32[]{:S(2)}) %collective-permute-start.1) | collective-permute-done | bytes 131104 | tf_op jit(solution)/shard_map/ppermute | solution.py:642
  82.7 0.4 collective-permute-start.7
  83.1 0.1 collective-permute-done.3.refs_3_
  83.2 5.3 %collective-permute-done.5.refs_5_ = bf16[2,256,128]{2,1,0:T(8,128)(2,1)S(1)} collective-permute-done((bf16[2,256,128]{2,1,0:T(8,128)(2,1)S(1)}, bf16[2,256,128]{2,1,0:T(8,128)(2,1)S(1)}, u32[]{:S(2)}, u32[]{:S(2)}) %collective-permute-start.5) | collective-permute-done | bytes 131104 | tf_op jit(solution)/shard_map/ppermute | solution.py:642
  88.5 0.5 collective-permute-done.7.refs_7_
  88.9 1.9 %finish.1 = bf16[128,4096]{1,0:T(8,128)(2,1)} custom-call(s32[3]{0:T(128)S(1)} %pad_add_fusion.where_ref.after_ref, bf16[2,256,128]{2,1,0:T(8,128)(2,1)S(1)} %get-tuple-element.32.after_ref.refs_0_, bf16[2,256,128]{2,1,0:T(8,128)(2,1)S(1)} %collective-permute-done.1.refs_1_, bf16[2,256,128]{2,1,0:T(8,128)(2,1)S(1)} %collective-permute-done.2.refs_2_, ...), custom_call_target="tpu_custom_call" | custom-call | flops 3000000000 | tf_op jit(solution)/shard_map/finish/pallas_call | solution.py:599
  (35 shorter events, 0.4 us)
Async XLA Ops:
  14.0 11.5 %copy-start.16 = (bf16[11,2,2,2,4096]{4,3,2,1,0:T(2,128)(2,1)S(1)}, bf16[11,2,2,2,4096]{4,3,2,1,0:T(2,128)(2,1)}, u32[]{:S(2)}) copy-start(bf16[11,2,2,2,4096]{4,3,2,1,0:T(2,128)(2,1)} %param.7) | copy-start | bytes 2162692
  14.0 32.8 %all-to-all-start = ((bf16[128,5,8,128]{3,2,1,0:T(8,128)(2,1)}), bf16[128,5,8,128]{3,2,1,0:T(8,128)(2,1)S(1)}, u32[]{:S(2)}, u32[]{:S(2)}) async-start(bf16[128,5,8,128]{3,2,1,0:T(8,128)(2,1)} %route.1), calls=%async_computation | async-start | bytes 2621440 | tf_op jit(solution)/shard_map/all_to_all | solution.py:626
  27.6 0.9 copy-start.10
  27.8 1.6 %copy-start.12 = (bf16[11,2,2,64,64]{4,3,2,1,0:T(8,128)(2,1)}, bf16[11,2,2,64,64]{4,3,2,1,0:T(8,128)(2,1)S(1)}, u32[]{:S(2)}) copy-start(bf16[11,2,2,64,64]{4,3,2,1,0:T(8,128)(2,1)S(1)} %get-tuple-element.41) | copy-start | bytes 1081348
  27.8 1.6 %copy-start.14 = (bf16[11,2,2,64,64]{4,3,2,1,0:T(8,128)(2,1)}, bf16[11,2,2,64,64]{4,3,2,1,0:T(8,128)(2,1)S(1)}, u32[]{:S(2)}) copy-start(bf16[11,2,2,64,64]{4,3,2,1,0:T(8,128)(2,1)S(1)} %get-tuple-element.42) | copy-start | bytes 1081348
  31.2 0.7 copy-start
  31.9 0.7 copy-start.2
  32.6 0.7 copy-start.4
  33.3 0.7 copy-start.6
  34.0 0.6 copy-start.8
  46.8 17.8 %copy-start.5 = (f32[2,2,16,8,128]{4,3,2,1,0:T(8,128)S(1)}, f32[2,2,16,8,128]{4,3,2,1,0:T(8,128)}, u32[]{:S(2)}) copy-start(f32[2,2,16,8,128]{4,3,2,1,0:T(8,128)} %copy-done.4) | copy-start | bytes 786436
  46.8 17.8 %copy-start.7 = (f32[2,2,16,8,128]{4,3,2,1,0:T(8,128)S(1)}, f32[2,2,16,8,128]{4,3,2,1,0:T(8,128)}, u32[]{:S(2)}) copy-start(f32[2,2,16,8,128]{4,3,2,1,0:T(8,128)} %copy-done.6) | copy-start | bytes 786436
  64.7 6.2 %copy-start.11 = (bf16[11,2,2,64,64]{4,3,2,1,0:T(8,128)(2,1)S(1)}, bf16[11,2,2,64,64]{4,3,2,1,0:T(8,128)(2,1)}, u32[]{:S(2)}) copy-start(bf16[11,2,2,64,64]{4,3,2,1,0:T(8,128)(2,1)} %copy-done.10) | copy-start | bytes 1081348
  64.7 6.2 %copy-start.13 = (bf16[11,2,2,64,64]{4,3,2,1,0:T(8,128)(2,1)S(1)}, bf16[11,2,2,64,64]{4,3,2,1,0:T(8,128)(2,1)}, u32[]{:S(2)}) copy-start(bf16[11,2,2,64,64]{4,3,2,1,0:T(8,128)(2,1)} %copy-done.12) | copy-start | bytes 1081348
  64.7 6.2 %copy-start.15 = (bf16[11,2,2,64,64]{4,3,2,1,0:T(8,128)(2,1)S(1)}, bf16[11,2,2,64,64]{4,3,2,1,0:T(8,128)(2,1)}, u32[]{:S(2)}) copy-start(bf16[11,2,2,64,64]{4,3,2,1,0:T(8,128)(2,1)} %copy-done.14) | copy-start | bytes 1081348
  69.4 2.9 %copy-start.1 = (f32[2,2,16,8,128]{4,3,2,1,0:T(8,128)S(1)}, f32[2,2,16,8,128]{4,3,2,1,0:T(8,128)}, u32[]{:S(2)}) copy-start(f32[2,2,16,8,128]{4,3,2,1,0:T(8,128)} %copy-done) | copy-start | bytes 786436
  69.4 2.9 %copy-start.3 = (f32[2,2,16,8,128]{4,3,2,1,0:T(8,128)S(1)}, f32[2,2,16,8,128]{4,3,2,1,0:T(8,128)}, u32[]{:S(2)}) copy-start(f32[2,2,16,8,128]{4,3,2,1,0:T(8,128)} %copy-done.2) | copy-start | bytes 786436
  69.4 2.9 %copy-start.9 = (f32[16,128]{1,0:T(8,128)S(1)}, f32[16,128]{1,0:T(8,128)}, u32[]{:S(2)}) copy-start(f32[16,128]{1,0:T(8,128)} %copy-done.8) | copy-start | bytes 24580
  69.5 2.8 %collective-permute-start = (bf16[2,2,2,256,128]{4,3,2,1,0:T(8,128)(2,1)S(1)}, bf16[2,2,2,256,128]{4,3,2,1,0:T(8,128)(2,1)S(1)}, u32[]{:S(2)}, u32[]{:S(2)}) collective-permute-start(bf16[2,2,2,256,128]{4,3,2,1,0:T(8,128)(2,1)S(1)} %get-tuple-element.27.mine_ref), channel_id=1, source_target_pairs={{0,1},{1,0},{2,3},{3,2},{4,5},{5,4},{6,7},{7,6},{8,9},{9,8},{10,11... | collective-permute-start | bytes 1572872 | tf_op jit(solution)/shard_map/ppermute | solution.py:636
  70.8 6.2 %collective-permute-start.4 = (bf16[2,2,2,256,128]{4,3,2,1,0:T(8,128)(2,1)S(1)}, bf16[2,2,2,256,128]{4,3,2,1,0:T(8,128)(2,1)S(1)}, u32[]{:S(2)}, u32[]{:S(2)}) collective-permute-start(bf16[2,2,2,256,128]{4,3,2,1,0:T(8,128)(2,1)S(1)} %get-tuple-element.36.mine_ref), channel_id=1, source_target_pairs={{0,1},{1,0},{2,3},{3,2},{4,5},{5,4},{6,7},{7,6},{8,9},{9,8},{10,11... | collective-permute-start | bytes 1572872 | tf_op jit(solution)/shard_map/ppermute | solution.py:636
  74.0 8.6 %collective-permute-start.1 = (bf16[2,256,128]{2,1,0:T(8,128)(2,1)S(1)}, bf16[2,256,128]{2,1,0:T(8,128)(2,1)S(1)}, u32[]{:S(2)}, u32[]{:S(2)}) collective-permute-start(bf16[2,256,128]{2,1,0:T(8,128)(2,1)S(1)} %get-tuple-element.33), channel_id=1, source_target_pairs={{0,16},{16,32},{32,48},{48,0},{64,80},{80,96},{96,112},{112,64},{1... | collective-permute-start | bytes 393224 | tf_op jit(solution)/shard_map/ppermute | solution.py:642
  74.1 8.9 %collective-permute-start.2 = (bf16[2,256,128]{2,1,0:T(8,128)(2,1)S(1)}, bf16[2,256,128]{2,1,0:T(8,128)(2,1)S(1)}, u32[]{:S(2)}, u32[]{:S(2)}) collective-permute-start(bf16[2,256,128]{2,1,0:T(8,128)(2,1)S(1)} %get-tuple-element.34), channel_id=1, source_target_pairs={{0,32},{16,48},{32,0},{48,16},{64,96},{80,112},{96,64},{112,80},{1... | collective-permute-start | bytes 393224 | tf_op jit(solution)/shard_map/ppermute | solution.py:642
  75.7 7.4 %collective-permute-start.3 = (bf16[2,256,128]{2,1,0:T(8,128)(2,1)S(1)}, bf16[2,256,128]{2,1,0:T(8,128)(2,1)S(1)}, u32[]{:S(2)}, u32[]{:S(2)}) collective-permute-start(bf16[2,256,128]{2,1,0:T(8,128)(2,1)S(1)} %get-tuple-element.35), channel_id=1, source_target_pairs={{0,48},{16,0},{32,16},{48,32},{64,112},{80,64},{96,80},{112,96},{1... | collective-permute-start | bytes 393224 | tf_op jit(solution)/shard_map/ppermute | solution.py:642
  78.7 9.8 %collective-permute-start.5 = (bf16[2,256,128]{2,1,0:T(8,128)(2,1)S(1)}, bf16[2,256,128]{2,1,0:T(8,128)(2,1)S(1)}, u32[]{:S(2)}, u32[]{:S(2)}) collective-permute-start(bf16[2,256,128]{2,1,0:T(8,128)(2,1)S(1)} %get-tuple-element.38), channel_id=1, source_target_pairs={{0,16},{16,32},{32,48},{48,0},{64,80},{80,96},{96,112},{112,64},{1... | collective-permute-start | bytes 393224 | tf_op jit(solution)/shard_map/ppermute | solution.py:642
  79.2 9.3 %collective-permute-start.6 = (bf16[2,256,128]{2,1,0:T(8,128)(2,1)S(1)}, bf16[2,256,128]{2,1,0:T(8,128)(2,1)S(1)}, u32[]{:S(2)}, u32[]{:S(2)}) collective-permute-start(bf16[2,256,128]{2,1,0:T(8,128)(2,1)S(1)} %get-tuple-element.39), channel_id=1, source_target_pairs={{0,32},{16,48},{32,0},{48,16},{64,96},{80,112},{96,64},{112,80},{1... | collective-permute-start | bytes 393224 | tf_op jit(solution)/shard_map/ppermute | solution.py:642
  82.7 6.2 %collective-permute-start.7 = (bf16[2,256,128]{2,1,0:T(8,128)(2,1)S(1)}, bf16[2,256,128]{2,1,0:T(8,128)(2,1)S(1)}, u32[]{:S(2)}, u32[]{:S(2)}) collective-permute-start(bf16[2,256,128]{2,1,0:T(8,128)(2,1)S(1)} %get-tuple-element.40), channel_id=1, source_target_pairs={{0,48},{16,0},{32,16},{48,32},{64,112},{80,64},{96,80},{112,96},{1... | collective-permute-start | bytes 393224 | tf_op jit(solution)/shard_map/ppermute | solution.py:642

commit v7 on v6

--- a/solution.py
+++ b/solution.py
@@ -75,8 +75,7 @@
 
     def several(step, held):
         spans = [
-            pl.ds(pl.multiple_of((step * RANK_UNROLL + u) * width, width), width)
-            for u in range(RANK_UNROLL)
+            pl.ds((step * RANK_UNROLL + u) * width, width) for u in range(RANK_UNROLL)
         ]
         hits = []
         for u, span in enumerate(spans):
@@ -114,7 +113,9 @@
             rows_ref[1:2, span] = jnp.where(sibling < 2, -1.0, key)
         return held
 
-    lax.fori_loop(0, own_ref.shape[1] // width // RANK_UNROLL, several, start)
+    held = start
+    for step in range(own_ref.shape[1] // width // RANK_UNROLL):
+        held = several(step, held)
 
 
 def place_sources(high, rows_ref, charge_ref, hold, accs):
@@ -146,7 +147,7 @@
 
 
 def route_kernel(
-    own_hbm, point_hbm, value_hbm, send_ref, own, point, value, rows, charge, tri, hold, sems
+    own_hbm, point_hbm, value_hbm, send_hbm, own, point, value, rows, charge, tri, hold, send, sems
 ):
     copies = [
         pltpu.make_async_copy(source, target, sems.at[number])
@@ -164,36 +165,40 @@
         lambda *accs: rank_sources(own, point, value, rows, charge, tri, accs),
         *[pltpu.ACC(number % 2)((128, 256), F32) for number in range(2 * RANK_UNROLL)],
     )
+    halves = []
     for high in range(2):
         pl.run_scoped(
             lambda *accs, high=high: place_sources(high, rows, charge, hold, accs),
             *[pltpu.ACC(number)((544, 256), F32) for number in range(2)],
         )
-    for number in range(32):
-        high, low = number // 16, number % 16
-        first = high * 64 + low
-        for group in range(4):
-            at = low * 32 + group * 8
-            for y in range(4):
-                tile = hold[high, y // 2, at : at + 8, y % 2 * 128 : y % 2 * 128 + 128]
-                send_ref[first + group * 16, y] = tile.astype(BF16)
-        tile = [
-            hold[high, y // 2, pl.ds(512 + 16 * kind + low, 1), y % 2 * 128 : y % 2 * 128 + 128]
-            for kind in range(2)
-            for y in range(4)
-        ]
-        tile = jnp.concatenate(tile, axis=0).astype(BF16)
-        for group in range(4):
-            send_ref[first + group * 16, 4] = tile
+        for low in range(16):
+            first = high * 64 + low
+            for group in range(4):
+                at = low * 32 + group * 8
+                for y in range(4):
+                    tile = hold[high, y // 2, at : at + 8, y % 2 * 128 : y % 2 * 128 + 128]
+                    send[first + group * 16, y] = tile.astype(BF16)
+            tile = [
+                hold[high, y // 2, pl.ds(512 + 16 * kind + low, 1), y % 2 * 128 : y % 2 * 128 + 128]
+                for kind in range(2)
+                for y in range(4)
+            ]
+            tile = jnp.concatenate(tile, axis=0).astype(BF16)
+            for group in range(4):
+                send[first + group * 16, 4] = tile
+        span = pl.ds(high * 64, 64)
+        halves.append(pltpu.make_async_copy(send.at[span], send_hbm.at[span], sems.at[3 + high]))
+        halves[high].start()
+    for copy in halves:
+        copy.wait()
 
 
 def route(owner, point, value):
     sources = owner.shape[1]
-    vmem = pl.BlockSpec(memory_space=pltpu.VMEM)
     return pl.pallas_call(
         route_kernel,
         in_specs=[pl.BlockSpec(memory_space=pltpu.HBM)] * 3,
-        out_specs=vmem,
+        out_specs=pl.BlockSpec(memory_space=pltpu.HBM),
         out_shape=jax.ShapeDtypeStruct((128, 5, 8, 128), BF16),
         scratch_shapes=[
             pltpu.VMEM((1, sources), jnp.int32),
@@ -203,7 +208,8 @@
             pltpu.VMEM((32, sources), BF16),
             pltpu.VMEM((BLOCK, BLOCK), BF16),
             pltpu.VMEM((2, 2, 544, 256), F32),
-            pltpu.SemaphoreType.DMA((3,)),
+            pltpu.VMEM((128, 5, 8, 128), BF16),
+            pltpu.SemaphoreType.DMA((5,)),
         ],
         compiler_params=pltpu.CompilerParams(vmem_limit_bytes=60 * MIB),
         cost_estimate=cost(15),
@@ -636,10 +642,11 @@
         other = lax.ppermute(mine, "gy", cores)
         outs = outer(where, mine, other, outer_mats, tables, last)
         last = outs[0]
-        got.append(outs[0])
-        for shift in range(1, 4):
+        arrived = {0: outs[0]}
+        for shift in (2, 1, 3):
             pairs = [(i, i // 4 * 4 + (i + shift) % 4) for i in range(lax.axis_size("gx"))]
-            got.append(lax.ppermute(outs[shift], "gx", pairs))
+            arrived[shift] = lax.ppermute(outs[shift], "gx", pairs)
+        got += [arrived[shift] for shift in range(4)]
     return finish(where, got).reshape(128, 1, 1, 4096)
 
 

time: 91.2 us -> 90.1 us (0.988)
  Pallas kernels: 43.6 us -> 42.5 us
    pallas_call x1, Pallas kernels: 14 us -> 12.9 us  [route(): pl.pallas_call(route_kernel, in_specs=[pl.BlockSpec(memory_space=pltpu.HB...]
where the time goes in v7:
time: 90.1 us; the launch traced here: 89.9 us
  Pallas kernels  42.5 us (47%)
  waiting for transfers between devices  21 us (23%)
  starting transfers between devices  18.6 us (21%)
  local copies, waits for them, and re-layouts  6.31 us (7%)
  other arithmetic  1.13 us (1%)
    pallas_call x1, Pallas kernels, leaves(): pl.pallas_call(leaves_kernel, in_specs=[vmem], out_specs=vmem, out_shape=...  17.8 us
    pallas_call x1, Pallas kernels, route(): pl.pallas_call(route_kernel, in_specs=[pl.BlockSpec(memory_space=pltpu.HB...  12.9 us
    all_to_all x1, waiting for transfers between devices, body(): lax.all_to_all(send, ('gx', 'gy'), split_axis=0, concat_axis=0, tiled=True)  12.2 us
    all_to_all x1, starting transfers between devices, body(): lax.all_to_all(send, ('gx', 'gy'), split_axis=0, concat_axis=0, tiled=True)  11.5 us
    ppermute x6, waiting for transfers between devices, body(): arrived[shift] = lax.ppermute(outs[shift], 'gx', pairs)  7.45 us
    ppermute x6, starting transfers between devices, body(): arrived[shift] = lax.ppermute(outs[shift], 'gx', pairs)  5.69 us
    unnamed x35, local copies, waits for them, and re-layouts  4.98 us
    pallas_call x1, Pallas kernels, inner(): pl.pallas_call(inner_kernel, in_specs=[vmem] * 6, out_specs=[vmem] * 2, o...  4.72 us
  transfers between devices with their start and end apart: 9, of which 6 were waited for; matrix products, arithmetic and copies ran while one was open for 4% of the time, Pallas kernels for 6%

profile of v7, /device:TPU:1, one launch (start us, length us, event | category | flops | bytes accessed | tf_op | source)
XLA Modules:
  0.0 89.9 jit_solution(8968026194017607311)
XLA Ops:
  0.0 12.9 %route.1 = bf16[128,5,8,128]{3,2,1,0:T(8,128)(2,1)} custom-call(s32[1,8192]{1,0:T(1,128)} %bitcast.13, s32[2,8192]{1,0:T(2,128)} %point_hbm.1, bf16[32,8192]{1,0:T(8,128)(2,1)} %value_hbm.1), custom_call_target="tpu_custom_call" | custom-call | flops 15000000512 | tf_op jit(solution)/shard_map/route/pallas_call | solution.py:198
  12.9 11.5 %all-to-all-start = ((bf16[128,5,8,128]{3,2,1,0:T(8,128)(2,1)}), bf16[128,5,8,128]{3,2,1,0:T(8,128)(2,1)S(1)}, u32[]{:S(2)}, u32[]{:S(2)}) async-start(bf16[128,5,8,128]{3,2,1,0:T(8,128)(2,1)} %route.1), calls=%async_computation | async-start | bytes 2621440 | tf_op jit(solution)/shard_map/all_to_all | solution.py:632
  24.4 0.9 copy.5
  25.3 1.1 %reshape.10 = bf16[11,2,2,2,64,64]{5,4,2,1,0,3:T(8,128)(2,1)S(1)} reshape(bf16[11,2,2,2,4096]{4,2,1,0,3:T(2,128)(2,1)S(1)} %copy.5) | data formatting | bytes 1441792 | tf_op jit(solution)/shard_map/reshape | solution.py:618
  26.4 0.1 fusion
  26.6 0.1 slice_bitcast_fusion
  26.7 0.7 copy-done.10
  27.4 0.8 maximum_maximum_fusion
  28.4 1.7 %phases.1 = (f32[8,16,8,128]{3,2,1,0:T(8,128)S(1)}, f32[8,16,8,128]{3,2,1,0:T(8,128)S(1)}, f32[2,2,16,8,128]{4,3,2,1,0:T(8,128)S(1)}, f32[2,2,16,8,128]{4,3,2,1,...) custom-call(s32[3]{0:T(128)S(1)} %pad_add_fusion.where_ref.after_ref), custom_call_target="tpu_custom_call" | custom-call | flops 2000000000 | tf_op jit(solution)/shard_map/phases/pallas_call | solution.py:263
  30.1 0.7 copy-done
  30.8 0.7 copy-done.2
  31.5 0.7 copy-done.4
  32.2 0.7 copy-done.6
  32.9 0.6 copy-done.8
  33.5 12.2 %all-to-all-done.got_ref = bf16[128,5,8,128]{3,2,1,0:T(8,128)(2,1)S(1)} async-done(((bf16[128,5,8,128]{3,2,1,0:T(8,128)(2,1)}), bf16[128,5,8,128]{3,2,1,0:T(8,128)(2,1)S(1)}, u32[]{:S(2)}, u32[]{:S(2)}) %all-to-all-start) | async-done | bytes 1310752 | tf_op jit(solution)/shard_map/all_to_all | solution.py:632
  45.7 17.8 %leaves.1.leaf_ref = f32[2,2048,128]{2,1,0:T(8,128)S(1)} custom-call(bf16[128,5,8,128]{3,2,1,0:T(8,128)(2,1)S(1)} %all-to-all-done.got_ref), custom_call_target="tpu_custom_call" | custom-call | flops 19000000512 | tf_op jit(solution)/shard_map/leaves/pallas_call | solution.py:368
  63.6 4.7 %inner.1 = (bf16[2,2,2,256,128]{4,3,2,1,0:T(8,128)(2,1)S(1)}, bf16[2,2,2,256,128]{4,3,2,1,0:T(8,128)(2,1)S(1)}) custom-call(f32[2,2048,128]{2,1,0:T(8,128)S(1)} %leaves.1.leaf_ref, bf16[9,2,2,128,128]{4,3,2,1,0:T(8,128)(2,1)S(1)} %slice.18.mats_ref, f32[8,16,8,128]{3,2,1,0:T(8,128)S(1)} %get-tuple-element.23.level_c, ...), custom_call_target="tpu_custom_call" | custom-call | flops 5000000000 | tf_op jit(solution)/shard_map/inner/pallas_call | solution.py:504
  68.4 1.3 %collective-permute-start = (bf16[2,2,2,256,128]{4,3,2,1,0:T(8,128)(2,1)S(1)}, bf16[2,2,2,256,128]{4,3,2,1,0:T(8,128)(2,1)S(1)}, u32[]{:S(2)}, u32[]{:S(2)}) collective-permute-start(bf16[2,2,2,256,128]{4,3,2,1,0:T(8,128)(2,1)S(1)} %get-tuple-element.27.mine_ref), channel_id=1, source_target_pairs={{0,1},{1,0},{2,3},{3,2},{4,5},{5,4},{6,7},{7,6},{8,9},{9,8},{10,11... | collective-permute-start | bytes 1572872 | tf_op jit(solution)/shard_map/ppermute | solution.py:642
  69.8 0.2 maximum_maximum_fusion.1.mats_ref
  69.9 1.3 %collective-permute-done.other_ref = bf16[2,2,2,256,128]{4,3,2,1,0:T(8,128)(2,1)S(1)} collective-permute-done((bf16[2,2,2,256,128]{4,3,2,1,0:T(8,128)(2,1)S(1)}, bf16[2,2,2,256,128]{4,3,2,1,0:T(8,128)(2,1)S(1)}, u32[]{:S(2)}, u32[]{:S(2)}) %collective-permute-start) | collective-permute-done | bytes 524320 | tf_op jit(solution)/shard_map/ppermute | solution.py:642
  71.2 1.7 %outer.2 = (bf16[2,256,128]{2,1,0:T(8,128)(2,1)S(1)}, bf16[2,256,128]{2,1,0:T(8,128)(2,1)S(1)}, bf16[2,256,128]{2,1,0:T(8,128)(2,1)S(1)}, bf16[2,256,128]{2,1,0:T(8,128)(2,1)S(1)}) custom-call(s32[3]{0:T(128)S(1)} %pad_add_fusion.where_ref.after_ref, bf16[2,2,2,256,128]{4,3,2,1,0:T(8,128)(2,1)S(1)} %get-tuple-element.27.mine_ref, ...), custom_call_target="tpu_custom_call" | custom-call | flops 3000000000 | tf_op jit(solution)/shard_map/outer/pallas_call | solution.py:551
  73.0 1.6 %collective-permute-start.2 = (bf16[2,256,128]{2,1,0:T(8,128)(2,1)S(1)}, bf16[2,256,128]{2,1,0:T(8,128)(2,1)S(1)}, u32[]{:S(2)}, u32[]{:S(2)}) collective-permute-start(bf16[2,256,128]{2,1,0:T(8,128)(2,1)S(1)} %get-tuple-element.34), channel_id=1, source_target_pairs={{0,32},{16,48},{32,0},{48,16},{64,96},{80,112},{96,64},{112,80},{1... | collective-permute-start | bytes 393224 | tf_op jit(solution)/shard_map/ppermute | solution.py:648
  74.6 1.2 %collective-permute-start.3 = (bf16[2,256,128]{2,1,0:T(8,128)(2,1)S(1)}, bf16[2,256,128]{2,1,0:T(8,128)(2,1)S(1)}, u32[]{:S(2)}, u32[]{:S(2)}) collective-permute-start(bf16[2,256,128]{2,1,0:T(8,128)(2,1)S(1)} %get-tuple-element.35), channel_id=1, source_target_pairs={{0,48},{16,0},{32,16},{48,32},{64,112},{80,64},{96,80},{112,96},{1... | collective-permute-start | bytes 393224 | tf_op jit(solution)/shard_map/ppermute | solution.py:648
  75.9 1.7 %outer.3 = (bf16[2,256,128]{2,1,0:T(8,128)(2,1)S(1)}, bf16[2,256,128]{2,1,0:T(8,128)(2,1)S(1)}, bf16[2,256,128]{2,1,0:T(8,128)(2,1)S(1)}, bf16[2,256,128]{2,1,0:T(8,128)(2,1)S(1)}) custom-call(s32[3]{0:T(128)S(1)} %pad_add_fusion.where_ref.after_ref, bf16[2,2,2,256,128]{4,3,2,1,0:T(8,128)(2,1)S(1)} %get-tuple-element.36.mine_ref, ...), custom_call_target="tpu_custom_call" | custom-call | flops 3000000000 | tf_op jit(solution)/shard_map/outer/pallas_call | solution.py:551
  77.6 0.5 collective-permute-start.5
  78.1 1.9 %collective-permute-start.6 = (bf16[2,256,128]{2,1,0:T(8,128)(2,1)S(1)}, bf16[2,256,128]{2,1,0:T(8,128)(2,1)S(1)}, u32[]{:S(2)}, u32[]{:S(2)}) collective-permute-start(bf16[2,256,128]{2,1,0:T(8,128)(2,1)S(1)} %get-tuple-element.39), channel_id=1, source_target_pairs={{0,32},{16,48},{32,0},{48,16},{64,96},{80,112},{96,64},{112,80},{1... | collective-permute-start | bytes 393224 | tf_op jit(solution)/shard_map/ppermute | solution.py:648
  80.0 1.6 %collective-permute-done.1.refs_1_ = bf16[2,256,128]{2,1,0:T(8,128)(2,1)S(1)} collective-permute-done((bf16[2,256,128]{2,1,0:T(8,128)(2,1)S(1)}, bf16[2,256,128]{2,1,0:T(8,128)(2,1)S(1)}, u32[]{:S(2)}, u32[]{:S(2)}) %collective-permute-start.1) | collective-permute-done | bytes 131104 | tf_op jit(solution)/shard_map/ppermute | solution.py:648
  81.5 0.4 collective-permute-start.7
  82.0 0.1 collective-permute-done.3.refs_3_
  82.1 5.3 %collective-permute-done.5.refs_5_ = bf16[2,256,128]{2,1,0:T(8,128)(2,1)S(1)} collective-permute-done((bf16[2,256,128]{2,1,0:T(8,128)(2,1)S(1)}, bf16[2,256,128]{2,1,0:T(8,128)(2,1)S(1)}, u32[]{:S(2)}, u32[]{:S(2)}) %collective-permute-start.5) | collective-permute-done | bytes 131104 | tf_op jit(solution)/shard_map/ppermute | solution.py:648
  87.4 0.4 collective-permute-done.7.refs_7_
  87.8 1.9 %finish.1 = bf16[128,4096]{1,0:T(8,128)(2,1)} custom-call(s32[3]{0:T(128)S(1)} %pad_add_fusion.where_ref.after_ref, bf16[2,256,128]{2,1,0:T(8,128)(2,1)S(1)} %get-tuple-element.32.after_ref.refs_0_, bf16[2,256,128]{2,1,0:T(8,128)(2,1)S(1)} %collective-permute-done.1.refs_1_, bf16[2,256,128]{2,1,0:T(8,128)(2,1)S(1)} %collective-permute-done.2.refs_2_, ...), custom_call_target="tpu_custom_call" | custom-call | flops 3000000000 | tf_op jit(solution)/shard_map/finish/pallas_call | solution.py:605
  (35 shorter events, 0.4 us)
Async XLA Ops:
  12.9 11.5 %copy-start.16 = (bf16[11,2,2,2,4096]{4,3,2,1,0:T(2,128)(2,1)S(1)}, bf16[11,2,2,2,4096]{4,3,2,1,0:T(2,128)(2,1)}, u32[]{:S(2)}) copy-start(bf16[11,2,2,2,4096]{4,3,2,1,0:T(2,128)(2,1)} %param.7) | copy-start | bytes 2162692
  12.9 32.8 %all-to-all-start = ((bf16[128,5,8,128]{3,2,1,0:T(8,128)(2,1)}), bf16[128,5,8,128]{3,2,1,0:T(8,128)(2,1)S(1)}, u32[]{:S(2)}, u32[]{:S(2)}) async-start(bf16[128,5,8,128]{3,2,1,0:T(8,128)(2,1)} %route.1), calls=%async_computation | async-start | bytes 2621440 | tf_op jit(solution)/shard_map/all_to_all | solution.py:632
  26.5 0.9 copy-start.10
  26.7 1.6 %copy-start.12 = (bf16[11,2,2,64,64]{4,3,2,1,0:T(8,128)(2,1)}, bf16[11,2,2,64,64]{4,3,2,1,0:T(8,128)(2,1)S(1)}, u32[]{:S(2)}) copy-start(bf16[11,2,2,64,64]{4,3,2,1,0:T(8,128)(2,1)S(1)} %get-tuple-element.41) | copy-start | bytes 1081348
  26.7 1.6 %copy-start.14 = (bf16[11,2,2,64,64]{4,3,2,1,0:T(8,128)(2,1)}, bf16[11,2,2,64,64]{4,3,2,1,0:T(8,128)(2,1)S(1)}, u32[]{:S(2)}) copy-start(bf16[11,2,2,64,64]{4,3,2,1,0:T(8,128)(2,1)S(1)} %get-tuple-element.42) | copy-start | bytes 1081348
  30.1 0.7 copy-start
  30.8 0.7 copy-start.2
  31.5 0.7 copy-start.4
  32.2 0.7 copy-start.6
  32.9 0.6 copy-start.8
  45.7 17.8 %copy-start.5 = (f32[2,2,16,8,128]{4,3,2,1,0:T(8,128)S(1)}, f32[2,2,16,8,128]{4,3,2,1,0:T(8,128)}, u32[]{:S(2)}) copy-start(f32[2,2,16,8,128]{4,3,2,1,0:T(8,128)} %copy-done.4) | copy-start | bytes 786436
  45.7 17.8 %copy-start.7 = (f32[2,2,16,8,128]{4,3,2,1,0:T(8,128)S(1)}, f32[2,2,16,8,128]{4,3,2,1,0:T(8,128)}, u32[]{:S(2)}) copy-start(f32[2,2,16,8,128]{4,3,2,1,0:T(8,128)} %copy-done.6) | copy-start | bytes 786436
  63.6 6.2 %copy-start.11 = (bf16[11,2,2,64,64]{4,3,2,1,0:T(8,128)(2,1)S(1)}, bf16[11,2,2,64,64]{4,3,2,1,0:T(8,128)(2,1)}, u32[]{:S(2)}) copy-start(bf16[11,2,2,64,64]{4,3,2,1,0:T(8,128)(2,1)} %copy-done.10) | copy-start | bytes 1081348
  63.6 6.2 %copy-start.13 = (bf16[11,2,2,64,64]{4,3,2,1,0:T(8,128)(2,1)S(1)}, bf16[11,2,2,64,64]{4,3,2,1,0:T(8,128)(2,1)}, u32[]{:S(2)}) copy-start(bf16[11,2,2,64,64]{4,3,2,1,0:T(8,128)(2,1)} %copy-done.12) | copy-start | bytes 1081348
  63.6 6.2 %copy-start.15 = (bf16[11,2,2,64,64]{4,3,2,1,0:T(8,128)(2,1)S(1)}, bf16[11,2,2,64,64]{4,3,2,1,0:T(8,128)(2,1)}, u32[]{:S(2)}) copy-start(bf16[11,2,2,64,64]{4,3,2,1,0:T(8,128)(2,1)} %copy-done.14) | copy-start | bytes 1081348
  68.3 2.9 %copy-start.1 = (f32[2,2,16,8,128]{4,3,2,1,0:T(8,128)S(1)}, f32[2,2,16,8,128]{4,3,2,1,0:T(8,128)}, u32[]{:S(2)}) copy-start(f32[2,2,16,8,128]{4,3,2,1,0:T(8,128)} %copy-done) | copy-start | bytes 786436
  68.3 2.9 %copy-start.3 = (f32[2,2,16,8,128]{4,3,2,1,0:T(8,128)S(1)}, f32[2,2,16,8,128]{4,3,2,1,0:T(8,128)}, u32[]{:S(2)}) copy-start(f32[2,2,16,8,128]{4,3,2,1,0:T(8,128)} %copy-done.2) | copy-start | bytes 786436
  68.3 2.9 %copy-start.9 = (f32[16,128]{1,0:T(8,128)S(1)}, f32[16,128]{1,0:T(8,128)}, u32[]{:S(2)}) copy-start(f32[16,128]{1,0:T(8,128)} %copy-done.8) | copy-start | bytes 24580
  68.4 2.8 %collective-permute-start = (bf16[2,2,2,256,128]{4,3,2,1,0:T(8,128)(2,1)S(1)}, bf16[2,2,2,256,128]{4,3,2,1,0:T(8,128)(2,1)S(1)}, u32[]{:S(2)}, u32[]{:S(2)}) collective-permute-start(bf16[2,2,2,256,128]{4,3,2,1,0:T(8,128)(2,1)S(1)} %get-tuple-element.27.mine_ref), channel_id=1, source_target_pairs={{0,1},{1,0},{2,3},{3,2},{4,5},{5,4},{6,7},{7,6},{8,9},{9,8},{10,11... | collective-permute-start | bytes 1572872 | tf_op jit(solution)/shard_map/ppermute | solution.py:642
  69.7 6.2 %collective-permute-start.4 = (bf16[2,2,2,256,128]{4,3,2,1,0:T(8,128)(2,1)S(1)}, bf16[2,2,2,256,128]{4,3,2,1,0:T(8,128)(2,1)S(1)}, u32[]{:S(2)}, u32[]{:S(2)}) collective-permute-start(bf16[2,2,2,256,128]{4,3,2,1,0:T(8,128)(2,1)S(1)} %get-tuple-element.36.mine_ref), channel_id=1, source_target_pairs={{0,1},{1,0},{2,3},{3,2},{4,5},{5,4},{6,7},{7,6},{8,9},{9,8},{10,11... | collective-permute-start | bytes 1572872 | tf_op jit(solution)/shard_map/ppermute | solution.py:642
  72.9 8.6 %collective-permute-start.1 = (bf16[2,256,128]{2,1,0:T(8,128)(2,1)S(1)}, bf16[2,256,128]{2,1,0:T(8,128)(2,1)S(1)}, u32[]{:S(2)}, u32[]{:S(2)}) collective-permute-start(bf16[2,256,128]{2,1,0:T(8,128)(2,1)S(1)} %get-tuple-element.33), channel_id=1, source_target_pairs={{0,16},{16,32},{32,48},{48,0},{64,80},{80,96},{96,112},{112,64},{1... | collective-permute-start | bytes 393224 | tf_op jit(solution)/shard_map/ppermute | solution.py:648
  73.0 8.9 %collective-permute-start.2 = (bf16[2,256,128]{2,1,0:T(8,128)(2,1)S(1)}, bf16[2,256,128]{2,1,0:T(8,128)(2,1)S(1)}, u32[]{:S(2)}, u32[]{:S(2)}) collective-permute-start(bf16[2,256,128]{2,1,0:T(8,128)(2,1)S(1)} %get-tuple-element.34), channel_id=1, source_target_pairs={{0,32},{16,48},{32,0},{48,16},{64,96},{80,112},{96,64},{112,80},{1... | collective-permute-start | bytes 393224 | tf_op jit(solution)/shard_map/ppermute | solution.py:648
  74.6 7.4 %collective-permute-start.3 = (bf16[2,256,128]{2,1,0:T(8,128)(2,1)S(1)}, bf16[2,256,128]{2,1,0:T(8,128)(2,1)S(1)}, u32[]{:S(2)}, u32[]{:S(2)}) collective-permute-start(bf16[2,256,128]{2,1,0:T(8,128)(2,1)S(1)} %get-tuple-element.35), channel_id=1, source_target_pairs={{0,48},{16,0},{32,16},{48,32},{64,112},{80,64},{96,80},{112,96},{1... | collective-permute-start | bytes 393224 | tf_op jit(solution)/shard_map/ppermute | solution.py:648
  77.6 9.8 %collective-permute-start.5 = (bf16[2,256,128]{2,1,0:T(8,128)(2,1)S(1)}, bf16[2,256,128]{2,1,0:T(8,128)(2,1)S(1)}, u32[]{:S(2)}, u32[]{:S(2)}) collective-permute-start(bf16[2,256,128]{2,1,0:T(8,128)(2,1)S(1)} %get-tuple-element.38), channel_id=1, source_target_pairs={{0,16},{16,32},{32,48},{48,0},{64,80},{80,96},{96,112},{112,64},{1... | collective-permute-start | bytes 393224 | tf_op jit(solution)/shard_map/ppermute | solution.py:648
  78.1 9.3 %collective-permute-start.6 = (bf16[2,256,128]{2,1,0:T(8,128)(2,1)S(1)}, bf16[2,256,128]{2,1,0:T(8,128)(2,1)S(1)}, u32[]{:S(2)}, u32[]{:S(2)}) collective-permute-start(bf16[2,256,128]{2,1,0:T(8,128)(2,1)S(1)} %get-tuple-element.39), channel_id=1, source_target_pairs={{0,32},{16,48},{32,0},{48,16},{64,96},{80,112},{96,64},{112,80},{1... | collective-permute-start | bytes 393224 | tf_op jit(solution)/shard_map/ppermute | solution.py:648
  81.5 6.3 %collective-permute-start.7 = (bf16[2,256,128]{2,1,0:T(8,128)(2,1)S(1)}, bf16[2,256,128]{2,1,0:T(8,128)(2,1)S(1)}, u32[]{:S(2)}, u32[]{:S(2)}) collective-permute-start(bf16[2,256,128]{2,1,0:T(8,128)(2,1)S(1)} %get-tuple-element.40), channel_id=1, source_target_pairs={{0,48},{16,0},{32,16},{48,32},{64,112},{80,64},{96,80},{112,96},{1... | collective-permute-start | bytes 393224 | tf_op jit(solution)/shard_map/ppermute | solution.py:648

commit v8 on v7

--- a/solution.py
+++ b/solution.py
@@ -586,12 +586,11 @@
             for side in range(2):
                 start = (2 * number + side) * 256
                 held[:, start : start + 256] = made[:, side * 128 : side * 128 + 128].T
-            if number % 2 == 1:
-                copies[number // 2].start()
+            copies[number].start()
 
     copies = []
-    for number in range(4):
-        span = pl.ds(number * 1024, 1024)
+    for number in range(8):
+        span = pl.ds(number * 512, 512)
         copies.append(
             pltpu.make_async_copy(held.at[:, span], out_ref.at[:, span], sems.at[number])
         )
@@ -607,7 +606,7 @@
         in_specs=[pl.BlockSpec(memory_space=pltpu.SMEM)] + [vmem] * 8,
         out_specs=pl.BlockSpec(memory_space=pltpu.HBM),
         out_shape=jax.ShapeDtypeStruct((128, 4096), BF16),
-        scratch_shapes=[pltpu.VMEM((128, 4096), BF16), pltpu.SemaphoreType.DMA((4,))],
+        scratch_shapes=[pltpu.VMEM((128, 4096), BF16), pltpu.SemaphoreType.DMA((8,))],
         compiler_params=pltpu.CompilerParams(vmem_limit_bytes=40 * MIB),
         cost_estimate=cost(3),
         name="finish",

time: 90.1 us -> 90.1 us (level)
  no operation moved by 1% of the time
where the time goes in v8:
time: 90.1 us; the launch traced here: 89.9 us
  Pallas kernels  42.5 us (47%)
  waiting for transfers between devices  21 us (23%)
  starting transfers between devices  18.6 us (21%)
  local copies, waits for them, and re-layouts  6.31 us (7%)
  other arithmetic  1.13 us (1%)
    pallas_call x1, Pallas kernels, leaves(): pl.pallas_call(leaves_kernel, in_specs=[vmem], out_specs=vmem, out_shape=...  17.8 us
    pallas_call x1, Pallas kernels, route(): pl.pallas_call(route_kernel, in_specs=[pl.BlockSpec(memory_space=pltpu.HB...  12.9 us
    all_to_all x1, waiting for transfers between devices, body(): lax.all_to_all(send, ('gx', 'gy'), split_axis=0, concat_axis=0, tiled=True)  12.2 us
    all_to_all x1, starting transfers between devices, body(): lax.all_to_all(send, ('gx', 'gy'), split_axis=0, concat_axis=0, tiled=True)  11.5 us
    ppermute x6, waiting for transfers between devices, body(): arrived[shift] = lax.ppermute(outs[shift], 'gx', pairs)  7.45 us
    ppermute x6, starting transfers between devices, body(): arrived[shift] = lax.ppermute(outs[shift], 'gx', pairs)  5.69 us
    unnamed x35, local copies, waits for them, and re-layouts  4.98 us
    pallas_call x1, Pallas kernels, inner(): pl.pallas_call(inner_kernel, in_specs=[vmem] * 6, out_specs=[vmem] * 2, o...  4.72 us
  transfers between devices with their start and end apart: 9, of which 6 were waited for; matrix products, arithmetic and copies ran while one was open for 4% of the time, Pallas kernels for 6%

profile of v8, /device:TPU:1, one launch (start us, length us, event | category | flops | bytes accessed | tf_op | source)
XLA Modules:
  0.0 89.9 jit_solution(13691560942158478238)
XLA Ops:
  0.0 12.9 %route.1 = bf16[128,5,8,128]{3,2,1,0:T(8,128)(2,1)} custom-call(s32[1,8192]{1,0:T(1,128)} %bitcast.13, s32[2,8192]{1,0:T(2,128)} %point_hbm.1, bf16[32,8192]{1,0:T(8,128)(2,1)} %value_hbm.1), custom_call_target="tpu_custom_call" | custom-call | flops 15000000512 | tf_op jit(solution)/shard_map/route/pallas_call | solution.py:198
  12.9 11.5 %all-to-all-start = ((bf16[128,5,8,128]{3,2,1,0:T(8,128)(2,1)}), bf16[128,5,8,128]{3,2,1,0:T(8,128)(2,1)S(1)}, u32[]{:S(2)}, u32[]{:S(2)}) async-start(bf16[128,5,8,128]{3,2,1,0:T(8,128)(2,1)} %route.1), calls=%async_computation | async-start | bytes 2621440 | tf_op jit(solution)/shard_map/all_to_all | solution.py:631
  24.4 0.9 copy.5
  25.3 1.1 %reshape.10 = bf16[11,2,2,2,64,64]{5,4,2,1,0,3:T(8,128)(2,1)S(1)} reshape(bf16[11,2,2,2,4096]{4,2,1,0,3:T(2,128)(2,1)S(1)} %copy.5) | data formatting | bytes 1441792 | tf_op jit(solution)/shard_map/reshape | solution.py:617
  26.4 0.1 fusion
  26.6 0.1 slice_bitcast_fusion
  26.7 0.7 copy-done.10
  27.4 0.8 maximum_maximum_fusion
  28.4 1.7 %phases.1 = (f32[8,16,8,128]{3,2,1,0:T(8,128)S(1)}, f32[8,16,8,128]{3,2,1,0:T(8,128)S(1)}, f32[2,2,16,8,128]{4,3,2,1,0:T(8,128)S(1)}, f32[2,2,16,8,128]{4,3,2,1,...) custom-call(s32[3]{0:T(128)S(1)} %pad_add_fusion.where_ref.after_ref), custom_call_target="tpu_custom_call" | custom-call | flops 2000000000 | tf_op jit(solution)/shard_map/phases/pallas_call | solution.py:263
  30.1 0.7 copy-done
  30.8 0.7 copy-done.2
  31.5 0.7 copy-done.4
  32.2 0.7 copy-done.6
  32.9 0.6 copy-done.8
  33.5 12.2 %all-to-all-done.got_ref = bf16[128,5,8,128]{3,2,1,0:T(8,128)(2,1)S(1)} async-done(((bf16[128,5,8,128]{3,2,1,0:T(8,128)(2,1)}), bf16[128,5,8,128]{3,2,1,0:T(8,128)(2,1)S(1)}, u32[]{:S(2)}, u32[]{:S(2)}) %all-to-all-start) | async-done | bytes 1310752 | tf_op jit(solution)/shard_map/all_to_all | solution.py:631
  45.7 17.8 %leaves.1.leaf_ref = f32[2,2048,128]{2,1,0:T(8,128)S(1)} custom-call(bf16[128,5,8,128]{3,2,1,0:T(8,128)(2,1)S(1)} %all-to-all-done.got_ref), custom_call_target="tpu_custom_call" | custom-call | flops 19000000512 | tf_op jit(solution)/shard_map/leaves/pallas_call | solution.py:368
  63.6 4.7 %inner.1 = (bf16[2,2,2,256,128]{4,3,2,1,0:T(8,128)(2,1)S(1)}, bf16[2,2,2,256,128]{4,3,2,1,0:T(8,128)(2,1)S(1)}) custom-call(f32[2,2048,128]{2,1,0:T(8,128)S(1)} %leaves.1.leaf_ref, bf16[9,2,2,128,128]{4,3,2,1,0:T(8,128)(2,1)S(1)} %slice.18.mats_ref, f32[8,16,8,128]{3,2,1,0:T(8,128)S(1)} %get-tuple-element.23.level_c, ...), custom_call_target="tpu_custom_call" | custom-call | flops 5000000000 | tf_op jit(solution)/shard_map/inner/pallas_call | solution.py:504
  68.4 1.3 %collective-permute-start = (bf16[2,2,2,256,128]{4,3,2,1,0:T(8,128)(2,1)S(1)}, bf16[2,2,2,256,128]{4,3,2,1,0:T(8,128)(2,1)S(1)}, u32[]{:S(2)}, u32[]{:S(2)}) collective-permute-start(bf16[2,2,2,256,128]{4,3,2,1,0:T(8,128)(2,1)S(1)} %get-tuple-element.27.mine_ref), channel_id=1, source_target_pairs={{0,1},{1,0},{2,3},{3,2},{4,5},{5,4},{6,7},{7,6},{8,9},{9,8},{10,11... | collective-permute-start | bytes 1572872 | tf_op jit(solution)/shard_map/ppermute | solution.py:641
  69.8 0.2 maximum_maximum_fusion.1.mats_ref
  69.9 1.3 %collective-permute-done.other_ref = bf16[2,2,2,256,128]{4,3,2,1,0:T(8,128)(2,1)S(1)} collective-permute-done((bf16[2,2,2,256,128]{4,3,2,1,0:T(8,128)(2,1)S(1)}, bf16[2,2,2,256,128]{4,3,2,1,0:T(8,128)(2,1)S(1)}, u32[]{:S(2)}, u32[]{:S(2)}) %collective-permute-start) | collective-permute-done | bytes 524320 | tf_op jit(solution)/shard_map/ppermute | solution.py:641
  71.2 1.7 %outer.2 = (bf16[2,256,128]{2,1,0:T(8,128)(2,1)S(1)}, bf16[2,256,128]{2,1,0:T(8,128)(2,1)S(1)}, bf16[2,256,128]{2,1,0:T(8,128)(2,1)S(1)}, bf16[2,256,128]{2,1,0:T(8,128)(2,1)S(1)}) custom-call(s32[3]{0:T(128)S(1)} %pad_add_fusion.where_ref.after_ref, bf16[2,2,2,256,128]{4,3,2,1,0:T(8,128)(2,1)S(1)} %get-tuple-element.27.mine_ref, ...), custom_call_target="tpu_custom_call" | custom-call | flops 3000000000 | tf_op jit(solution)/shard_map/outer/pallas_call | solution.py:551
  73.0 1.6 %collective-permute-start.2 = (bf16[2,256,128]{2,1,0:T(8,128)(2,1)S(1)}, bf16[2,256,128]{2,1,0:T(8,128)(2,1)S(1)}, u32[]{:S(2)}, u32[]{:S(2)}) collective-permute-start(bf16[2,256,128]{2,1,0:T(8,128)(2,1)S(1)} %get-tuple-element.34), channel_id=1, source_target_pairs={{0,32},{16,48},{32,0},{48,16},{64,96},{80,112},{96,64},{112,80},{1... | collective-permute-start | bytes 393224 | tf_op jit(solution)/shard_map/ppermute | solution.py:647
  74.6 1.2 %collective-permute-start.3 = (bf16[2,256,128]{2,1,0:T(8,128)(2,1)S(1)}, bf16[2,256,128]{2,1,0:T(8,128)(2,1)S(1)}, u32[]{:S(2)}, u32[]{:S(2)}) collective-permute-start(bf16[2,256,128]{2,1,0:T(8,128)(2,1)S(1)} %get-tuple-element.35), channel_id=1, source_target_pairs={{0,48},{16,0},{32,16},{48,32},{64,112},{80,64},{96,80},{112,96},{1... | collective-permute-start | bytes 393224 | tf_op jit(solution)/shard_map/ppermute | solution.py:647
  75.9 1.7 %outer.3 = (bf16[2,256,128]{2,1,0:T(8,128)(2,1)S(1)}, bf16[2,256,128]{2,1,0:T(8,128)(2,1)S(1)}, bf16[2,256,128]{2,1,0:T(8,128)(2,1)S(1)}, bf16[2,256,128]{2,1,0:T(8,128)(2,1)S(1)}) custom-call(s32[3]{0:T(128)S(1)} %pad_add_fusion.where_ref.after_ref, bf16[2,2,2,256,128]{4,3,2,1,0:T(8,128)(2,1)S(1)} %get-tuple-element.36.mine_ref, ...), custom_call_target="tpu_custom_call" | custom-call | flops 3000000000 | tf_op jit(solution)/shard_map/outer/pallas_call | solution.py:551
  77.6 0.5 collective-permute-start.5
  78.1 1.9 %collective-permute-start.6 = (bf16[2,256,128]{2,1,0:T(8,128)(2,1)S(1)}, bf16[2,256,128]{2,1,0:T(8,128)(2,1)S(1)}, u32[]{:S(2)}, u32[]{:S(2)}) collective-permute-start(bf16[2,256,128]{2,1,0:T(8,128)(2,1)S(1)} %get-tuple-element.39), channel_id=1, source_target_pairs={{0,32},{16,48},{32,0},{48,16},{64,96},{80,112},{96,64},{112,80},{1... | collective-permute-start | bytes 393224 | tf_op jit(solution)/shard_map/ppermute | solution.py:647
  80.0 1.6 %collective-permute-done.1.refs_1_ = bf16[2,256,128]{2,1,0:T(8,128)(2,1)S(1)} collective-permute-done((bf16[2,256,128]{2,1,0:T(8,128)(2,1)S(1)}, bf16[2,256,128]{2,1,0:T(8,128)(2,1)S(1)}, u32[]{:S(2)}, u32[]{:S(2)}) %collective-permute-start.1) | collective-permute-done | bytes 131104 | tf_op jit(solution)/shard_map/ppermute | solution.py:647
  81.5 0.4 collective-permute-start.7
  82.0 0.1 collective-permute-done.3.refs_3_
  82.1 5.3 %collective-permute-done.5.refs_5_ = bf16[2,256,128]{2,1,0:T(8,128)(2,1)S(1)} collective-permute-done((bf16[2,256,128]{2,1,0:T(8,128)(2,1)S(1)}, bf16[2,256,128]{2,1,0:T(8,128)(2,1)S(1)}, u32[]{:S(2)}, u32[]{:S(2)}) %collective-permute-start.5) | collective-permute-done | bytes 131104 | tf_op jit(solution)/shard_map/ppermute | solution.py:647
  87.4 0.4 collective-permute-done.7.refs_7_
  87.8 1.9 %finish.1 = bf16[128,4096]{1,0:T(8,128)(2,1)} custom-call(s32[3]{0:T(128)S(1)} %pad_add_fusion.where_ref.after_ref, bf16[2,256,128]{2,1,0:T(8,128)(2,1)S(1)} %get-tuple-element.32.after_ref.refs_0_, bf16[2,256,128]{2,1,0:T(8,128)(2,1)S(1)} %collective-permute-done.1.refs_1_, bf16[2,256,128]{2,1,0:T(8,128)(2,1)S(1)} %collective-permute-done.2.refs_2_, ...), custom_call_target="tpu_custom_call" | custom-call | flops 3000000000 | tf_op jit(solution)/shard_map/finish/pallas_call | solution.py:604
  (35 shorter events, 0.4 us)
Async XLA Ops:
  12.9 11.5 %copy-start.16 = (bf16[11,2,2,2,4096]{4,3,2,1,0:T(2,128)(2,1)S(1)}, bf16[11,2,2,2,4096]{4,3,2,1,0:T(2,128)(2,1)}, u32[]{:S(2)}) copy-start(bf16[11,2,2,2,4096]{4,3,2,1,0:T(2,128)(2,1)} %param.7) | copy-start | bytes 2162692
  12.9 32.8 %all-to-all-start = ((bf16[128,5,8,128]{3,2,1,0:T(8,128)(2,1)}), bf16[128,5,8,128]{3,2,1,0:T(8,128)(2,1)S(1)}, u32[]{:S(2)}, u32[]{:S(2)}) async-start(bf16[128,5,8,128]{3,2,1,0:T(8,128)(2,1)} %route.1), calls=%async_computation | async-start | bytes 2621440 | tf_op jit(solution)/shard_map/all_to_all | solution.py:631
  26.5 0.9 copy-start.10
  26.7 1.6 %copy-start.12 = (bf16[11,2,2,64,64]{4,3,2,1,0:T(8,128)(2,1)}, bf16[11,2,2,64,64]{4,3,2,1,0:T(8,128)(2,1)S(1)}, u32[]{:S(2)}) copy-start(bf16[11,2,2,64,64]{4,3,2,1,0:T(8,128)(2,1)S(1)} %get-tuple-element.41) | copy-start | bytes 1081348
  26.7 1.6 %copy-start.14 = (bf16[11,2,2,64,64]{4,3,2,1,0:T(8,128)(2,1)}, bf16[11,2,2,64,64]{4,3,2,1,0:T(8,128)(2,1)S(1)}, u32[]{:S(2)}) copy-start(bf16[11,2,2,64,64]{4,3,2,1,0:T(8,128)(2,1)S(1)} %get-tuple-element.42) | copy-start | bytes 1081348
  30.1 0.7 copy-start
  30.8 0.7 copy-start.2
  31.5 0.7 copy-start.4
  32.2 0.7 copy-start.6
  32.9 0.6 copy-start.8
  45.7 17.8 %copy-start.5 = (f32[2,2,16,8,128]{4,3,2,1,0:T(8,128)S(1)}, f32[2,2,16,8,128]{4,3,2,1,0:T(8,128)}, u32[]{:S(2)}) copy-start(f32[2,2,16,8,128]{4,3,2,1,0:T(8,128)} %copy-done.4) | copy-start | bytes 786436
  45.7 17.8 %copy-start.7 = (f32[2,2,16,8,128]{4,3,2,1,0:T(8,128)S(1)}, f32[2,2,16,8,128]{4,3,2,1,0:T(8,128)}, u32[]{:S(2)}) copy-start(f32[2,2,16,8,128]{4,3,2,1,0:T(8,128)} %copy-done.6) | copy-start | bytes 786436
  63.6 6.2 %copy-start.11 = (bf16[11,2,2,64,64]{4,3,2,1,0:T(8,128)(2,1)S(1)}, bf16[11,2,2,64,64]{4,3,2,1,0:T(8,128)(2,1)}, u32[]{:S(2)}) copy-start(bf16[11,2,2,64,64]{4,3,2,1,0:T(8,128)(2,1)} %copy-done.10) | copy-start | bytes 1081348
  63.6 6.2 %copy-start.13 = (bf16[11,2,2,64,64]{4,3,2,1,0:T(8,128)(2,1)S(1)}, bf16[11,2,2,64,64]{4,3,2,1,0:T(8,128)(2,1)}, u32[]{:S(2)}) copy-start(bf16[11,2,2,64,64]{4,3,2,1,0:T(8,128)(2,1)} %copy-done.12) | copy-start | bytes 1081348
  63.6 6.2 %copy-start.15 = (bf16[11,2,2,64,64]{4,3,2,1,0:T(8,128)(2,1)S(1)}, bf16[11,2,2,64,64]{4,3,2,1,0:T(8,128)(2,1)}, u32[]{:S(2)}) copy-start(bf16[11,2,2,64,64]{4,3,2,1,0:T(8,128)(2,1)} %copy-done.14) | copy-start | bytes 1081348
  68.3 2.9 %copy-start.1 = (f32[2,2,16,8,128]{4,3,2,1,0:T(8,128)S(1)}, f32[2,2,16,8,128]{4,3,2,1,0:T(8,128)}, u32[]{:S(2)}) copy-start(f32[2,2,16,8,128]{4,3,2,1,0:T(8,128)} %copy-done) | copy-start | bytes 786436
  68.3 2.9 %copy-start.3 = (f32[2,2,16,8,128]{4,3,2,1,0:T(8,128)S(1)}, f32[2,2,16,8,128]{4,3,2,1,0:T(8,128)}, u32[]{:S(2)}) copy-start(f32[2,2,16,8,128]{4,3,2,1,0:T(8,128)} %copy-done.2) | copy-start | bytes 786436
  68.3 2.9 %copy-start.9 = (f32[16,128]{1,0:T(8,128)S(1)}, f32[16,128]{1,0:T(8,128)}, u32[]{:S(2)}) copy-start(f32[16,128]{1,0:T(8,128)} %copy-done.8) | copy-start | bytes 24580
  68.4 2.8 %collective-permute-start = (bf16[2,2,2,256,128]{4,3,2,1,0:T(8,128)(2,1)S(1)}, bf16[2,2,2,256,128]{4,3,2,1,0:T(8,128)(2,1)S(1)}, u32[]{:S(2)}, u32[]{:S(2)}) collective-permute-start(bf16[2,2,2,256,128]{4,3,2,1,0:T(8,128)(2,1)S(1)} %get-tuple-element.27.mine_ref), channel_id=1, source_target_pairs={{0,1},{1,0},{2,3},{3,2},{4,5},{5,4},{6,7},{7,6},{8,9},{9,8},{10,11... | collective-permute-start | bytes 1572872 | tf_op jit(solution)/shard_map/ppermute | solution.py:641
  69.7 6.2 %collective-permute-start.4 = (bf16[2,2,2,256,128]{4,3,2,1,0:T(8,128)(2,1)S(1)}, bf16[2,2,2,256,128]{4,3,2,1,0:T(8,128)(2,1)S(1)}, u32[]{:S(2)}, u32[]{:S(2)}) collective-permute-start(bf16[2,2,2,256,128]{4,3,2,1,0:T(8,128)(2,1)S(1)} %get-tuple-element.36.mine_ref), channel_id=1, source_target_pairs={{0,1},{1,0},{2,3},{3,2},{4,5},{5,4},{6,7},{7,6},{8,9},{9,8},{10,11... | collective-permute-start | bytes 1572872 | tf_op jit(solution)/shard_map/ppermute | solution.py:641
  72.9 8.6 %collective-permute-start.1 = (bf16[2,256,128]{2,1,0:T(8,128)(2,1)S(1)}, bf16[2,256,128]{2,1,0:T(8,128)(2,1)S(1)}, u32[]{:S(2)}, u32[]{:S(2)}) collective-permute-start(bf16[2,256,128]{2,1,0:T(8,128)(2,1)S(1)} %get-tuple-element.33), channel_id=1, source_target_pairs={{0,16},{16,32},{32,48},{48,0},{64,80},{80,96},{96,112},{112,64},{1... | collective-permute-start | bytes 393224 | tf_op jit(solution)/shard_map/ppermute | solution.py:647
  73.0 8.9 %collective-permute-start.2 = (bf16[2,256,128]{2,1,0:T(8,128)(2,1)S(1)}, bf16[2,256,128]{2,1,0:T(8,128)(2,1)S(1)}, u32[]{:S(2)}, u32[]{:S(2)}) collective-permute-start(bf16[2,256,128]{2,1,0:T(8,128)(2,1)S(1)} %get-tuple-element.34), channel_id=1, source_target_pairs={{0,32},{16,48},{32,0},{48,16},{64,96},{80,112},{96,64},{112,80},{1... | collective-permute-start | bytes 393224 | tf_op jit(solution)/shard_map/ppermute | solution.py:647
  74.6 7.4 %collective-permute-start.3 = (bf16[2,256,128]{2,1,0:T(8,128)(2,1)S(1)}, bf16[2,256,128]{2,1,0:T(8,128)(2,1)S(1)}, u32[]{:S(2)}, u32[]{:S(2)}) collective-permute-start(bf16[2,256,128]{2,1,0:T(8,128)(2,1)S(1)} %get-tuple-element.35), channel_id=1, source_target_pairs={{0,48},{16,0},{32,16},{48,32},{64,112},{80,64},{96,80},{112,96},{1... | collective-permute-start | bytes 393224 | tf_op jit(solution)/shard_map/ppermute | solution.py:647
  77.6 9.8 %collective-permute-start.5 = (bf16[2,256,128]{2,1,0:T(8,128)(2,1)S(1)}, bf16[2,256,128]{2,1,0:T(8,128)(2,1)S(1)}, u32[]{:S(2)}, u32[]{:S(2)}) collective-permute-start(bf16[2,256,128]{2,1,0:T(8,128)(2,1)S(1)} %get-tuple-element.38), channel_id=1, source_target_pairs={{0,16},{16,32},{32,48},{48,0},{64,80},{80,96},{96,112},{112,64},{1... | collective-permute-start | bytes 393224 | tf_op jit(solution)/shard_map/ppermute | solution.py:647
  78.1 9.3 %collective-permute-start.6 = (bf16[2,256,128]{2,1,0:T(8,128)(2,1)S(1)}, bf16[2,256,128]{2,1,0:T(8,128)(2,1)S(1)}, u32[]{:S(2)}, u32[]{:S(2)}) collective-permute-start(bf16[2,256,128]{2,1,0:T(8,128)(2,1)S(1)} %get-tuple-element.39), channel_id=1, source_target_pairs={{0,32},{16,48},{32,0},{48,16},{64,96},{80,112},{96,64},{112,80},{1... | collective-permute-start | bytes 393224 | tf_op jit(solution)/shard_map/ppermute | solution.py:647
  81.5 6.3 %collective-permute-start.7 = (bf16[2,256,128]{2,1,0:T(8,128)(2,1)S(1)}, bf16[2,256,128]{2,1,0:T(8,128)(2,1)S(1)}, u32[]{:S(2)}, u32[]{:S(2)}) collective-permute-start(bf16[2,256,128]{2,1,0:T(8,128)(2,1)S(1)} %get-tuple-element.40), channel_id=1, source_target_pairs={{0,48},{16,0},{32,16},{48,32},{64,112},{80,64},{96,80},{112,96},{1... | collective-permute-start | bytes 393224 | tf_op jit(solution)/shard_map/ppermute | solution.py:647
